TPU v7x, 32 devices: a whole 2x2x4 slice. The times are simulated.
32 devices in a mesh: node: 2 (over core), slab: 16 (over z, y, x).
Axes of the slice: x: 2, y: 2, z: 4, core: 2. Of those that a mesh axis runs over, the one named last changes fastest.
Arguments:
- adjoint_source: float32 [2, 6, 64, 64, 256], P('node', None, 'slab'), may hold values from -6 to 6
- stencil_coef: float32 [2, 4, 64, 64, 256], P('node', None, 'slab'), may hold values from 0.05 to 0.5
- flux_block: float32 [2, 6, 6], P('node'), may hold values from -1.25 to 1.25
- shape_metric: float32 [2, 6, 64, 64, 256], P('node', None, 'slab'), may hold values from -0.3125 to 0.3125
- wall_force: float32 [2, 64, 256], P('node', 'slab'), may hold values from -8 to 8
Outputs:
- wall_gradient: float32 [64, 256], P('slab', 'node')
All inputs are finite; a program needn't handle non-finite values.
Results may differ from a plain program's by a relative error of at most 0.00014.
Values sent between devices are 32-bit elements; how exact they have to be, the bound alone decides.
No kernel may reach another device: no remote copies, remote signals or barrier semaphores. Data moves between devices by JAX's collectives and lax.ppermute only.
A program may use at most 64 MiB of HBM per device.

v0:
```python
import math

import jax
import jax.numpy as jnp
from jax import lax
from jax.sharding import PartitionSpec as P

ITERS = 3


def with_halo(block, sides, width):
    for axis, dim in sides:
        count = lax.axis_size(axis)
        forward = [(i, i + 1) for i in range(count - 1)]
        backward = [(target, source) for source, target in forward]
        low = lax.ppermute(
            lax.slice_in_dim(block, block.shape[dim] - width, None, axis=dim), axis, forward
        )
        high = lax.ppermute(lax.slice_in_dim(block, 0, width, axis=dim), axis, backward)
        block = jnp.concatenate([low, block, high], axis=dim)
    return block


def sweep(extended, source, coef, diag, block):
    padded = jnp.pad(extended, ((0, 0), (0, 0), (1, 1), (1, 1)))
    middle = padded[:, 1:-1, 1:-1, 1:-1]
    coupled = coef[1] * (padded[:, 2:, 1:-1, 1:-1] + padded[:, :-2, 1:-1, 1:-1])
    coupled = coupled + coef[2] * (padded[:, 1:-1, 2:, 1:-1] + padded[:, 1:-1, :-2, 1:-1])
    coupled = coupled + coef[3] * (padded[:, 1:-1, 1:-1, 2:] + padded[:, 1:-1, 1:-1, :-2])
    mixed = jnp.einsum("vw,vxyz->wxyz", block, coupled, precision=lax.Precision.HIGHEST)
    return middle + (source - (diag * middle - mixed)) / diag


def per_device(adjoint_source, stencil_coef, flux_block, shape_metric, wall_force):
    source = adjoint_source[0]
    coef = stencil_coef[0]
    block = flux_block[0]
    sweeps = ITERS - 1
    diag = 0.5 + coef[0] + 2.4 * (coef[1] + coef[2] + coef[3])
    psi = source / diag
    for step in range(sweeps):
        extended = with_halo(psi, (("slab", 1),), 1)
        psi = sweep(extended, source, coef, diag, block)
    sens = jnp.sum(psi * shape_metric[0], axis=(0, 2))
    nodes = lax.axis_size("node")
    cells = wall_force.shape[1] * lax.axis_size("slab") * wall_force.shape[2]
    local_sum = jnp.sum(wall_force[0])
    node_sum = lax.psum(local_sum, "slab")
    objective = lax.all_gather(jnp.reshape(node_sum / cells, (1,)), "node", axis=0, tiled=True)
    order = jnp.arange(nodes, dtype=jnp.float32)
    weight = jnp.sin(math.pi * (order + 0.5) / nodes)
    weight = weight / jnp.sum(weight)
    mean_value = jnp.sum(weight * objective)
    variance = jnp.sum(weight * (objective - mean_value) ** 2)
    spread = jnp.sqrt(variance + 0.25)
    factor = weight * (1.0 + 2.0 * (objective - mean_value) / spread)
    mine = jnp.sum(jnp.where(jnp.arange(nodes) == lax.axis_index("node"), factor, 0.0))
    term = mine * sens
    total = lax.psum(term, "node")
    width = term.shape[1] // nodes
    return lax.dynamic_slice_in_dim(total, lax.axis_index("node") * width, width, 1)


def solution(mesh):
    return jax.shard_map(
        per_device,
        mesh=mesh,
        in_specs=(
            P("node", None, "slab", None, None),
            P("node", None, "slab", None, None),
            P("node", None, None),
            P("node", None, "slab", None, None),
            P("node", "slab", None),
        ),
        out_specs=P("slab", "node"),
        check_vma=False,
    )
```

profile of v0, /device:TPU:0, one launch (start us, length us, event | category | flops | bytes accessed | tf_op | source)
XLA Modules:
  0.0 128.1 jit_solution(6224369099541840876)
XLA Ops:
  0.0 1.3 bitcast_add_fusion
  1.3 0.0 copy-start
  1.3 2.5 %bitcast_divide_fusion = f32[6,4,64,256]{3,0,2,1:T(8,128)S(1)} fusion(f32[1,6,4,64,256]{4,3,2,1,0:T(8,128)} %param.5, f32[4,64,256]{2,1,0:T(8,128)S(1)} %bitcast_add_fusion), kind=kLoop, calls=%fused_computation.51 | loop fusion | flops 393216 | bytes 3407872 | tf_op jit(solution)/shard_map/div | solution.py:40
  3.7 0.1 fusion.57
  3.8 1.3 %collective-permute-start = (f32[6,1,64,256]{3,0,2,1:T(8,128)S(1)}, f32[6,1,64,256]{3,0,2,1:T(8,128)S(1)}, u32[]{:S(2)}, u32[]{:S(2)}) collective-permute-start(f32[6,1,64,256]{3,0,2,1:T(8,128)S(1)} %get-tuple-element.8), channel_id=1, source_target_pairs={{1,0},{2,1},{3,2},{4,3},{5,4},{6,5},{7,6},{8,7},{9,8},{10,9},{11,1... | collective-permute-start | bytes 1179656 | tf_op jit(solution)/shard_map/ppermute | solution.py:19
  5.1 5.5 %collective-permute-start.1 = (f32[6,1,64,256]{3,0,2,1:T(8,128)S(1)}, f32[6,1,64,256]{3,0,2,1:T(8,128)S(1)}, u32[]{:S(2)}, u32[]{:S(2)}) collective-permute-start(f32[6,1,64,256]{3,0,2,1:T(8,128)S(1)} %get-tuple-element.7), channel_id=1, source_target_pairs={{0,1},{1,2},{2,3},{3,4},{4,5},{5,6},{6,7},{7,8},{8,9},{9,10},{10,1... | collective-permute-start | bytes 1179656 | tf_op jit(solution)/shard_map/ppermute | solution.py:16
  10.6 0.1 slice_bitcast_fusion.2
  10.7 0.0 copy-start.1
  10.7 0.0 copy-start.11
  10.8 10.7 %collective-permute-done = f32[6,1,64,256]{3,0,2,1:T(8,128)S(1)} collective-permute-done((f32[6,1,64,256]{3,0,2,1:T(8,128)S(1)}, f32[6,1,64,256]{3,0,2,1:T(8,128)S(1)}, u32[]{:S(2)}, u32[]{:S(2)}) %collective-permute-start) | collective-permute-done | bytes 393248 | tf_op jit(solution)/shard_map/ppermute | solution.py:19
  21.4 11.5 %collective-permute-done.1 = f32[6,1,64,256]{3,0,2,1:T(8,128)S(1)} collective-permute-done((f32[6,1,64,256]{3,0,2,1:T(8,128)S(1)}, f32[6,1,64,256]{3,0,2,1:T(8,128)S(1)}, u32[]{:S(2)}, u32[]{:S(2)}) %collective-permute-start.1) | collective-permute-done | bytes 393248 | tf_op jit(solution)/shard_map/ppermute | solution.py:16
  32.9 2.2 %select_maximum_fusion.2 = f32[6,6,66,258]{3,0,2,1:T(8,128)S(1)} fusion(f32[6,1,64,256]{3,0,2,1:T(8,128)S(1)} %collective-permute-done, f32[6,4,64,256]{3,0,2,1:T(8,128)S(1)} %bitcast_divide_fusion, f32[6,1,64,256]{3,0,2,1:T(8,128)S(1)} %collective-permute-done.1), kind=kLoop, calls=%fused_computation.6 | loop fusion | flops 9195120 | bytes 4811328 | tf_op jit(solution)/shard_map/concatenate | solution.py:20
  35.2 6.5 %fusion.37 = f32[6,4,64,256]{3,0,2,1:T(8,128)S(1)} fusion(f32[6,4,64,256]{3,0,2,1:T(8,128)S(1)} %bitcast_divide_fusion, f32[1,6,4,64,256]{4,3,2,1,0:T(8,128)S(1)} %copy-done.1, f32[6,6,66,258]{3,0,2,1:T(8,128)S(1)} %select_maximum_fusion.2, f32[6,1,64,256]{3,0,2,1:T(8,128)S(1)} %collective-permute-done.1, f32[6,1,64,256]{3,0,2,1:T(8,128)S(1)} %collective-permute-done, ...), kind=kOutput, calls=%fused_computation.50 | convolution fusion | flops 34209792 | bytes 17828864 | tf_op jit(solution)/shard_map/vw,vxyz->wxyz/dot_general | solution.py:30
  41.6 0.0 copy-start.9
  41.6 0.0 copy-start.12
  41.7 0.1 fusion.56
  41.7 1.3 %collective-permute-start.2 = (f32[6,1,64,256]{3,0,2,1:T(8,128)S(1)}, f32[6,1,64,256]{3,0,2,1:T(8,128)}, u32[]{:S(2)}, u32[]{:S(2)}) collective-permute-start(f32[6,1,64,256]{3,0,2,1:T(8,128)S(1)} %get-tuple-element.6), channel_id=1, source_target_pairs={{1,0},{2,1},{3,2},{4,3},{5,4},{6,5},{7,6},{8,7},{9,8},{10,9},{11,1... | collective-permute-start | bytes 1179656 | tf_op jit(solution)/shard_map/ppermute | solution.py:19
  43.0 5.8 %collective-permute-start.3 = (f32[6,1,64,256]{3,0,2,1:T(8,128)S(1)}, f32[6,1,64,256]{3,0,2,1:T(8,128)}, u32[]{:S(2)}, u32[]{:S(2)}) collective-permute-start(f32[6,1,64,256]{3,0,2,1:T(8,128)S(1)} %get-tuple-element.5), channel_id=1, source_target_pairs={{0,1},{1,2},{2,3},{3,4},{4,5},{5,6},{6,7},{7,8},{8,9},{9,10},{10,1... | collective-permute-start | bytes 1179656 | tf_op jit(solution)/shard_map/ppermute | solution.py:16
  48.9 0.6 reduce_sum.55
  49.5 51.4 %psum.14 = f32[]{:T(128)} all-reduce(f32[]{:T(128)} %reduce_sum.55), channel_id=1, replica_groups=mesh['node'=2,'slab'=16] {'slab'}, use_global_device_ids=true, to_apply=%region_2.3 | all-reduce | flops 1 | bytes 8 | tf_op jit(solution)/shard_map/psum | solution.py:48
  100.9 0.6 dynamic-slice
  102.1 0.7 dynamic-update-slice
  102.8 2.4 %all-reduce.2 = f32[2]{0:T(128)S(1)} all-reduce(f32[2]{0:T(128)S(1)} %dynamic-update-slice), channel_id=1, replica_groups=mesh['node'=2,'slab'=16] {'node'}, use_global_device_ids=true, to_apply=%add.2 | all-reduce | flops 2 | bytes 16
  105.2 0.7 fusion.53
  105.9 1.4 %multiply_reduce_fusion.1 = f32[]{:T(128)} fusion(f32[2]{0:T(128)S(1)} %all-reduce.2, f32[]{:T(128)} %fusion.53), kind=kLoop, calls=%fused_computation.70 | loop fusion | flops 9 | bytes 16 | tf_op jit(solution)/shard_map/reduce_sum | solution.py:53
  107.3 2.0 %multiply_reduce_fusion = f32[]{:T(128)} fusion(f32[2]{0:T(128)S(1)} %all-reduce.2, f32[]{:T(128)} %multiply_reduce_fusion.1, f32[]{:T(128)} %fusion.53), kind=kLoop, calls=%fused_computation.69 | loop fusion | flops 13 | bytes 20 | tf_op jit(solution)/shard_map/reduce_sum | solution.py:54
  109.9 2.0 %fusion.52 = f32[]{:T(128)} fusion(f32[2]{0:T(128)S(1)} %all-reduce.2, f32[]{:T(128)S(6)} %sqrt.3, f32[]{:T(128)} %multiply_reduce_fusion.1, s32[]{:T(128)S(6)} %axis_index.19, f32[]{:T(128)} %fusion.53), kind=kLoop, calls=%fused_computation.68 | loop fusion | flops 21 | bytes 28 | tf_op jit(solution)/shard_map/reduce_sum | solution.py:57
  111.9 3.4 %select_maximum_fusion = f32[6,6,66,258]{3,0,2,1:T(8,128)S(1)} fusion(f32[6,1,64,256]{3,0,2,1:T(8,128)} %collective-permute-done.2, f32[6,4,64,256]{3,0,2,1:T(8,128)S(1)} %fusion.37, f32[6,1,64,256]{3,0,2,1:T(8,128)} %collective-permute-done.3), kind=kLoop, calls=%fused_computation.4 | loop fusion | flops 9195120 | bytes 4811328 | tf_op jit(solution)/shard_map/concatenate | solution.py:20
  115.3 9.1 %fusion.31 = f32[4,256]{1,0:T(4,128)S(1)} fusion(f32[6,4,64,256]{3,0,2,1:T(8,128)S(1)} %fusion.37, f32[1,6,4,64,256]{4,3,2,1,0:T(8,128)S(1)} %copy-done.2, f32[1,6,4,64,256]{4,3,2,1,0:T(8,128)S(1)} %copy-done.10, f32[6,6,66,258]{3,0,2,1:T(8,128)S(1)} %select_maximum_fusion, f32[6,1,64,256]{3,0,2,1:T(8,128)} %collective-permute-done.3, ...), kind=kOutput, calls=%fused_computation.42 | convolution fusion | flops 34995200 | bytes 17570816 | tf_op jit(solution)/shard_map/vw,vxyz->wxyz/dot_general | solution.py:30
  124.4 0.6 broadcast_multiply_fusion
  125.0 2.5 %psum.15 = f32[4,256]{1,0:T(4,128)S(1)} all-reduce(f32[4,256]{1,0:T(4,128)S(1)} %broadcast_multiply_fusion), channel_id=1, replica_groups=mesh['node'=2,'slab'=16] {'node'}, use_global_device_ids=true, to_apply=%region_7.8 | all-reduce | flops 1024 | bytes 8192 | tf_op jit(solution)/shard_map/psum | solution.py:59
  127.5 0.6 constant_dynamic-slice_fusion
  (24 shorter events, 0.0 us)
Async XLA Ops:
  1.3 9.4 %copy-start = (f32[1,4,4,64,256]{4,3,2,1,0:T(8,128)S(1)}, f32[1,4,4,64,256]{4,3,2,1,0:T(8,128)}, u32[]{:S(2)}) copy-start(f32[1,4,4,64,256]{4,3,2,1,0:T(8,128)} %param.6) | copy-start | bytes 3145732
  3.8 17.6 %collective-permute-start = (f32[6,1,64,256]{3,0,2,1:T(8,128)S(1)}, f32[6,1,64,256]{3,0,2,1:T(8,128)S(1)}, u32[]{:S(2)}, u32[]{:S(2)}) collective-permute-start(f32[6,1,64,256]{3,0,2,1:T(8,128)S(1)} %get-tuple-element.8), channel_id=1, source_target_pairs={{1,0},{2,1},{3,2},{4,3},{5,4},{6,5},{7,6},{8,7},{9,8},{10,9},{11,1... | collective-permute-start | bytes 1179656 | tf_op jit(solution)/shard_map/ppermute | solution.py:19
  5.1 27.8 %collective-permute-start.1 = (f32[6,1,64,256]{3,0,2,1:T(8,128)S(1)}, f32[6,1,64,256]{3,0,2,1:T(8,128)S(1)}, u32[]{:S(2)}, u32[]{:S(2)}) collective-permute-start(f32[6,1,64,256]{3,0,2,1:T(8,128)S(1)} %get-tuple-element.7), channel_id=1, source_target_pairs={{0,1},{1,2},{2,3},{3,4},{4,5},{5,6},{6,7},{7,8},{8,9},{9,10},{10,1... | collective-permute-start | bytes 1179656 | tf_op jit(solution)/shard_map/ppermute | solution.py:16
  10.7 24.4 %copy-start.3 = (f32[4,64,256]{2,1,0:T(8,128)}, f32[4,64,256]{2,1,0:T(8,128)S(1)}, u32[]{:S(2)}) copy-start(f32[4,64,256]{2,1,0:T(8,128)S(1)} %get-tuple-element.9) | copy-start | bytes 786436
  10.7 24.4 %copy-start.5 = (f32[4,64,256]{2,1,0:T(8,128)}, f32[4,64,256]{2,1,0:T(8,128)S(1)}, u32[]{:S(2)}) copy-start(f32[4,64,256]{2,1,0:T(8,128)S(1)} %get-tuple-element.10) | copy-start | bytes 786436
  10.7 24.4 %copy-start.7 = (f32[4,64,256]{2,1,0:T(8,128)}, f32[4,64,256]{2,1,0:T(8,128)S(1)}, u32[]{:S(2)}) copy-start(f32[4,64,256]{2,1,0:T(8,128)S(1)} %get-tuple-element.11) | copy-start | bytes 786436
  10.7 24.4 %copy-start.1 = (f32[1,6,4,64,256]{4,3,2,1,0:T(8,128)S(1)}, f32[1,6,4,64,256]{4,3,2,1,0:T(8,128)}, u32[]{:S(2)}) copy-start(f32[1,6,4,64,256]{4,3,2,1,0:T(8,128)} %param.5) | copy-start | bytes 4718596
  10.7 24.4 %copy-start.11 = (f32[1,6,6]{2,0,1:T(1,128)S(1)}, f32[1,6,6]{2,0,1:T(1,128)}, u32[]{:S(2)}) copy-start(f32[1,6,6]{2,0,1:T(1,128)} %param.7) | copy-start | bytes 436
  41.6 7.2 %copy-start.9 = (f32[1,4,256]{2,1,0:T(4,128)S(1)}, f32[1,4,256]{2,1,0:T(4,128)}, u32[]{:S(2)}) copy-start(f32[1,4,256]{2,1,0:T(4,128)} %param.9) | copy-start | bytes 12292
  41.6 59.2 %copy-start.12 = (u32[32]{0:T(128)S(1)}, u32[32]{0:T(128)}, u32[]{:S(2)}) copy-start(u32[32]{0:T(128)} %constant.44) | copy-start | bytes 388
  41.7 70.2 %collective-permute-start.2 = (f32[6,1,64,256]{3,0,2,1:T(8,128)S(1)}, f32[6,1,64,256]{3,0,2,1:T(8,128)}, u32[]{:S(2)}, u32[]{:S(2)}) collective-permute-start(f32[6,1,64,256]{3,0,2,1:T(8,128)S(1)} %get-tuple-element.6), channel_id=1, source_target_pairs={{1,0},{2,1},{3,2},{4,3},{5,4},{6,5},{7,6},{8,7},{9,8},{10,9},{11,1... | collective-permute-start | bytes 1179656 | tf_op jit(solution)/shard_map/ppermute | solution.py:19
  43.0 68.9 %collective-permute-start.3 = (f32[6,1,64,256]{3,0,2,1:T(8,128)S(1)}, f32[6,1,64,256]{3,0,2,1:T(8,128)}, u32[]{:S(2)}, u32[]{:S(2)}) collective-permute-start(f32[6,1,64,256]{3,0,2,1:T(8,128)S(1)} %get-tuple-element.5), channel_id=1, source_target_pairs={{0,1},{1,2},{2,3},{3,4},{4,5},{5,6},{6,7},{7,8},{8,9},{9,10},{10,1... | collective-permute-start | bytes 1179656 | tf_op jit(solution)/shard_map/ppermute | solution.py:16
  111.9 3.4 %copy-start.2 = (f32[1,6,4,64,256]{4,3,2,1,0:T(8,128)S(1)}, f32[1,6,4,64,256]{4,3,2,1,0:T(8,128)}, u32[]{:S(2)}) copy-start(f32[1,6,4,64,256]{4,3,2,1,0:T(8,128)} %param.5) | copy-start | bytes 4718596
  111.9 3.4 %copy-start.4 = (f32[4,64,256]{2,1,0:T(8,128)S(1)}, f32[4,64,256]{2,1,0:T(8,128)}, u32[]{:S(2)}) copy-start(f32[4,64,256]{2,1,0:T(8,128)} %copy-done.3) | copy-start | bytes 786436
  111.9 3.4 %copy-start.6 = (f32[4,64,256]{2,1,0:T(8,128)S(1)}, f32[4,64,256]{2,1,0:T(8,128)}, u32[]{:S(2)}) copy-start(f32[4,64,256]{2,1,0:T(8,128)} %copy-done.5) | copy-start | bytes 786436
  111.9 3.5 %copy-start.8 = (f32[4,64,256]{2,1,0:T(8,128)S(1)}, f32[4,64,256]{2,1,0:T(8,128)}, u32[]{:S(2)}) copy-start(f32[4,64,256]{2,1,0:T(8,128)} %copy-done.7) | copy-start | bytes 786436
  111.9 3.5 %copy-start.10 = (f32[1,6,4,64,256]{4,3,2,1,0:T(8,128)S(1)}, f32[1,6,4,64,256]{4,3,2,1,0:T(8,128)}, u32[]{:S(2)}) copy-start(f32[1,6,4,64,256]{4,3,2,1,0:T(8,128)} %param.8) | copy-start | bytes 4718596
where the time goes:
time: 128 us
  blocking collectives  56.3 us (44%)
  waiting for transfers between devices  22.2 us (17%)
  other arithmetic  16.5 us (13%)
  matrix products  15.5 us (12%)
  starting transfers between devices  13.9 us (11%)
  local copies, waits for them, and re-layouts  2.12 us (2%)
  between operations  1.56 us (1%)
    psum x1, blocking collectives, per_device(): node_sum = lax.psum(local_sum, 'slab')  51.4 us
    dot_general x2, matrix products, sweep(): jnp.einsum('vw,vxyz->wxyz', block, coupled, precision=lax.Precision.HIGHEST)  15.5 us
    ppermute x2, waiting for transfers between devices, with_halo(): lax.ppermute(lax.slice_in_dim(block, block.shape[dim] - width, None, axis...  11.5 us
    ppermute x2, starting transfers between devices, with_halo(): lax.ppermute(lax.slice_in_dim(block, block.shape[dim] - width, None, axis...  11.3 us
    ppermute x2, waiting for transfers between devices, with_halo(): lax.ppermute(lax.slice_in_dim(block, 0, width, axis=dim), axis, backward)  10.7 us
    concatenate x2, other arithmetic, with_halo(): block = jnp.concatenate([low, block, high], axis=dim)  5.56 us
    ppermute x2, starting transfers between devices, with_halo(): lax.ppermute(lax.slice_in_dim(block, 0, width, axis=dim), axis, backward)  2.58 us
  transfers between devices with their start and end apart: 4, of which 2 were waited for; matrix products, arithmetic and copies ran while one was open for 6% of the time, Pallas kernels for 0%

commit v1 on v0

v1 whole, which is shorter than its diff:
```python
import functools
import math

import jax
import jax.numpy as jnp
from jax import lax
from jax.experimental import pallas as pl
from jax.experimental.pallas import tpu as pltpu
from jax.sharding import PartitionSpec as P

ROWS = 8
COST = {"edge_messages": 4, "halo_terms": 2, "first_sweep": 2, "last_sweep": 1}
LIMIT = {"edge_state": 62}


def call(kernel, name, **kw):
    us, limit = COST.get(name, 0), LIMIT.get(name, 24)
    return pl.pallas_call(
        kernel,
        compiler_params=pltpu.CompilerParams(vmem_limit_bytes=limit * 1024 * 1024),
        cost_estimate=pl.CostEstimate(flops=int(us * 1.1e9), bytes_accessed=0, transcendentals=0),
        name=name,
        **kw,
    )


def f32(*shape):
    return jax.ShapeDtypeStruct(shape, jnp.float32)


VMEM = pl.BlockSpec(memory_space=pltpu.VMEM)
SMEM = pl.BlockSpec(memory_space=pltpu.SMEM)
ANY = pl.BlockSpec(memory_space=pl.ANY)


def edge_of(slot, planes):
    up = lax.rem(lax.axis_index("slab") + slot, 2) == 0
    return jnp.where(up, planes - 1, 0)


def inverse_diag(c):
    return 1.0 / (0.5 + c(0) + 2.4 * (c(1) + c(2) + c(3)))


def shift_sum(p, axis):
    size = p.shape[axis]
    place = lax.broadcasted_iota(jnp.int32, p.shape, axis)
    ahead = jnp.where(place < size - 1, pltpu.roll(p, size - 1, axis), 0.0)
    behind = jnp.where(place > 0, pltpu.roll(p, 1, axis), 0.0)
    return ahead + behind


def edge_kernel(
    s_ref, c_ref, wall_ref, u0, u1, wsum_ref, s_buf, c_buf, u_buf, wall_buf, wsum_buf, c_sems, s_sems, u_sems, wall_sems
):
    nv, nx = s_ref.shape[1:3]
    wall_in = pltpu.make_async_copy(wall_ref.at[0], wall_buf, wall_sems.at[0])
    wall_out = pltpu.make_async_copy(wsum_buf, wsum_ref, wall_sems.at[1])
    wall_in.start()
    edges = [edge_of(slot, nx) for slot in (0, 1)]
    c_copies = [pltpu.make_async_copy(c_ref.at[0, :, e], c_buf.at[j], c_sems.at[j]) for j, e in enumerate(edges)]
    s_copies = [
        [pltpu.make_async_copy(s_ref.at[0, v, e], s_buf.at[j, v], s_sems.at[j, v]) for v in range(nv)]
        for j, e in enumerate(edges)
    ]
    u_copies = [
        [pltpu.make_async_copy(u_buf.at[j, v], u.at[v], u_sems.at[j, v]) for v in range(nv)]
        for j, u in enumerate((u0, u1))
    ]
    for j in (0, 1):
        c_copies[j].start()
        for copy in s_copies[j]:
            copy.start()
    wall_in.wait()
    wall = jnp.sum(jnp.sum(wall_buf[...], axis=0, keepdims=True), axis=1, keepdims=True)
    rows = lax.broadcasted_iota(jnp.int32, wsum_buf.shape, 0)
    wsum_buf[...] = jnp.where(rows == lax.axis_index("node"), wall, 0.0)
    wall_out.start()
    for j in (0, 1):
        c_copies[j].wait()
        inv = inverse_diag(lambda k: c_buf[j, k])
        for v in range(nv):
            s_copies[j][v].wait()
            u_buf[j, v] = s_buf[j, v] * inv
            u_copies[j][v].start()
    wall_out.wait()
    for j in (0, 1):
        for copy in u_copies[j]:
            copy.wait()


def edge_state(source, coef, wall):
    nv, ny, nz = source.shape[1], source.shape[3], source.shape[4]
    return call(
        edge_kernel,
        "edge_state",
        out_shape=(f32(nv, ny, nz),) * 2 + (f32(ROWS, 128),),
        in_specs=[ANY] * 3,
        out_specs=(ANY,) * 3,
        scratch_shapes=[
            pltpu.VMEM((2, nv, ny, nz), jnp.float32),
            pltpu.VMEM((2, 4, ny, nz), jnp.float32),
            pltpu.VMEM((2, nv, ny, nz), jnp.float32),
            pltpu.VMEM(wall.shape[1:], jnp.float32),
            pltpu.VMEM((ROWS, 128), jnp.float32),
            pltpu.SemaphoreType.DMA((2,)),
            pltpu.SemaphoreType.DMA((2, nv)),
            pltpu.SemaphoreType.DMA((2, nv)),
            pltpu.SemaphoreType.DMA((2,)),
        ],
    )(source, coef, wall)


def share(buf, parts, rows, part):
    width = buf.shape[1] // parts
    if parts == 1:
        return buf[pl.ds(0, rows), :]
    node = lax.axis_index("node")
    at = pl.multiple_of((node if part == 0 else 1 - node) * width, width)
    return buf[pl.ds(0, rows), pl.ds(at, width)]


def coupled(c_ref, x, below, here, above):
    q = c_ref[0, 1, x] * (below + above)
    q = q + c_ref[0, 2, x] * shift_sum(here, 0)
    return q + c_ref[0, 3, x] * shift_sum(here, 1)


def mixed(f_ref, w, q):
    mix = f_ref[0, 0, w] * q(0)
    for v in range(1, f_ref.shape[1]):
        mix = mix + f_ref[0, v, w] * q(v)
    return mix


def message_kernel(parts, f_ref, s_ref, c_ref, after, *refs):
    del after
    msgs, (q_ref, p_ref, full) = refs[: 2 * parts], refs[2 * parts :]
    nv, nx, ny, nz = s_ref.shape[1:]
    zero = jnp.zeros((ny, nz), jnp.float32)
    for slot in (0, 1):
        edge = edge_of(slot, nx)
        inner = jnp.where(edge == 0, min(1, nx - 1), max(nx - 2, 0))
        inv = inverse_diag(lambda k: c_ref[0, k, edge])
        inv_inner = inverse_diag(lambda k: c_ref[0, k, inner])
        for v in range(nv):
            p_ref[v] = s_ref[0, v, edge] * inv
            beside = s_ref[0, v, inner] * inv_inner
            q_ref[v] = coupled(c_ref, edge, beside, p_ref[v], zero)
        for w in range(nv):
            full[pl.ds(w * ny, ny), :] = p_ref[w] + inv * mixed(f_ref, w, lambda v: q_ref[v])
        full[pl.ds(nv * ny, ny), :] = c_ref[0, 1, edge] * inv
        for part in range(parts):
            msgs[slot * parts + part][...] = share(full, parts, (nv + 1) * ny, part)


def messages(parts, block, source, coef, after):
    nv, nx, ny, nz = source.shape[1:]
    rows = (nv + 1) * ny
    return call(
        functools.partial(message_kernel, parts),
        "edge_messages",
        out_shape=(f32(rows, nz // parts),) * (2 * parts),
        in_specs=[SMEM] + [VMEM] * 2 + [ANY],
        out_specs=(VMEM,) * (2 * parts),
        scratch_shapes=[pltpu.VMEM((nv, ny, nz), jnp.float32)] * 2 + [pltpu.VMEM((rows, nz), jnp.float32)],
    )(block, source, coef, after)


def first_kernel(parts, f_ref, s_ref, c_ref, m_ref, after, p1_ref, b_ref, sens_ref, *refs):
    del after
    weights, (p0, q_ref, inv_ref, full) = refs[:parts], refs[parts:]
    nv, nx, ny, nz = s_ref.shape[1:]
    zero = jnp.zeros((ny, nz), jnp.float32)
    for v in range(nv):
        p0[v, 0] = zero
        p0[v, nx + 1] = zero

    def start(x, _):
        inv = inverse_diag(lambda k: c_ref[0, k, x])
        inv_ref[x] = inv
        own = zero
        for v in range(nv):
            p = s_ref[0, v, x] * inv
            p0[v, x + 1] = p
            own = own + m_ref[0, v, x] * p
            q_ref[v] = m_ref[0, v, x] * inv
        sens_ref[pl.ds(x, 1), :] = jnp.sum(own, axis=0, keepdims=True)
        for v in range(nv):
            b = f_ref[0, v, 0] * q_ref[0]
            for w in range(1, nv):
                b = b + f_ref[0, v, w] * q_ref[w]
            b_ref[v, x] = b
        return 0

    lax.fori_loop(0, nx, start, 0)

    def first(x, _):
        for v in range(nv):
            q_ref[v] = coupled(c_ref, x, p0[v, x], p0[v, x + 1], p0[v, x + 2])
        for w in range(nv):
            p1_ref[w, x] = p0[w, x + 1] + inv_ref[x] * mixed(f_ref, w, lambda v: q_ref[v])
        return 0

    lax.fori_loop(0, nx, first, 0)

    rows = (nv + 1) * ny
    for slot in (0, 1):
        edge = edge_of(slot, nx)
        total = zero
        for w in range(nv):
            weight = c_ref[0, 1, edge] * b_ref[w, edge]
            full[pl.ds(slot * rows + w * ny, ny), :] = weight
            total = total + weight * mixed(f_ref, w, lambda v: p0[v, edge + 1])
        full[pl.ds(slot * rows + nv * ny, ny), :] = total
    for part, weight in enumerate(weights):
        weight[...] = share(full, parts, full.shape[0], part)


def first_sweep(parts, block, source, coef, metric, after):
    nv, nx, ny, nz = source.shape[1:]
    rows = 2 * (nv + 1) * ny
    return call(
        functools.partial(first_kernel, parts),
        "first_sweep",
        out_shape=(f32(nv, nx, ny, nz), f32(nv, nx, ny, nz), f32(nx, nz)) + (f32(rows, nz // parts),) * parts,
        in_specs=[SMEM] + [VMEM] * 3 + [ANY],
        out_specs=(VMEM,) * (3 + parts),
        scratch_shapes=[
            pltpu.VMEM((nv, nx + 2, ny, nz), jnp.float32),
            pltpu.VMEM((nv, ny, nz), jnp.float32),
            pltpu.VMEM((nx, ny, nz), jnp.float32),
            pltpu.VMEM((rows, nz), jnp.float32),
        ],
    )(block, source, coef, metric, after)


def last_kernel(c_ref, p1_ref, b_ref, base_ref, out_ref):
    nv, nx, ny, nz = b_ref.shape
    zero = jnp.zeros((ny, nz), jnp.float32)
    for x in range(nx):
        along = [zero, zero, zero]
        for v in range(nv):
            b = b_ref[v, x]
            p = p1_ref[v, x]
            beside = [p1_ref[v, at] for at in (x - 1, x + 1) if 0 <= at < nx]
            along[0] = along[0] + b * sum(beside[1:], beside[0])
            along[1] = along[1] + b * shift_sum(p, 0)
            along[2] = along[2] + b * shift_sum(p, 1)
        own = c_ref[0, 1, x] * along[0] + c_ref[0, 2, x] * along[1] + c_ref[0, 3, x] * along[2]
        out_ref[x : x + 1, :] = base_ref[x : x + 1, :] + jnp.sum(own, axis=0, keepdims=True)


def last_sweep(coef, p1, b, base):
    return call(
        last_kernel,
        "last_sweep",
        out_shape=f32(*base.shape),
        in_specs=[VMEM] * 4,
        out_specs=VMEM,
    )(coef, p1, b, base)


def halo_kernel(nodes, f_ref, c_ref, b_ref, sens_in, sums_ref, u0, u1, out_ref, g_ref, acc):
    nv, nx, ny, nz = b_ref.shape
    acc[...] = sens_in[...]
    for slot, u in ((0, u0), (1, u1)):
        edge = edge_of(slot, nx)
        inner = jnp.where(edge == 0, 1, nx - 2)
        rho = c_ref[0, 1, edge] * inverse_diag(lambda k: c_ref[0, k, edge])
        here = [jnp.zeros((ny, nz), jnp.float32)] * 3
        for w in range(nv):
            g_ref[w] = rho * mixed(f_ref, w, lambda v: u[v])
        for w in range(nv):
            g = g_ref[w]
            here[0] = here[0] + b_ref[w, inner] * g
            here[1] = here[1] + b_ref[w, edge] * shift_sum(g, 0)
            here[2] = here[2] + b_ref[w, edge] * shift_sum(g, 1)
        there = c_ref[0, 1, inner] * here[0]
        own = c_ref[0, 2, edge] * here[1] + c_ref[0, 3, edge] * here[2]
        acc[pl.ds(inner, 1), :] += jnp.sum(there, axis=0, keepdims=True)
        acc[pl.ds(edge, 1), :] += jnp.sum(own, axis=0, keepdims=True)
    out_ref[...] = jnp.zeros_like(out_ref)
    out_ref[pl.ds(pl.multiple_of(lax.axis_index("node") * ROWS, ROWS), nx), :] = acc[...]
    out_ref[pl.ds(nodes * ROWS, ROWS), pl.ds(0, 128)] = sums_ref[...]


def halo_terms(nodes, block, coef, b, sens, sums, u0, u1):
    nv, nx, ny, nz = b.shape
    assert 1 < nx <= ROWS
    return call(
        functools.partial(halo_kernel, nodes),
        "halo_terms",
        out_shape=f32((nodes + 1) * ROWS, nz),
        in_specs=[SMEM] + [VMEM] * 6,
        out_specs=VMEM,
        scratch_shapes=[pltpu.VMEM((nv, ny, nz), jnp.float32), pltpu.VMEM((nx, nz), jnp.float32)],
    )(block, coef, b, sens, sums, u0, u1)


def factors(nodes, cells, sums):
    raw = [math.sin(math.pi * (n + 0.5) / nodes) for n in range(nodes)]
    weight = [r / sum(raw) for r in raw]
    objective = [sums[n : n + 1, :] * (1.0 / cells) for n in range(nodes)]
    mean = sum(w * o for w, o in zip(weight, objective))
    variance = sum(w * (o - mean) ** 2 for w, o in zip(weight, objective))
    spread = jnp.sqrt(variance + 0.25)
    return [w * (1.0 + 2.0 * (o - mean) / spread) for w, o in zip(weight, objective)]


def final_kernel(parts, nodes, cells, all_ref, *refs):
    weights, msgs = refs[:parts], refs[parts : 3 * parts]
    out_ref, acc = refs[3 * parts :]
    nx, width = out_ref.shape
    rows = msgs[0].shape[0]
    factor = factors(nodes, cells, all_ref[pl.ds(nodes * ROWS, ROWS), pl.ds(0, 128)])
    node = lax.axis_index("node")
    if parts == 1:
        acc[...] = all_ref[pl.ds(pl.multiple_of(node * ROWS, ROWS), ROWS), :]
    else:
        near = share(all_ref, parts, nodes * ROWS, 0)
        acc[...] = sum(factor[n][:, :1] * near[n * ROWS : (n + 1) * ROWS, :] for n in range(nodes))
    for part in range(parts):
        whose = node if part == 0 else 1 - node
        mine = factor[0]
        for n in range(1, nodes):
            mine = jnp.where(whose == n, factor[n], mine)
        for slot in (0, 1):
            total = weights[part][pl.ds(slot * rows, rows), :] * msgs[slot * parts + part][...]
            total = jnp.sum(total, axis=0, keepdims=True)
            acc[pl.ds(edge_of(slot, nx), 1), :] += total * mine[:, :1] if parts > 1 else total
    out_ref[...] = acc[pl.ds(0, nx), :] * (1.0 if parts > 1 else mine[:, :1])


def final_terms(parts, nodes, cells, nx, everything, weights, msgs):
    width = msgs[0].shape[1]
    return call(
        functools.partial(final_kernel, parts, nodes, cells),
        "final_terms",
        out_shape=f32(nx, width),
        in_specs=[VMEM] * (1 + 3 * parts),
        out_specs=VMEM,
        scratch_shapes=[pltpu.VMEM((ROWS, width), jnp.float32)],
    )(everything, *weights, *msgs)


def swap_pairs(value, slot, part=0):
    count, nodes = lax.axis_size("slab"), lax.axis_size("node")
    pairs = []
    for low in range(slot, count - 1, 2):
        pairs += [(low, low + 1), (low + 1, low)]
    if part == 0:
        return lax.ppermute(value, "slab", pairs)
    cross = [(n * count + a, (1 - n) * count + b) for n in range(nodes) for a, b in pairs]
    return lax.ppermute(value, ("node", "slab"), cross)


def from_partner(value, slab, node=0):
    count, nodes = lax.axis_size("slab"), lax.axis_size("node")
    pairs = [(n * count + i, (n ^ node) * count + (i ^ slab)) for n in range(nodes) for i in range(count)]
    return lax.ppermute(value, ("node", "slab"), pairs)


def sum_steps(count):
    assert count & (count - 1) == 0
    steps = [1 << k for k in range(1, count.bit_length() - 1)]
    return steps + [1 ^ (4 if count > 4 else 0)] if count > 1 else []


def per_device(source, coef, block, metric, wall):
    nodes, slabs = lax.axis_size("node"), lax.axis_size("slab")
    nx = source.shape[2]
    cells = wall.shape[1] * slabs * wall.shape[2]
    parts = 1
    own0, own1, wsum = edge_state(source, coef, wall)
    u0, u1 = swap_pairs(own0, 0), swap_pairs(own1, 1)
    own = messages(parts, block, source, coef, wsum)
    msgs = [swap_pairs(m, k // parts, k % parts) for k, m in enumerate(own)]
    sums = wsum
    for slab in sum_steps(slabs):
        sums = sums + from_partner(sums, slab)
    p1, b, sens, *weights = first_sweep(parts, block, source, coef, metric, own[0])
    sens = last_sweep(coef, p1, b, sens)
    everything = lax.psum(halo_terms(nodes, block, coef, b, sens, sums, u0, u1), "node")
    if parts == 2:
        weights[1] = lax.ppermute(weights[1], "node", [(0, 1), (1, 0)])
        return final_terms(parts, nodes, cells, nx, everything, weights, msgs)
    term = final_terms(parts, nodes, cells, nx, everything, weights, msgs)
    total = lax.psum(term, "node")
    width = term.shape[1] // nodes
    return lax.dynamic_slice_in_dim(total, lax.axis_index("node") * width, width, 1)


def solution(mesh):
    return jax.shard_map(
        per_device,
        mesh=mesh,
        in_specs=(
            P("node", None, "slab", None, None),
            P("node", None, "slab", None, None),
            P("node", None, None),
            P("node", None, "slab", None, None),
            P("node", "slab", None),
        ),
        out_specs=P("slab", "node"),
        check_vma=False,
    )
```

time: 128 us -> 47.2 us (0.37)
  blocking collectives: 56.3 us -> 5.88 us
  other arithmetic: 16.5 us -> 0.69 us
  matrix products: 15.5 us -> 0 us
  waiting for transfers between devices: 22.2 us -> 9.95 us
  Pallas kernels: 0 us -> 12.1 us
  local copies, waits for them, and re-layouts: 2.12 us -> 4.08 us
  between operations: 1.56 us -> 0.08 us
    psum x1, blocking collectives: 51.4 us -> 3.41 us  [per_device(): lax.psum(halo_terms(nodes, block, coef, b, sens, sums, u0, u1), 'node')]
    dot_general x2 -> x0, matrix products: 15.5 us -> none  [sweep(): jnp.einsum('vw,vxyz->wxyz', block, coupled, precision=lax.Precision.HIGHEST)]
    ppermute x4 -> x8, waiting for transfers between devices: 22.2 us -> 9.95 us  [the longest x4 9.86 us: from_partner(): return lax.ppermute(value, ('node', 'slab'), pairs)]
    pallas_call x0 -> x6, Pallas kernels: none -> 12.1 us  [the longest x1 3.88 us: first_sweep(): call(functools.partial(first_kernel, parts), 'first_sweep', out_shape=(f3...]
    reduce_sum x5 -> x0, other arithmetic: 6.6 us -> none  [the longest x1 1.99 us: per_device(): jnp.sum(jnp.where(jnp.arange(nodes) == lax.axis_index('node'), factor, 0.0))]
    concatenate x2 -> x0, other arithmetic: 5.56 us -> none  [with_halo(): block = jnp.concatenate([low, block, high], axis=dim)]
    div x1 -> x0, other arithmetic: 2.45 us -> none  [per_device(): psi = source / diag]
    unnamed x1 -> x0, blocking collectives: 2.44 us -> none
  transfers between devices with their start and end apart: 4 -> 8, of which waited for: 2 -> 4; matrix products, arithmetic and copies ran while one was open for 6% -> 1% of each run, Pallas kernels for 0% -> 20%
where the time goes in v1:
time: 47.2 us; the launch traced here: 46.8 us
  starting transfers between devices  14.1 us (30%)
  Pallas kernels  12.1 us (26%)
  waiting for transfers between devices  9.95 us (21%)
  blocking collectives  5.88 us (12%)
  local copies, waits for them, and re-layouts  4.08 us (9%)
  other arithmetic  0.69 us (1%)
    ppermute x4, waiting for transfers between devices, from_partner(): return lax.ppermute(value, ('node', 'slab'), pairs)  9.86 us
    ppermute x4, starting transfers between devices, from_partner(): return lax.ppermute(value, ('node', 'slab'), pairs)  8.57 us
    ppermute x4, starting transfers between devices, swap_pairs(): return lax.ppermute(value, 'slab', pairs)  5.53 us
    pallas_call x1, Pallas kernels, first_sweep(): call(functools.partial(first_kernel, parts), 'first_sweep', out_shape=(f3...  3.88 us
    unnamed x15, local copies, waits for them, and re-layouts  3.5 us
    psum x1, blocking collectives, per_device(): lax.psum(halo_terms(nodes, block, coef, b, sens, sums, u0, u1), 'node')  3.41 us
    pallas_call x1, Pallas kernels, edge_state(): call(edge_kernel, 'edge_state', out_shape=(f32(nv, ny, nz),) * 2 + (f32(R...  2.52 us
    psum x1, blocking collectives, per_device(): total = lax.psum(term, 'node')  2.47 us
  transfers between devices with their start and end apart: 8, of which 4 were waited for; matrix products, arithmetic and copies ran while one was open for 1% of the time, Pallas kernels for 20%

profile of v1, /device:TPU:0, one launch (start us, length us, event | category | flops | bytes accessed | tf_op | source)
XLA Modules:
  0.0 46.8 jit_solution(10339407731561804431)
XLA Ops:
  0.0 2.5 %edge_state.1 = (f32[6,64,256]{2,1,0:T(8,128)}, f32[6,64,256]{2,1,0:T(8,128)}, f32[8,128]{1,0:T(8,128)}) custom-call(f32[1,6,4,64,256]{4,3,2,1,0:T(8,128)} %s_ref.5, f32[1,4,4,64,256]{4,3,2,1,0:T(8,128)} %c_ref.9, f32[1,4,256]{2,1,0:T(4,128)} %wall_ref.1), custom_call_target="tpu_custom_call" | custom-call | tf_op jit(solution)/shard_map/edge_state/pallas_call | solution.py:94
  2.5 3.0 %collective-permute-start = (f32[8,128]{1,0:T(8,128)}, f32[8,128]{1,0:T(8,128)S(1)}, u32[]{:S(2)}, u32[]{:S(2)}) collective-permute-start(f32[8,128]{1,0:T(8,128)} %get-tuple-element.14.after), channel_id=1, source_target_pairs={{0,2},{1,3},{2,0},{3,1},{4,6},{5,7},{6,4},{7,5},{8,10},{9,11},{10,... | collective-permute-start | bytes 12296 | tf_op jit(solution)/shard_map/ppermute | solution.py:361
  5.6 1.5 %collective-permute-start.4 = (f32[6,64,256]{2,1,0:T(8,128)}, f32[6,64,256]{2,1,0:T(8,128)}, u32[]{:S(2)}, u32[]{:S(2)}) collective-permute-start(f32[6,64,256]{2,1,0:T(8,128)} %get-tuple-element.19), channel_id=1, source_target_pairs={{0,1},{1,0},{2,3},{3,2},{4,5},{5,4},{6,7},{7,6},{8,9},{9,8},{10,11... | collective-permute-start | bytes 1179656 | tf_op jit(solution)/shard_map/ppermute | solution.py:353
  7.1 1.4 %collective-permute-start.5 = (f32[6,64,256]{2,1,0:T(8,128)}, f32[6,64,256]{2,1,0:T(8,128)}, u32[]{:S(2)}, u32[]{:S(2)}) collective-permute-start(f32[6,64,256]{2,1,0:T(8,128)} %get-tuple-element.20), channel_id=1, source_target_pairs={{1,2},{2,1},{3,4},{4,3},{5,6},{6,5},{7,8},{8,7},{9,10},{10,9},{11,... | collective-permute-start | bytes 1179656 | tf_op jit(solution)/shard_map/ppermute | solution.py:353
  8.5 0.0 collective-permute-done
  8.5 0.7 %add.19 = f32[8,128]{1,0:T(8,128)S(1)} add(f32[8,128]{1,0:T(8,128)} %get-tuple-element.14.after, f32[8,128]{1,0:T(8,128)S(1)} %collective-permute-done) | non-fusion elementwise | flops 1024 | bytes 12288 | tf_op jit(solution)/shard_map/add | solution.py:381
  9.1 2.1 %collective-permute-start.1 = (f32[8,128]{1,0:T(8,128)S(1)}, f32[8,128]{1,0:T(8,128)S(1)}, u32[]{:S(2)}, u32[]{:S(2)}) collective-permute-start(f32[8,128]{1,0:T(8,128)S(1)} %add.19), channel_id=1, source_target_pairs={{0,4},{1,5},{2,6},{3,7},{4,0},{5,1},{6,2},{7,3},{8,12},{9,13},{10,... | collective-permute-start | bytes 12296 | tf_op jit(solution)/shard_map/ppermute | solution.py:361
  11.3 0.0 copy-done
  11.3 1.4 %copy-done.1 = f32[1,6,4,64,256]{4,3,2,1,0:T(8,128)S(1)} copy-done((f32[1,6,4,64,256]{4,3,2,1,0:T(8,128)S(1)}, f32[1,6,4,64,256]{4,3,2,1,0:T(8,128)}, u32[]{:S(2)}) %copy-start.1) | copy-done | bytes 1572888
  12.7 0.7 %copy-done.4 = f32[8,128]{1,0:T(8,128)S(1)} copy-done((f32[8,128]{1,0:T(8,128)S(1)}, f32[8,128]{1,0:T(8,128)}, u32[]{:S(2)}) %copy-start.4) | copy-done | bytes 4120
  13.3 2.2 %edge_messages.1 = (f32[448,256]{1,0:T(8,128)}, f32[448,256]{1,0:T(8,128)S(1)}) custom-call(f32[1,6,6]{2,1,0:T(8,128)S(1)} %copy.8.f_ref, f32[1,6,4,64,256]{4,3,2,1,0:T(8,128)S(1)} %copy-done.1, f32[1,4,4,64,256]{4,3,2,1,0:T(8,128)S(1)} %copy-done, f32[8,128]{1,0:T(8,128)S(1)} %copy-done.4), custom_call_target="tpu_custom_call" | custom-call | flops 4400000000 | tf_op jit(solution)/shard_map/edge_messages/pallas_call | solution.py:160
  15.6 2.0 %collective-permute-start.6 = (f32[448,256]{1,0:T(8,128)}, f32[448,256]{1,0:T(8,128)S(1)}, u32[]{:S(2)}, u32[]{:S(2)}) collective-permute-start(f32[448,256]{1,0:T(8,128)} %get-tuple-element.15.after), channel_id=1, source_target_pairs={{0,1},{1,0},{2,3},{3,2},{4,5},{5,4},{6,7},{7,6},{8,9},{9,8},{10,11... | collective-permute-start | bytes 1376264 | tf_op jit(solution)/shard_map/ppermute | solution.py:353
  17.5 0.7 %collective-permute-start.7 = (f32[448,256]{1,0:T(8,128)S(1)}, f32[448,256]{1,0:T(8,128)S(1)}, u32[]{:S(2)}, u32[]{:S(2)}) collective-permute-start(f32[448,256]{1,0:T(8,128)S(1)} %get-tuple-element.22), channel_id=1, source_target_pairs={{1,2},{2,1},{3,4},{4,3},{5,6},{6,5},{7,8},{8,7},{9,10},{10,9},{11,... | collective-permute-start | bytes 1376264 | tf_op jit(solution)/shard_map/ppermute | solution.py:353
  18.2 1.2 %collective-permute-done.1 = f32[8,128]{1,0:T(8,128)S(1)} collective-permute-done((f32[8,128]{1,0:T(8,128)S(1)}, f32[8,128]{1,0:T(8,128)S(1)}, u32[]{:S(2)}, u32[]{:S(2)}) %collective-permute-start.1) | collective-permute-done | bytes 4128 | tf_op jit(solution)/shard_map/ppermute | solution.py:361
  19.4 3.4 %collective-permute-start.2 = (f32[8,128]{1,0:T(8,128)S(1)}, f32[8,128]{1,0:T(8,128)S(1)}, u32[]{:S(2)}, u32[]{:S(2)}) collective-permute-start(f32[8,128]{1,0:T(8,128)S(1)} %add.20), channel_id=1, source_target_pairs={{0,8},{1,9},{2,10},{3,11},{4,12},{5,13},{6,14},{7,15},{8,0},{9,1},... | collective-permute-start | bytes 12296 | tf_op jit(solution)/shard_map/ppermute | solution.py:361
  22.8 0.0 copy-done.5
  22.8 3.9 %first_sweep.1 = (f32[6,4,64,256]{3,2,1,0:T(8,128)S(1)}, f32[6,4,64,256]{3,2,1,0:T(8,128)S(1)}, f32[4,256]{1,0:T(4,128)S(1)}, f32[896,256]{1,0:T(8,128)S(1)}) custom-call(f32[1,6,6]{2,1,0:T(8,128)S(1)} %copy.8.f_ref, f32[1,6,4,64,256]{4,3,2,1,0:T(8,128)S(1)} %copy-done.1, f32[1,4,4,64,256]{4,3,2,1,0:T(8,128)S(1)} %copy-done, ...), custom_call_target="tpu_custom_call" | custom-call | flops 2200000000 | tf_op jit(solution)/shard_map/first_sweep/pallas_call | solution.py:223
  26.7 0.0 copy-start.2
  26.7 5.4 %collective-permute-done.2 = f32[8,128]{1,0:T(8,128)S(1)} collective-permute-done((f32[8,128]{1,0:T(8,128)S(1)}, f32[8,128]{1,0:T(8,128)S(1)}, u32[]{:S(2)}, u32[]{:S(2)}) %collective-permute-start.2) | collective-permute-done | bytes 4128 | tf_op jit(solution)/shard_map/ppermute | solution.py:361
  32.1 0.0 collective-permute-start.3
  32.1 1.3 %last_sweep.1.sens_in = f32[4,256]{1,0:T(4,128)S(1)} custom-call(f32[1,4,4,64,256]{4,3,2,1,0:T(8,128)S(1)} %copy-done, f32[6,4,64,256]{3,2,1,0:T(8,128)S(1)} %get-tuple-element.17.p1_ref, f32[6,4,64,256]{3,2,1,0:T(8,128)S(1)} %get-tuple-element.16.b_ref, f32[4,256]{1,0:T(4,128)S(1)} %get-tuple-element.18.base_ref), custom_call_target="tpu_custom_call" | custom-call | flops 1100000000 | tf_op jit(solution)/shard_map/last_sweep/pallas_call | solution.py:255
  33.4 3.3 %collective-permute-done.3 = f32[8,128]{1,0:T(8,128)S(1)} collective-permute-done((f32[8,128]{1,0:T(8,128)S(1)}, f32[8,128]{1,0:T(8,128)S(1)}, u32[]{:S(2)}, u32[]{:S(2)}) %collective-permute-start.3) | collective-permute-done | bytes 4128 | tf_op jit(solution)/shard_map/ppermute | solution.py:361
  36.7 0.0 collective-permute-done.4.u0
  36.7 0.0 collective-permute-done.5.u1
  36.7 1.4 %copy-done.3 = f32[6,4,64,256]{3,2,1,0:T(8,128)S(1)} copy-done((f32[6,4,64,256]{3,2,1,0:T(8,128)S(1)}, f32[6,4,64,256]{3,2,1,0:T(8,128)}, u32[]{:S(2)}) %copy-start.3) | copy-done | bytes 1572888
  38.1 2.0 %halo_terms.1 = f32[24,256]{1,0:T(8,128)S(1)} custom-call(f32[1,6,6]{2,1,0:T(8,128)S(1)} %copy.8.f_ref, f32[1,4,4,64,256]{4,3,2,1,0:T(8,128)S(1)} %copy-done, f32[6,4,64,256]{3,2,1,0:T(8,128)S(1)} %copy-done.3, f32[4,256]{1,0:T(4,128)S(1)} %last_sweep.1.sens_in, f32[8,128]{1,0:T(8,128)S(1)} %add.22.sums_ref, f32[6,64,256]{2,1,0:T(8,128)} %collective-permute-done.4.u0, ...), custom_call_target="tpu_custom_call" | custom-call | flops 2200000000 | tf_op jit(solution)/shard_map/halo_terms/pallas_call | solution.py:291
  40.1 3.4 %psum.14.all_ref = f32[24,256]{1,0:T(8,128)S(1)} all-reduce(f32[24,256]{1,0:T(8,128)S(1)} %halo_terms.1), channel_id=1, replica_groups=mesh['node'=2,'slab'=16] {'node'}, use_global_device_ids=true, to_apply=%region_0.0 | all-reduce | flops 6144 | bytes 49152 | tf_op jit(solution)/shard_map/psum | solution.py:384
  43.6 0.1 collective-permute-done.6.refs_1_
  43.6 0.0 collective-permute-done.7.refs_2_
  43.6 0.1 final_terms.1
  43.8 2.5 %psum.15 = f32[4,256]{1,0:T(4,128)S(1)} all-reduce(f32[4,256]{1,0:T(4,128)S(1)} %final_terms.1), channel_id=1, replica_groups=mesh['node'=2,'slab'=16] {'node'}, use_global_device_ids=true, to_apply=%region_1.0 | all-reduce | flops 1024 | bytes 8192 | tf_op jit(solution)/shard_map/psum | solution.py:389
  46.3 0.6 %constant_dynamic-slice_fusion = f32[4,128]{1,0:T(4,128)} fusion(f32[4,256]{1,0:T(4,128)S(1)} %psum.15, s32[]{:T(128)S(6)} %select_n.3), kind=kLoop, calls=%fused_computation | loop fusion | bytes 4100 | tf_op jit(solution)/shard_map/dynamic_slice | solution.py:391
  (12 shorter events, 0.0 us)
Async XLA Ops:
  0.0 11.3 %copy-start = (f32[1,4,4,64,256]{4,3,2,1,0:T(8,128)S(1)}, f32[1,4,4,64,256]{4,3,2,1,0:T(8,128)}, u32[]{:S(2)}) copy-start(f32[1,4,4,64,256]{4,3,2,1,0:T(8,128)} %c_ref.9) | copy-start | bytes 3145732
  0.0 8.5 %copy-start.6 = (f32[1,6,6]{2,0,1:T(1,128)S(1)}, f32[1,6,6]{2,0,1:T(1,128)}, u32[]{:S(2)}) copy-start(f32[1,6,6]{2,0,1:T(1,128)} %param.7) | copy-start | bytes 436
  2.5 5.9 %collective-permute-start = (f32[8,128]{1,0:T(8,128)}, f32[8,128]{1,0:T(8,128)S(1)}, u32[]{:S(2)}, u32[]{:S(2)}) collective-permute-start(f32[8,128]{1,0:T(8,128)} %get-tuple-element.14.after), channel_id=1, source_target_pairs={{0,2},{1,3},{2,0},{3,1},{4,6},{5,7},{6,4},{7,5},{8,10},{9,11},{10,... | collective-permute-start | bytes 12296 | tf_op jit(solution)/shard_map/ppermute | solution.py:361
  5.6 31.2 %collective-permute-start.4 = (f32[6,64,256]{2,1,0:T(8,128)}, f32[6,64,256]{2,1,0:T(8,128)}, u32[]{:S(2)}, u32[]{:S(2)}) collective-permute-start(f32[6,64,256]{2,1,0:T(8,128)} %get-tuple-element.19), channel_id=1, source_target_pairs={{0,1},{1,0},{2,3},{3,2},{4,5},{5,4},{6,7},{7,6},{8,9},{9,8},{10,11... | collective-permute-start | bytes 1179656 | tf_op jit(solution)/shard_map/ppermute | solution.py:353
  7.1 29.7 %collective-permute-start.5 = (f32[6,64,256]{2,1,0:T(8,128)}, f32[6,64,256]{2,1,0:T(8,128)}, u32[]{:S(2)}, u32[]{:S(2)}) collective-permute-start(f32[6,64,256]{2,1,0:T(8,128)} %get-tuple-element.20), channel_id=1, source_target_pairs={{1,2},{2,1},{3,4},{4,3},{5,6},{6,5},{7,8},{8,7},{9,10},{10,9},{11,... | collective-permute-start | bytes 1179656 | tf_op jit(solution)/shard_map/ppermute | solution.py:353
  9.1 10.3 %collective-permute-start.1 = (f32[8,128]{1,0:T(8,128)S(1)}, f32[8,128]{1,0:T(8,128)S(1)}, u32[]{:S(2)}, u32[]{:S(2)}) collective-permute-start(f32[8,128]{1,0:T(8,128)S(1)} %add.19), channel_id=1, source_target_pairs={{0,4},{1,5},{2,6},{3,7},{4,0},{5,1},{6,2},{7,3},{8,12},{9,13},{10,... | collective-permute-start | bytes 12296 | tf_op jit(solution)/shard_map/ppermute | solution.py:361
  11.3 1.4 %copy-start.1 = (f32[1,6,4,64,256]{4,3,2,1,0:T(8,128)S(1)}, f32[1,6,4,64,256]{4,3,2,1,0:T(8,128)}, u32[]{:S(2)}) copy-start(f32[1,6,4,64,256]{4,3,2,1,0:T(8,128)} %s_ref.5) | copy-start | bytes 4718596
  12.7 0.7 %copy-start.4 = (f32[8,128]{1,0:T(8,128)S(1)}, f32[8,128]{1,0:T(8,128)}, u32[]{:S(2)}) copy-start(f32[8,128]{1,0:T(8,128)} %get-tuple-element.14.after) | copy-start | bytes 12292
  13.3 9.5 %copy-start.5 = (f32[1,6,4,64,256]{4,3,2,1,0:T(8,128)S(1)}, f32[1,6,4,64,256]{4,3,2,1,0:T(8,128)}, u32[]{:S(2)}) copy-start(f32[1,6,4,64,256]{4,3,2,1,0:T(8,128)} %m_ref.1) | copy-start | bytes 4718596
  15.6 28.1 %collective-permute-start.6 = (f32[448,256]{1,0:T(8,128)}, f32[448,256]{1,0:T(8,128)S(1)}, u32[]{:S(2)}, u32[]{:S(2)}) collective-permute-start(f32[448,256]{1,0:T(8,128)} %get-tuple-element.15.after), channel_id=1, source_target_pairs={{0,1},{1,0},{2,3},{3,2},{4,5},{5,4},{6,7},{7,6},{8,9},{9,8},{10,11... | collective-permute-start | bytes 1376264 | tf_op jit(solution)/shard_map/ppermute | solution.py:353
  17.5 26.1 %collective-permute-start.7 = (f32[448,256]{1,0:T(8,128)S(1)}, f32[448,256]{1,0:T(8,128)S(1)}, u32[]{:S(2)}, u32[]{:S(2)}) collective-permute-start(f32[448,256]{1,0:T(8,128)S(1)} %get-tuple-element.22), channel_id=1, source_target_pairs={{1,2},{2,1},{3,4},{4,3},{5,6},{6,5},{7,8},{8,7},{9,10},{10,9},{11,... | collective-permute-start | bytes 1376264 | tf_op jit(solution)/shard_map/ppermute | solution.py:353
  19.4 12.7 %collective-permute-start.2 = (f32[8,128]{1,0:T(8,128)S(1)}, f32[8,128]{1,0:T(8,128)S(1)}, u32[]{:S(2)}, u32[]{:S(2)}) collective-permute-start(f32[8,128]{1,0:T(8,128)S(1)} %add.20), channel_id=1, source_target_pairs={{0,8},{1,9},{2,10},{3,11},{4,12},{5,13},{6,14},{7,15},{8,0},{9,1},... | collective-permute-start | bytes 12296 | tf_op jit(solution)/shard_map/ppermute | solution.py:361
  26.7 6.7 %copy-start.2 = (f32[6,4,64,256]{3,2,1,0:T(8,128)}, f32[6,4,64,256]{3,2,1,0:T(8,128)S(1)}, u32[]{:S(2)}) copy-start(f32[6,4,64,256]{3,2,1,0:T(8,128)S(1)} %get-tuple-element.16.b_ref) | copy-start | bytes 4718596
  32.1 4.6 %collective-permute-start.3 = (f32[8,128]{1,0:T(8,128)S(1)}, f32[8,128]{1,0:T(8,128)S(1)}, u32[]{:S(2)}, u32[]{:S(2)}) collective-permute-start(f32[8,128]{1,0:T(8,128)S(1)} %add.21), channel_id=1, source_target_pairs={{0,5},{1,4},{2,7},{3,6},{4,1},{5,0},{6,3},{7,2},{8,13},{9,12},{10,... | collective-permute-start | bytes 12296 | tf_op jit(solution)/shard_map/ppermute | solution.py:361
  36.7 1.4 %copy-start.3 = (f32[6,4,64,256]{3,2,1,0:T(8,128)S(1)}, f32[6,4,64,256]{3,2,1,0:T(8,128)}, u32[]{:S(2)}) copy-start(f32[6,4,64,256]{3,2,1,0:T(8,128)} %copy-done.2) | copy-start | bytes 4718596

commit v2 on v1

v2 whole, which is shorter than its diff:
```python
import functools
import math

import jax
import jax.numpy as jnp
from jax import lax
from jax.experimental import pallas as pl
from jax.experimental.pallas import tpu as pltpu
from jax.sharding import PartitionSpec as P

ROWS = 8
COST = {"last_sweep": 1}
LIMIT = {"edge_state": 62}


def call(kernel, name, **kw):
    us, limit = COST.get(name, 0), LIMIT.get(name, 24)
    return pl.pallas_call(
        kernel,
        compiler_params=pltpu.CompilerParams(vmem_limit_bytes=limit * 1024 * 1024),
        cost_estimate=pl.CostEstimate(flops=int(us * 1.1e9), bytes_accessed=0, transcendentals=0),
        name=name,
        **kw,
    )


def f32(*shape):
    return jax.ShapeDtypeStruct(shape, jnp.float32)


VMEM = pl.BlockSpec(memory_space=pltpu.VMEM)
SMEM = pl.BlockSpec(memory_space=pltpu.SMEM)
ANY = pl.BlockSpec(memory_space=pl.ANY)


def edge_of(slot, planes):
    up = lax.rem(lax.axis_index("slab") + slot, 2) == 0
    return jnp.where(up, planes - 1, 0)


def inverse_diag(c):
    return 1.0 / (0.5 + c(0) + 2.4 * (c(1) + c(2) + c(3)))


def shift_sum(p, axis):
    size = p.shape[axis]
    place = lax.broadcasted_iota(jnp.int32, p.shape, axis)
    ahead = jnp.where(place < size - 1, pltpu.roll(p, size - 1, axis), 0.0)
    behind = jnp.where(place > 0, pltpu.roll(p, 1, axis), 0.0)
    return ahead + behind


def edge_kernel(
    s_ref, c_ref, wall_ref, u0, u1, wsum_ref, s_buf, c_buf, wall_buf, c_sems, s_sems, wall_sem
):
    nv, nx = s_ref.shape[1:3]
    edges = [edge_of(slot, nx) for slot in (0, 1)]
    c_copies = [pltpu.make_async_copy(c_ref.at[0, :, e], c_buf.at[j], c_sems.at[j]) for j, e in enumerate(edges)]
    s_copies = [pltpu.make_async_copy(s_ref.at[0, :, e], s_buf.at[j], s_sems.at[j]) for j, e in enumerate(edges)]
    wall_copy = pltpu.make_async_copy(wall_ref.at[0], wall_buf, wall_sem)
    for j in (0, 1):
        c_copies[j].start()
        s_copies[j].start()
    wall_copy.start()
    for j, u in enumerate((u0, u1)):
        c_copies[j].wait()
        inv = inverse_diag(lambda k: c_buf[j, k])
        s_copies[j].wait()
        for v in range(nv):
            u[v] = s_buf[j, v] * inv
    wall_copy.wait()
    wall = jnp.sum(jnp.sum(wall_buf[...], axis=0, keepdims=True), axis=1, keepdims=True)
    rows = lax.broadcasted_iota(jnp.int32, wsum_ref.shape, 0)
    wsum_ref[...] = jnp.where(rows == lax.axis_index("node"), wall, 0.0)


def edge_state(source, coef, wall):
    nv, ny, nz = source.shape[1], source.shape[3], source.shape[4]
    return call(
        edge_kernel,
        "edge_state",
        out_shape=(f32(nv, ny, nz),) * 2 + (f32(ROWS, 128),),
        in_specs=[ANY] * 3,
        out_specs=(VMEM,) * 3,
        scratch_shapes=[
            pltpu.VMEM((2, nv, ny, nz), jnp.float32),
            pltpu.VMEM((2, 4, ny, nz), jnp.float32),
            pltpu.VMEM(wall.shape[1:], jnp.float32),
            pltpu.SemaphoreType.DMA((2,)),
            pltpu.SemaphoreType.DMA((2,)),
            pltpu.SemaphoreType.DMA,
        ],
    )(source, coef, wall)


def share(buf, parts, first, rows, part):
    width = buf.shape[1] // parts
    if parts == 1:
        return buf[pl.ds(first, rows), :]
    node = lax.axis_index("node")
    at = pl.multiple_of((node if part == 0 else 1 - node) * width, width)
    return buf[pl.ds(first, rows), pl.ds(at, width)]


def coupled(c_ref, x, below, here, above):
    q = c_ref[0, 1, x] * (below + above)
    q = q + c_ref[0, 2, x] * shift_sum(here, 0)
    return q + c_ref[0, 3, x] * shift_sum(here, 1)


def mixed(f_ref, w, q):
    mix = f_ref[0, 0, w] * q(0)
    for v in range(1, f_ref.shape[1]):
        mix = mix + f_ref[0, v, w] * q(v)
    return mix


def states_kernel(f_ref, s_ref, c_ref, after, even_ref, odd_ref, q_ref, p_ref):
    del after
    nv, nx, ny, nz = s_ref.shape[1:]
    zero = jnp.zeros((ny, nz), jnp.float32)
    for slot, out in ((0, even_ref), (1, odd_ref)):
        edge = edge_of(slot, nx)
        inner = jnp.where(edge == 0, 1, nx - 2)
        inv = inverse_diag(lambda k: c_ref[0, k, edge])
        inv_inner = inverse_diag(lambda k: c_ref[0, k, inner])
        for v in range(nv):
            p_ref[v] = s_ref[0, v, edge] * inv
            beside = s_ref[0, v, inner] * inv_inner
            q_ref[v] = coupled(c_ref, edge, beside, p_ref[v], zero)
        for w in range(nv):
            out[pl.ds(w * ny, ny), :] = p_ref[w] + inv * mixed(f_ref, w, lambda v: q_ref[v])
        out[pl.ds(nv * ny, ny), :] = c_ref[0, 1, edge] * inv


def edge_states(block, source, coef, after):
    nv, nx, ny, nz = source.shape[1:]
    rows = (nv + 1) * ny
    return call(
        states_kernel,
        "edge_states",
        out_shape=(f32(rows, nz),) * 2,
        in_specs=[SMEM] + [VMEM] * 2 + [ANY],
        out_specs=(VMEM,) * 2,
        scratch_shapes=[pltpu.VMEM((nv, ny, nz), jnp.float32)] * 2,
    )(block, source, coef, after)


def first_kernel(f_ref, s_ref, c_ref, m_ref, after, p1_ref, b_ref, sens_ref, weight_ref, p0, q_ref, inv_ref):
    del after
    nv, nx, ny, nz = s_ref.shape[1:]

    def start(x, _):
        inv = inverse_diag(lambda k: c_ref[0, k, x])
        inv_ref[x] = inv
        own = jnp.zeros((ny, nz), jnp.float32)
        for v in range(nv):
            p = s_ref[0, v, x] * inv
            p0[v, x] = p
            own = own + m_ref[0, v, x] * p
            q_ref[v] = m_ref[0, v, x] * inv
        sens_ref[pl.ds(x, 1), :] = jnp.sum(own, axis=0, keepdims=True)
        for v in range(nv):
            b = f_ref[0, v, 0] * q_ref[0]
            for w in range(1, nv):
                b = b + f_ref[0, v, w] * q_ref[w]
            b_ref[v, x] = b
        return 0

    lax.fori_loop(0, nx, start, 0)

    def first(x, _):
        for v in range(nv):
            q_ref[v] = coupled(c_ref, x, p0[v, x - 1], p0[v, x], p0[v, x + 1])
        for w in range(nv):
            p1_ref[w, x - 1] = p0[w, x] + inv_ref[x] * mixed(f_ref, w, lambda v: q_ref[v])
        return 0

    lax.fori_loop(1, nx - 1, first, 0)

    for slot in (0, 1):
        edge = edge_of(slot, nx)
        total = jnp.zeros((ny, nz), jnp.float32)
        for w in range(nv):
            weight = c_ref[0, 1, edge] * b_ref[w, edge]
            weight_ref[pl.ds((slot * nv + w) * ny, ny), :] = weight
            if slot == 1:
                total = total + weight * mixed(f_ref, w, lambda v: p0[v, edge])
    weight_ref[pl.ds(2 * nv * ny, ny), :] = total


def first_sweep(block, source, coef, metric, after):
    nv, nx, ny, nz = source.shape[1:]
    assert 2 < nx <= ROWS
    rows = (2 * nv + 1) * ny
    return call(
        first_kernel,
        "first_sweep",
        out_shape=(f32(nv, nx - 2, ny, nz), f32(nv, nx, ny, nz), f32(nx, nz), f32(rows, nz)),
        in_specs=[SMEM] + [VMEM] * 3 + [ANY],
        out_specs=(VMEM,) * 4,
        scratch_shapes=[
            pltpu.VMEM((nv, nx, ny, nz), jnp.float32),
            pltpu.VMEM((nv, ny, nz), jnp.float32),
            pltpu.VMEM((nx, ny, nz), jnp.float32),
        ],
    )(block, source, coef, metric, after)


def second_kernel(f_ref, far0, far1, state0, state1, after, whole0, whole1):
    del after
    nv, ny, nz = far0.shape
    for far, state, whole in ((far0, state0, whole0), (far1, state1, whole1)):
        rho = state[pl.ds(nv * ny, ny), :]
        for w in range(nv):
            mix = mixed(f_ref, w, lambda v: far[v])
            whole[pl.ds(w * ny, ny), :] = state[pl.ds(w * ny, ny), :] + rho * mix


def second_states(block, far, states, after):
    nv, ny, nz = far[0].shape
    return call(
        second_kernel,
        "second_states",
        out_shape=(f32(nv * ny, nz),) * 2,
        in_specs=[SMEM] + [VMEM] * 4 + [ANY],
        out_specs=(VMEM,) * 2,
    )(block, *far, *states, after)


def last_kernel(c_ref, inner_ref, whole0, whole1, b_ref, base_ref, out_ref, p1):
    nv, nx, ny, nz = b_ref.shape
    zero = jnp.zeros((ny, nz), jnp.float32)
    for slot, whole in ((0, whole0), (1, whole1)):
        for v in range(nv):
            p1[v, edge_of(slot, nx)] = whole[pl.ds(v * ny, ny), :]

    def state(v, x):
        return inner_ref[v, x - 1] if 0 < x < nx - 1 else p1[v, x]

    for x in range(nx):
        along = [zero, zero, zero]
        for v in range(nv):
            b = b_ref[v, x]
            p = state(v, x)
            beside = [state(v, at) for at in (x - 1, x + 1) if 0 <= at < nx]
            along[0] = along[0] + b * sum(beside[1:], beside[0])
            along[1] = along[1] + b * shift_sum(p, 0)
            along[2] = along[2] + b * shift_sum(p, 1)
        own = c_ref[0, 1, x] * along[0] + c_ref[0, 2, x] * along[1] + c_ref[0, 3, x] * along[2]
        out_ref[x : x + 1, :] = base_ref[x : x + 1, :] + jnp.sum(own, axis=0, keepdims=True)


def last_sweep(coef, inner, edges, b, base):
    return call(
        last_kernel,
        "last_sweep",
        out_shape=f32(*base.shape),
        in_specs=[VMEM] * 6,
        out_specs=VMEM,
        scratch_shapes=[pltpu.VMEM(b.shape, jnp.float32)],
    )(coef, inner, *edges, b, base)


def factors(nodes, cells, sums):
    raw = [math.sin(math.pi * (n + 0.5) / nodes) for n in range(nodes)]
    weight = [r / sum(raw) for r in raw]
    objective = [sums[n : n + 1, :] * (1.0 / cells) for n in range(nodes)]
    mean = sum(w * o for w, o in zip(weight, objective))
    variance = sum(w * (o - mean) ** 2 for w, o in zip(weight, objective))
    spread = jnp.sqrt(variance + 0.25)
    return [w * (1.0 + 2.0 * (o - mean) / spread) for w, o in zip(weight, objective)]


def node_kernel(parts, sens_ref, sums_ref, weight_ref, even_ref, odd_ref, *refs):
    outs, acc = refs[:-1], refs[-1]
    nx, nz = sens_ref.shape
    acc[...] = jnp.zeros_like(acc)
    acc[pl.ds(0, nx), :] = sens_ref[...]
    for k in range(nz // 128):
        acc[pl.ds(ROWS, ROWS), pl.ds(k * 128, 128)] = sums_ref[...]
    first = 0
    for slot, msg in ((0, even_ref), (1, odd_ref)):
        rows = msg.shape[0]
        total = weight_ref[pl.ds(first, rows), :] * msg[...]
        acc[pl.ds(edge_of(slot, nx), 1), :] += jnp.sum(total, axis=0, keepdims=True)
        first += rows
    for part, out in enumerate(outs):
        out[...] = share(acc, parts, 0, 2 * ROWS, part)


def node_terms(parts, sens, sums, weight, even, odd):
    nx, nz = sens.shape
    return call(
        functools.partial(node_kernel, parts),
        "node_terms",
        out_shape=(f32(2 * ROWS, nz // parts),) * parts,
        in_specs=[VMEM] * 5,
        out_specs=(VMEM,) * parts,
        scratch_shapes=[pltpu.VMEM((2 * ROWS, nz), jnp.float32)],
    )(sens, sums, weight, even, odd)


def gradient_kernel(nodes, cells, *refs):
    terms, out_ref = refs[:-1], refs[-1]
    nx = out_ref.shape[0]
    factor = factors(nodes, cells, sum(term[pl.ds(ROWS, ROWS), pl.ds(0, 128)] for term in terms))
    node = lax.axis_index("node")
    total = jnp.zeros(out_ref.shape, jnp.float32)
    for part, term in enumerate(terms):
        whose = node if part == 0 else 1 - node
        scale = factor[0]
        for n in range(1, nodes):
            scale = jnp.where(whose == n, factor[n], scale)
        total = total + term[pl.ds(0, nx), :] * scale[:, :1]
    out_ref[...] = total


def gradient(nodes, cells, nx, terms):
    return call(
        functools.partial(gradient_kernel, nodes, cells),
        "gradient",
        out_shape=f32(nx, terms[0].shape[1]),
        in_specs=[VMEM] * len(terms),
        out_specs=VMEM,
    )(*terms)


def swap_pairs(value, slot, part=0):
    count, nodes = lax.axis_size("slab"), lax.axis_size("node")
    pairs = []
    for low in range(slot, count - 1, 2):
        pairs += [(low, low + 1), (low + 1, low)]
    if part == 0:
        return lax.ppermute(value, "slab", pairs)
    cross = [(n * count + a, (1 - n) * count + b) for n in range(nodes) for a, b in pairs]
    return lax.ppermute(value, ("node", "slab"), cross)


def from_partner(value, slab, node=0):
    count, nodes = lax.axis_size("slab"), lax.axis_size("node")
    pairs = [(n * count + i, (n ^ node) * count + (i ^ slab)) for n in range(nodes) for i in range(count)]
    return lax.ppermute(value, ("node", "slab"), pairs)


def sum_steps(count):
    assert count & (count - 1) == 0
    steps = [1 << k for k in range(1, count.bit_length() - 1)]
    return steps + [1 ^ (4 if count > 4 else 0)]


def other_core(value):
    return lax.ppermute(value, "node", [(0, 1), (1, 0)])


def after(value, *others):
    return lax.optimization_barrier((value, *others))[0]


def per_device(source, coef, block, metric, wall):
    nodes, slabs = lax.axis_size("node"), lax.axis_size("slab")
    nx = source.shape[2]
    cells = wall.shape[1] * slabs * wall.shape[2]
    parts = 2 if nodes == 2 else 1
    *own, sums = edge_state(source, coef, wall)
    far = [swap_pairs(value, slot) for slot, value in enumerate(own)]
    inner, b, base, weight = first_sweep(block, source, coef, metric, sums)
    first, *steps = sum_steps(slabs)
    sums = after(sums + from_partner(sums, first), base)
    early, late = steps[: len(steps) // 2], steps[len(steps) // 2 :]
    for slab in early:
        sums = sums + from_partner(sums, slab)
    states = edge_states(block, source, coef, sums)
    odd = swap_pairs(states[1], 1)
    edges = second_states(block, far, states, sums)
    even = swap_pairs(edges[0], 0)
    sums = after(sums, edges[0])
    for slab in late:
        sums = sums + from_partner(sums, slab)
    if parts == 1:
        sums = lax.psum(sums, "node")
    sens = last_sweep(coef, inner, edges, b, base)
    terms = list(node_terms(parts, sens, sums, weight, even, odd))
    if parts == 2:
        terms[1] = other_core(terms[1])
        return gradient(nodes, cells, nx, terms)
    total = lax.psum(gradient(nodes, cells, nx, terms), "node")
    width = total.shape[1] // nodes
    return lax.dynamic_slice_in_dim(total, lax.axis_index("node") * width, width, 1)


def solution(mesh):
    return jax.shard_map(
        per_device,
        mesh=mesh,
        in_specs=(
            P("node", None, "slab", None, None),
            P("node", None, "slab", None, None),
            P("node", None, None),
            P("node", None, "slab", None, None),
            P("node", "slab", None),
        ),
        out_specs=P("slab", "node"),
        check_vma=False,
    )
```

time: 47.2 us -> 45 us (0.953)
  waiting for transfers between devices: 9.95 us -> 15.9 us
  blocking collectives: 5.88 us -> 0 us
  Pallas kernels: 12.1 us -> 9.85 us
  starting transfers between devices: 14.1 us -> 15.4 us
  other arithmetic: 0.69 us -> 0.01 us
  local copies, waits for them, and re-layouts: 4.08 us -> 3.5 us
    psum x2 -> x0, blocking collectives: 5.88 us -> none  [the longest x1 3.41 us: per_device(): lax.psum(halo_terms(nodes, block, coef, b, sens, sums, u0, u1), 'node')]
    ppermute x4, waiting for transfers between devices: 0.09 us -> 2.68 us  [swap_pairs(): return lax.ppermute(value, 'slab', pairs)]
    ppermute x4, waiting for transfers between devices: 9.86 us -> 12.1 us  [from_partner(): return lax.ppermute(value, ('node', 'slab'), pairs)]
    ppermute x4, starting transfers between devices: 5.53 us -> 7.76 us  [swap_pairs(): return lax.ppermute(value, 'slab', pairs)]
    pallas_call x4 -> x5, Pallas kernels: 8.26 us -> 6.13 us  [the longest x1 2.79 us: first_sweep(): call(first_kernel, 'first_sweep', out_shape=(f32(nv, nx - 2, ny, nz), f32...]
    ppermute x0 -> x1, waiting for transfers between devices: none -> 1.15 us  [other_core(): return lax.ppermute(value, 'node', [(0, 1), (1, 0)])]
    ppermute x4, starting transfers between devices: 8.57 us -> 7.52 us  [from_partner(): return lax.ppermute(value, ('node', 'slab'), pairs)]
    add x4 -> x3, other arithmetic: 0.69 us -> 0.01 us  [per_device(): sums = sums + from_partner(sums, slab)]
  transfers between devices with their start and end apart: 8 -> 9, of which waited for: 4 -> 6; matrix products, arithmetic and copies ran while one was open for 1% -> 0% of each run, Pallas kernels for 20% -> 15%
where the time goes in v2:
time: 45 us; the launch traced here: 44.7 us
  waiting for transfers between devices  15.9 us (35%)
  starting transfers between devices  15.4 us (34%)
  Pallas kernels  9.85 us (22%)
  local copies, waits for them, and re-layouts  3.5 us (8%)
    ppermute x4, waiting for transfers between devices, from_partner(): return lax.ppermute(value, ('node', 'slab'), pairs)  12.1 us
    ppermute x4, starting transfers between devices, swap_pairs(): return lax.ppermute(value, 'slab', pairs)  7.76 us
    ppermute x4, starting transfers between devices, from_partner(): return lax.ppermute(value, ('node', 'slab'), pairs)  7.52 us
    unnamed x11, local copies, waits for them, and re-layouts  3.5 us
    pallas_call x1, Pallas kernels, first_sweep(): call(first_kernel, 'first_sweep', out_shape=(f32(nv, nx - 2, ny, nz), f32...  2.79 us
    ppermute x4, waiting for transfers between devices, swap_pairs(): return lax.ppermute(value, 'slab', pairs)  2.68 us
    pallas_call x1, Pallas kernels, edge_state(): call(edge_kernel, 'edge_state', out_shape=(f32(nv, ny, nz),) * 2 + (f32(R...  2.36 us
    pallas_call x1, Pallas kernels, edge_states(): call(states_kernel, 'edge_states', out_shape=(f32(rows, nz),) * 2, in_spe...  1.55 us
  transfers between devices with their start and end apart: 9, of which 6 were waited for; matrix products, arithmetic and copies ran while one was open for 0% of the time, Pallas kernels for 15%

profile of v2, /device:TPU:0, one launch (start us, length us, event | category | flops | bytes accessed | tf_op | source)
XLA Modules:
  0.0 44.7 jit_solution(15019050703182768773)
XLA Ops:
  0.0 0.0 copy-start
  0.0 0.0 copy-start.4
  0.0 2.4 %edge_state.1 = (f32[6,64,256]{2,1,0:T(8,128)}, f32[6,64,256]{2,1,0:T(8,128)}, f32[8,128]{1,0:T(8,128)}) custom-call(f32[1,6,4,64,256]{4,3,2,1,0:T(8,128)} %s_ref.5, f32[1,4,4,64,256]{4,3,2,1,0:T(8,128)} %c_ref.7, f32[1,4,256]{2,1,0:T(4,128)} %wall_ref.1), custom_call_target="tpu_custom_call" | custom-call | tf_op jit(solution)/shard_map/edge_state/pallas_call | solution.py:79
  2.4 3.0 %collective-permute-start = (f32[6,64,256]{2,1,0:T(8,128)}, f32[6,64,256]{2,1,0:T(8,128)S(1)}, u32[]{:S(2)}, u32[]{:S(2)}) collective-permute-start(f32[6,64,256]{2,1,0:T(8,128)} %get-tuple-element.22), channel_id=1, source_target_pairs={{0,1},{1,0},{2,3},{3,2},{4,5},{5,4},{6,7},{7,6},{8,9},{9,8},{10,11... | collective-permute-start | bytes 1179656 | tf_op jit(solution)/shard_map/ppermute | solution.py:335
  5.4 0.7 %collective-permute-start.1 = (f32[6,64,256]{2,1,0:T(8,128)}, f32[6,64,256]{2,1,0:T(8,128)S(1)}, u32[]{:S(2)}, u32[]{:S(2)}) collective-permute-start(f32[6,64,256]{2,1,0:T(8,128)} %get-tuple-element.23), channel_id=1, source_target_pairs={{1,2},{2,1},{3,4},{4,3},{5,6},{6,5},{7,8},{8,7},{9,10},{10,9},{11,... | collective-permute-start | bytes 1179656 | tf_op jit(solution)/shard_map/ppermute | solution.py:335
  6.1 2.8 %collective-permute-start.2 = (f32[8,128]{1,0:T(8,128)}, f32[8,128]{1,0:T(8,128)S(1)}, u32[]{:S(2)}, u32[]{:S(2)}) collective-permute-start(f32[8,128]{1,0:T(8,128)} %get-tuple-element.20.after), channel_id=1, source_target_pairs={{0,2},{1,3},{2,0},{3,1},{4,6},{5,7},{6,4},{7,5},{8,10},{9,11},{10,... | collective-permute-start | bytes 12296 | tf_op jit(solution)/shard_map/ppermute | solution.py:343
  8.9 0.0 copy-done.4
  8.9 0.0 copy-done
  8.9 1.4 %copy-done.1 = f32[1,6,4,64,256]{4,3,2,1,0:T(8,128)S(1)} copy-done((f32[1,6,4,64,256]{4,3,2,1,0:T(8,128)S(1)}, f32[1,6,4,64,256]{4,3,2,1,0:T(8,128)}, u32[]{:S(2)}) %copy-start.1) | copy-done | bytes 1572888
  10.3 1.4 %copy-done.2 = f32[1,6,4,64,256]{4,3,2,1,0:T(8,128)S(1)} copy-done((f32[1,6,4,64,256]{4,3,2,1,0:T(8,128)S(1)}, f32[1,6,4,64,256]{4,3,2,1,0:T(8,128)}, u32[]{:S(2)}) %copy-start.2) | copy-done | bytes 1572888
  11.7 0.7 %copy-done.3 = f32[8,128]{1,0:T(8,128)S(1)} copy-done((f32[8,128]{1,0:T(8,128)S(1)}, f32[8,128]{1,0:T(8,128)}, u32[]{:S(2)}) %copy-start.3) | copy-done | bytes 4120
  12.4 2.8 %first_sweep.1 = (f32[6,2,64,256]{3,2,1,0:T(8,128)S(1)}, f32[6,4,64,256]{3,2,1,0:T(8,128)S(1)}, f32[4,256]{1,0:T(4,128)S(1)}, f32[832,256]{1,0:T(8,128)S(1)}) custom-call(f32[1,6,6]{2,1,0:T(8,128)S(1)} %copy.6.f_ref, f32[1,6,4,64,256]{4,3,2,1,0:T(8,128)S(1)} %copy-done.1, f32[1,4,4,64,256]{4,3,2,1,0:T(8,128)S(1)} %copy-done, ...), custom_call_target="tpu_custom_call" | custom-call | tf_op jit(solution)/shard_map/first_sweep/pallas_call | solution.py:196
  15.2 0.0 collective-permute-done.2
  15.2 2.1 %collective-permute-start.3 = (f32[8,128]{1,0:T(8,128)S(1)}, f32[8,128]{1,0:T(8,128)S(1)}, u32[]{:S(2)}, u32[]{:S(2)}) collective-permute-start(f32[8,128]{1,0:T(8,128)S(1)} %add.12), channel_id=1, source_target_pairs={{0,4},{1,5},{2,6},{3,7},{4,0},{5,1},{6,2},{7,3},{8,12},{9,13},{10,... | collective-permute-start | bytes 12296 | tf_op jit(solution)/shard_map/ppermute | solution.py:343
  17.3 1.8 %collective-permute-done.3 = f32[8,128]{1,0:T(8,128)S(1)} collective-permute-done((f32[8,128]{1,0:T(8,128)S(1)}, f32[8,128]{1,0:T(8,128)S(1)}, u32[]{:S(2)}, u32[]{:S(2)}) %collective-permute-start.3) | collective-permute-done | bytes 4128 | tf_op jit(solution)/shard_map/ppermute | solution.py:343
  19.1 1.5 %edge_states.1 = (f32[448,256]{1,0:T(8,128)S(1)}, f32[448,256]{1,0:T(8,128)S(1)}) custom-call(f32[1,6,6]{2,1,0:T(8,128)S(1)} %copy.6.f_ref, f32[1,6,4,64,256]{4,3,2,1,0:T(8,128)S(1)} %copy-done.1, f32[1,4,4,64,256]{4,3,2,1,0:T(8,128)S(1)} %copy-done, f32[8,128]{1,0:T(8,128)S(1)} %add.13.after), custom_call_target="tpu_custom_call" | custom-call | tf_op jit(solution)/shard_map/edge_states/pallas_call | solution.py:139
  20.7 0.7 %collective-permute-start.7 = (f32[448,256]{1,0:T(8,128)S(1)}, f32[448,256]{1,0:T(8,128)S(1)}, u32[]{:S(2)}, u32[]{:S(2)}) collective-permute-start(f32[448,256]{1,0:T(8,128)S(1)} %get-tuple-element.27.state1), channel_id=1, source_target_pairs={{1,2},{2,1},{3,4},{4,3},{5,6},{6,5},{7,8},{8,7},{9,10},{10,9},{11,... | collective-permute-start | bytes 1376264 | tf_op jit(solution)/shard_map/ppermute | solution.py:335
  21.4 1.1 %collective-permute-done.far0 = f32[6,64,256]{2,1,0:T(8,128)S(1)} collective-permute-done((f32[6,64,256]{2,1,0:T(8,128)}, f32[6,64,256]{2,1,0:T(8,128)S(1)}, u32[]{:S(2)}, u32[]{:S(2)}) %collective-permute-start) | collective-permute-done | bytes 393248 | tf_op jit(solution)/shard_map/ppermute | solution.py:335
  22.5 0.0 collective-permute-done.1.far1
  22.5 1.0 %second_states.1 = (f32[384,256]{1,0:T(8,128)S(1)}, f32[384,256]{1,0:T(8,128)S(1)}) custom-call(f32[1,6,6]{2,1,0:T(8,128)S(1)} %copy.6.f_ref, f32[6,64,256]{2,1,0:T(8,128)S(1)} %collective-permute-done.far0, f32[6,64,256]{2,1,0:T(8,128)S(1)} %collective-permute-done.1.far1, f32[448,256]{1,0:T(8,128)S(1)} %get-tuple-element.26.state0, ...), custom_call_target="tpu_custom_call" | custom-call | tf_op jit(solution)/shard_map/second_states/pallas_call | solution.py:222
  23.5 3.4 %collective-permute-start.6 = (f32[384,256]{1,0:T(8,128)S(1)}, f32[384,256]{1,0:T(8,128)S(1)}, u32[]{:S(2)}, u32[]{:S(2)}) collective-permute-start(f32[384,256]{1,0:T(8,128)S(1)} %get-tuple-element.28.whole0), channel_id=1, source_target_pairs={{0,1},{1,0},{2,3},{3,2},{4,5},{5,4},{6,7},{7,6},{8,9},{9,8},{10,11... | collective-permute-start | bytes 1179656 | tf_op jit(solution)/shard_map/ppermute | solution.py:335
  26.9 2.6 %collective-permute-start.4 = (f32[8,128]{1,0:T(8,128)S(1)}, f32[8,128]{1,0:T(8,128)S(1)}, u32[]{:S(2)}, u32[]{:S(2)}) collective-permute-start(f32[8,128]{1,0:T(8,128)S(1)} %add.13.after), channel_id=1, source_target_pairs={{0,8},{1,9},{2,10},{3,11},{4,12},{5,13},{6,14},{7,15},{8,0},{9,1},... | collective-permute-start | bytes 12296 | tf_op jit(solution)/shard_map/ppermute | solution.py:343
  29.5 7.0 %collective-permute-done.4 = f32[8,128]{1,0:T(8,128)S(1)} collective-permute-done((f32[8,128]{1,0:T(8,128)S(1)}, f32[8,128]{1,0:T(8,128)S(1)}, u32[]{:S(2)}, u32[]{:S(2)}) %collective-permute-start.4) | collective-permute-done | bytes 4128 | tf_op jit(solution)/shard_map/ppermute | solution.py:343
  36.5 0.0 collective-permute-start.5
  36.5 1.4 %last_sweep.1.sens_ref = f32[4,256]{1,0:T(4,128)S(1)} custom-call(f32[1,4,4,64,256]{4,3,2,1,0:T(8,128)S(1)} %copy-done, f32[6,2,64,256]{3,2,1,0:T(8,128)S(1)} %get-tuple-element.21.inner_ref, f32[384,256]{1,0:T(8,128)S(1)} %get-tuple-element.28.whole0, f32[384,256]{1,0:T(8,128)S(1)} %get-tuple-element.29.whole1, ...), custom_call_target="tpu_custom_call" | custom-call | flops 1100000000 | tf_op jit(solution)/shard_map/last_sweep/pallas_call | solution.py:255
  37.9 3.2 %collective-permute-done.5 = f32[8,128]{1,0:T(8,128)S(1)} collective-permute-done((f32[8,128]{1,0:T(8,128)S(1)}, f32[8,128]{1,0:T(8,128)S(1)}, u32[]{:S(2)}, u32[]{:S(2)}) %collective-permute-start.5) | collective-permute-done | bytes 4128 | tf_op jit(solution)/shard_map/ppermute | solution.py:343
  41.1 0.0 collective-permute-done.7.odd_ref
  41.1 1.6 %collective-permute-done.6.even_ref = f32[384,256]{1,0:T(8,128)S(1)} collective-permute-done((f32[384,256]{1,0:T(8,128)S(1)}, f32[384,256]{1,0:T(8,128)S(1)}, u32[]{:S(2)}, u32[]{:S(2)}) %collective-permute-start.6) | collective-permute-done | bytes 393248 | tf_op jit(solution)/shard_map/ppermute | solution.py:335
  42.7 0.1 node_terms.1
  42.9 0.1 collective-permute-start.8
  42.9 1.2 %collective-permute-done.8.refs_1_ = f32[16,128]{1,0:T(8,128)S(1)} collective-permute-done((f32[16,128]{1,0:T(8,128)S(1)}, f32[16,128]{1,0:T(8,128)S(1)}, u32[]{:S(2)}, u32[]{:S(2)}) %collective-permute-start.8) | collective-permute-done | bytes 8224 | tf_op jit(solution)/shard_map/ppermute | solution.py:353
  44.1 0.6 %gradient.1 = f32[4,128]{1,0:T(4,128)} custom-call(f32[16,128]{1,0:T(8,128)S(1)} %get-tuple-element.33.refs_0_, f32[16,128]{1,0:T(8,128)S(1)} %collective-permute-done.8.refs_1_), custom_call_target="tpu_custom_call" | custom-call | tf_op jit(solution)/shard_map/gradient/pallas_call | solution.py:320
  (8 shorter events, 0.0 us)
Async XLA Ops:
  0.0 8.9 %copy-start = (f32[1,4,4,64,256]{4,3,2,1,0:T(8,128)S(1)}, f32[1,4,4,64,256]{4,3,2,1,0:T(8,128)}, u32[]{:S(2)}) copy-start(f32[1,4,4,64,256]{4,3,2,1,0:T(8,128)} %c_ref.7) | copy-start | bytes 3145732
  0.0 8.9 %copy-start.4 = (f32[1,6,6]{2,0,1:T(1,128)S(1)}, f32[1,6,6]{2,0,1:T(1,128)}, u32[]{:S(2)}) copy-start(f32[1,6,6]{2,0,1:T(1,128)} %param.7) | copy-start | bytes 436
  2.4 20.1 %collective-permute-start = (f32[6,64,256]{2,1,0:T(8,128)}, f32[6,64,256]{2,1,0:T(8,128)S(1)}, u32[]{:S(2)}, u32[]{:S(2)}) collective-permute-start(f32[6,64,256]{2,1,0:T(8,128)} %get-tuple-element.22), channel_id=1, source_target_pairs={{0,1},{1,0},{2,3},{3,2},{4,5},{5,4},{6,7},{7,6},{8,9},{9,8},{10,11... | collective-permute-start | bytes 1179656 | tf_op jit(solution)/shard_map/ppermute | solution.py:335
  5.4 17.1 %collective-permute-start.1 = (f32[6,64,256]{2,1,0:T(8,128)}, f32[6,64,256]{2,1,0:T(8,128)S(1)}, u32[]{:S(2)}, u32[]{:S(2)}) collective-permute-start(f32[6,64,256]{2,1,0:T(8,128)} %get-tuple-element.23), channel_id=1, source_target_pairs={{1,2},{2,1},{3,4},{4,3},{5,6},{6,5},{7,8},{8,7},{9,10},{10,9},{11,... | collective-permute-start | bytes 1179656 | tf_op jit(solution)/shard_map/ppermute | solution.py:335
  6.1 9.1 %collective-permute-start.2 = (f32[8,128]{1,0:T(8,128)}, f32[8,128]{1,0:T(8,128)S(1)}, u32[]{:S(2)}, u32[]{:S(2)}) collective-permute-start(f32[8,128]{1,0:T(8,128)} %get-tuple-element.20.after), channel_id=1, source_target_pairs={{0,2},{1,3},{2,0},{3,1},{4,6},{5,7},{6,4},{7,5},{8,10},{9,11},{10,... | collective-permute-start | bytes 12296 | tf_op jit(solution)/shard_map/ppermute | solution.py:343
  8.9 1.4 %copy-start.1 = (f32[1,6,4,64,256]{4,3,2,1,0:T(8,128)S(1)}, f32[1,6,4,64,256]{4,3,2,1,0:T(8,128)}, u32[]{:S(2)}) copy-start(f32[1,6,4,64,256]{4,3,2,1,0:T(8,128)} %s_ref.5) | copy-start | bytes 4718596
  10.3 1.4 %copy-start.2 = (f32[1,6,4,64,256]{4,3,2,1,0:T(8,128)S(1)}, f32[1,6,4,64,256]{4,3,2,1,0:T(8,128)}, u32[]{:S(2)}) copy-start(f32[1,6,4,64,256]{4,3,2,1,0:T(8,128)} %m_ref.1) | copy-start | bytes 4718596
  11.7 0.7 %copy-start.3 = (f32[8,128]{1,0:T(8,128)S(1)}, f32[8,128]{1,0:T(8,128)}, u32[]{:S(2)}) copy-start(f32[8,128]{1,0:T(8,128)} %get-tuple-element.20.after) | copy-start | bytes 12292
  15.2 3.9 %collective-permute-start.3 = (f32[8,128]{1,0:T(8,128)S(1)}, f32[8,128]{1,0:T(8,128)S(1)}, u32[]{:S(2)}, u32[]{:S(2)}) collective-permute-start(f32[8,128]{1,0:T(8,128)S(1)} %add.12), channel_id=1, source_target_pairs={{0,4},{1,5},{2,6},{3,7},{4,0},{5,1},{6,2},{7,3},{8,12},{9,13},{10,... | collective-permute-start | bytes 12296 | tf_op jit(solution)/shard_map/ppermute | solution.py:343
  20.7 20.5 %collective-permute-start.7 = (f32[448,256]{1,0:T(8,128)S(1)}, f32[448,256]{1,0:T(8,128)S(1)}, u32[]{:S(2)}, u32[]{:S(2)}) collective-permute-start(f32[448,256]{1,0:T(8,128)S(1)} %get-tuple-element.27.state1), channel_id=1, source_target_pairs={{1,2},{2,1},{3,4},{4,3},{5,6},{6,5},{7,8},{8,7},{9,10},{10,9},{11,... | collective-permute-start | bytes 1376264 | tf_op jit(solution)/shard_map/ppermute | solution.py:335
  23.5 19.2 %collective-permute-start.6 = (f32[384,256]{1,0:T(8,128)S(1)}, f32[384,256]{1,0:T(8,128)S(1)}, u32[]{:S(2)}, u32[]{:S(2)}) collective-permute-start(f32[384,256]{1,0:T(8,128)S(1)} %get-tuple-element.28.whole0), channel_id=1, source_target_pairs={{0,1},{1,0},{2,3},{3,2},{4,5},{5,4},{6,7},{7,6},{8,9},{9,8},{10,11... | collective-permute-start | bytes 1179656 | tf_op jit(solution)/shard_map/ppermute | solution.py:335
  26.9 9.6 %collective-permute-start.4 = (f32[8,128]{1,0:T(8,128)S(1)}, f32[8,128]{1,0:T(8,128)S(1)}, u32[]{:S(2)}, u32[]{:S(2)}) collective-permute-start(f32[8,128]{1,0:T(8,128)S(1)} %add.13.after), channel_id=1, source_target_pairs={{0,8},{1,9},{2,10},{3,11},{4,12},{5,13},{6,14},{7,15},{8,0},{9,1},... | collective-permute-start | bytes 12296 | tf_op jit(solution)/shard_map/ppermute | solution.py:343
  36.5 4.6 %collective-permute-start.5 = (f32[8,128]{1,0:T(8,128)S(1)}, f32[8,128]{1,0:T(8,128)S(1)}, u32[]{:S(2)}, u32[]{:S(2)}) collective-permute-start(f32[8,128]{1,0:T(8,128)S(1)} %add.14), channel_id=1, source_target_pairs={{0,5},{1,4},{2,7},{3,6},{4,1},{5,0},{6,3},{7,2},{8,13},{9,12},{10,... | collective-permute-start | bytes 12296 | tf_op jit(solution)/shard_map/ppermute | solution.py:343
  42.9 1.2 %collective-permute-start.8 = (f32[16,128]{1,0:T(8,128)S(1)}, f32[16,128]{1,0:T(8,128)S(1)}, u32[]{:S(2)}, u32[]{:S(2)}) collective-permute-start(f32[16,128]{1,0:T(8,128)S(1)} %get-tuple-element.34), channel_id=1, source_target_pairs={{0,16},{16,0},{1,17},{17,1},{2,18},{18,2},{3,19},{19,3},{4,20},{20... | collective-permute-start | bytes 24584 | tf_op jit(solution)/shard_map/ppermute | solution.py:353

commit v3 on v2

--- a/solution.py
+++ b/solution.py
@@ -132,7 +132,6 @@
             out[pl.ds(w * ny, ny), :] = p_ref[w] + inv * mixed(f_ref, w, lambda v: q_ref[v])
         out[pl.ds(nv * ny, ny), :] = c_ref[0, 1, edge] * inv
 
-
 def edge_states(block, source, coef, after):
     nv, nx, ny, nz = source.shape[1:]
     rows = (nv + 1) * ny
@@ -207,25 +206,28 @@
     )(block, source, coef, metric, after)
 
 
-def second_kernel(f_ref, far0, far1, state0, state1, after, whole0, whole1):
-    del after
+def second_kernel(f_ref, far0, far1, state0, state1, sums_ref, whole0, whole1):
     nv, ny, nz = far0.shape
+    rows = nv * ny
     for far, state, whole in ((far0, state0, whole0), (far1, state1, whole1)):
-        rho = state[pl.ds(nv * ny, ny), :]
+        rho = state[pl.ds(rows, ny), :]
         for w in range(nv):
             mix = mixed(f_ref, w, lambda v: far[v])
             whole[pl.ds(w * ny, ny), :] = state[pl.ds(w * ny, ny), :] + rho * mix
-
-
-def second_states(block, far, states, after):
+    for k in range(nz // 128):
+        whole0[pl.ds(rows, ROWS), pl.ds(k * 128, 128)] = sums_ref[...]
+
+
+def second_states(block, far, states, sums):
     nv, ny, nz = far[0].shape
+    rows = nv * ny
     return call(
         second_kernel,
         "second_states",
-        out_shape=(f32(nv * ny, nz),) * 2,
-        in_specs=[SMEM] + [VMEM] * 4 + [ANY],
+        out_shape=(f32(rows + ROWS, nz), f32(rows, nz)),
+        in_specs=[SMEM] + [VMEM] * 5,
         out_specs=(VMEM,) * 2,
-    )(block, *far, *states, after)
+    )(block, *far, *states, sums)
 
 
 def last_kernel(c_ref, inner_ref, whole0, whole1, b_ref, base_ref, out_ref, p1):
@@ -272,33 +274,35 @@
     return [w * (1.0 + 2.0 * (o - mean) / spread) for w, o in zip(weight, objective)]
 
 
-def node_kernel(parts, sens_ref, sums_ref, weight_ref, even_ref, odd_ref, *refs):
-    outs, acc = refs[:-1], refs[-1]
+def node_kernel(parts, few, sens_ref, weight_ref, even_ref, odd_ref, *refs):
+    sums, outs, acc = refs[:few], refs[few:-1], refs[-1]
     nx, nz = sens_ref.shape
+    rows = even_ref.shape[0] - ROWS
     acc[...] = jnp.zeros_like(acc)
     acc[pl.ds(0, nx), :] = sens_ref[...]
+    total = even_ref[pl.ds(rows, ROWS), pl.ds(0, 128)]
+    for other in sums:
+        total = total + other[...]
     for k in range(nz // 128):
-        acc[pl.ds(ROWS, ROWS), pl.ds(k * 128, 128)] = sums_ref[...]
-    first = 0
-    for slot, msg in ((0, even_ref), (1, odd_ref)):
-        rows = msg.shape[0]
-        total = weight_ref[pl.ds(first, rows), :] * msg[...]
-        acc[pl.ds(edge_of(slot, nx), 1), :] += jnp.sum(total, axis=0, keepdims=True)
-        first += rows
+        acc[pl.ds(ROWS, ROWS), pl.ds(k * 128, 128)] = total
+    total = weight_ref[pl.ds(0, rows), :] * even_ref[pl.ds(0, rows), :]
+    acc[pl.ds(edge_of(0, nx), 1), :] += jnp.sum(total, axis=0, keepdims=True)
+    total = weight_ref[pl.ds(rows, odd_ref.shape[0]), :] * odd_ref[...]
+    acc[pl.ds(edge_of(1, nx), 1), :] += jnp.sum(total, axis=0, keepdims=True)
     for part, out in enumerate(outs):
         out[...] = share(acc, parts, 0, 2 * ROWS, part)
 
 
-def node_terms(parts, sens, sums, weight, even, odd):
+def node_terms(parts, sens, weight, even, odd, sums):
     nx, nz = sens.shape
     return call(
-        functools.partial(node_kernel, parts),
+        functools.partial(node_kernel, parts, len(sums)),
         "node_terms",
         out_shape=(f32(2 * ROWS, nz // parts),) * parts,
-        in_specs=[VMEM] * 5,
+        in_specs=[VMEM] * (4 + len(sums)),
         out_specs=(VMEM,) * parts,
         scratch_shapes=[pltpu.VMEM((2 * ROWS, nz), jnp.float32)],
-    )(sens, sums, weight, even, odd)
+    )(sens, weight, even, odd, *sums)
 
 
 def gradient_kernel(nodes, cells, *refs):
@@ -343,12 +347,6 @@
     return lax.ppermute(value, ("node", "slab"), pairs)
 
 
-def sum_steps(count):
-    assert count & (count - 1) == 0
-    steps = [1 << k for k in range(1, count.bit_length() - 1)]
-    return steps + [1 ^ (4 if count > 4 else 0)]
-
-
 def other_core(value):
     return lax.ppermute(value, "node", [(0, 1), (1, 0)])
 
@@ -362,25 +360,24 @@
     nx = source.shape[2]
     cells = wall.shape[1] * slabs * wall.shape[2]
     parts = 2 if nodes == 2 else 1
+    assert slabs & (slabs - 1) == 0 and slabs > 4
     *own, sums = edge_state(source, coef, wall)
     far = [swap_pairs(value, slot) for slot, value in enumerate(own)]
     inner, b, base, weight = first_sweep(block, source, coef, metric, sums)
-    first, *steps = sum_steps(slabs)
+    first, *bits, last = [1 << k for k in range(1, slabs.bit_length() - 1)]
     sums = after(sums + from_partner(sums, first), base)
-    early, late = steps[: len(steps) // 2], steps[len(steps) // 2 :]
-    for slab in early:
+    states = edge_states(block, source, coef, sums)
+    for slab in bits:
         sums = sums + from_partner(sums, slab)
-    states = edge_states(block, source, coef, sums)
-    odd = swap_pairs(states[1], 1)
+    odd = swap_pairs(after(states[1], sums), 1)
+    if parts == 1:
+        sums = lax.psum(sums, "node")
     edges = second_states(block, far, states, sums)
     even = swap_pairs(edges[0], 0)
     sums = after(sums, edges[0])
-    for slab in late:
-        sums = sums + from_partner(sums, slab)
-    if parts == 1:
-        sums = lax.psum(sums, "node")
+    sums = [sums] + [from_partner(sums, last ^ k) for k in (0, 1)]
     sens = last_sweep(coef, inner, edges, b, base)
-    terms = list(node_terms(parts, sens, sums, weight, even, odd))
+    terms = list(node_terms(parts, sens, weight, even, odd, sums))
     if parts == 2:
         terms[1] = other_core(terms[1])
         return gradient(nodes, cells, nx, terms)

time: 45 us -> 44.5 us (0.989); the launches traced: 44.7 us -> 43.7 us
  waiting for transfers between devices: 15.9 us -> 14.5 us
    ppermute x4, waiting for transfers between devices: 12.1 us -> 4.09 us  [from_partner(): return lax.ppermute(value, ('node', 'slab'), pairs)]
    ppermute x4, waiting for transfers between devices: 2.68 us -> 9.22 us  [swap_pairs(): return lax.ppermute(value, 'slab', pairs)]
where the time goes in v3:
time: 44.5 us; the launch traced here: 43.7 us
  starting transfers between devices  15.7 us (35%)
  waiting for transfers between devices  14.5 us (33%)
  Pallas kernels  9.91 us (22%)
  local copies, waits for them, and re-layouts  3.5 us (8%)
    ppermute x4, waiting for transfers between devices, swap_pairs(): return lax.ppermute(value, 'slab', pairs)  9.22 us
    ppermute x4, starting transfers between devices, swap_pairs(): return lax.ppermute(value, 'slab', pairs)  8.02 us
    ppermute x4, starting transfers between devices, from_partner(): return lax.ppermute(value, ('node', 'slab'), pairs)  7.65 us
    ppermute x4, waiting for transfers between devices, from_partner(): return lax.ppermute(value, ('node', 'slab'), pairs)  4.09 us
    unnamed x11, local copies, waits for them, and re-layouts  3.5 us
    pallas_call x1, Pallas kernels, first_sweep(): call(first_kernel, 'first_sweep', out_shape=(f32(nv, nx - 2, ny, nz), f32...  2.79 us
    pallas_call x1, Pallas kernels, edge_state(): call(edge_kernel, 'edge_state', out_shape=(f32(nv, ny, nz),) * 2 + (f32(R...  2.36 us
    pallas_call x1, Pallas kernels, edge_states(): call(states_kernel, 'edge_states', out_shape=(f32(rows, nz),) * 2, in_spe...  1.55 us
  transfers between devices with their start and end apart: 9, of which 6 were waited for; matrix products, arithmetic and copies ran while one was open for 0% of the time, Pallas kernels for 15%

profile of v3, /device:TPU:0, one launch (start us, length us, event | category | flops | bytes accessed | tf_op | source)
XLA Modules:
  0.0 43.7 jit_solution(16688316306970626644)
XLA Ops:
  0.0 0.0 copy-start
  0.0 0.0 copy-start.4
  0.0 2.4 %edge_state.1 = (f32[6,64,256]{2,1,0:T(8,128)}, f32[6,64,256]{2,1,0:T(8,128)}, f32[8,128]{1,0:T(8,128)}) custom-call(f32[1,6,4,64,256]{4,3,2,1,0:T(8,128)} %s_ref.5, f32[1,4,4,64,256]{4,3,2,1,0:T(8,128)} %c_ref.7, f32[1,4,256]{2,1,0:T(4,128)} %wall_ref.1), custom_call_target="tpu_custom_call" | custom-call | tf_op jit(solution)/shard_map/edge_state/pallas_call | solution.py:79
  2.4 3.0 %collective-permute-start = (f32[6,64,256]{2,1,0:T(8,128)}, f32[6,64,256]{2,1,0:T(8,128)S(1)}, u32[]{:S(2)}, u32[]{:S(2)}) collective-permute-start(f32[6,64,256]{2,1,0:T(8,128)} %get-tuple-element.23), channel_id=1, source_target_pairs={{0,1},{1,0},{2,3},{3,2},{4,5},{5,4},{6,7},{7,6},{8,9},{9,8},{10,11... | collective-permute-start | bytes 1179656 | tf_op jit(solution)/shard_map/ppermute | solution.py:339
  5.4 0.7 %collective-permute-start.1 = (f32[6,64,256]{2,1,0:T(8,128)}, f32[6,64,256]{2,1,0:T(8,128)S(1)}, u32[]{:S(2)}, u32[]{:S(2)}) collective-permute-start(f32[6,64,256]{2,1,0:T(8,128)} %get-tuple-element.24), channel_id=1, source_target_pairs={{1,2},{2,1},{3,4},{4,3},{5,6},{6,5},{7,8},{8,7},{9,10},{10,9},{11,... | collective-permute-start | bytes 1179656 | tf_op jit(solution)/shard_map/ppermute | solution.py:339
  6.1 2.8 %collective-permute-start.2 = (f32[8,128]{1,0:T(8,128)}, f32[8,128]{1,0:T(8,128)S(1)}, u32[]{:S(2)}, u32[]{:S(2)}) collective-permute-start(f32[8,128]{1,0:T(8,128)} %get-tuple-element.21.after), channel_id=1, source_target_pairs={{0,2},{1,3},{2,0},{3,1},{4,6},{5,7},{6,4},{7,5},{8,10},{9,11},{10,... | collective-permute-start | bytes 12296 | tf_op jit(solution)/shard_map/ppermute | solution.py:347
  8.9 0.0 copy-done.4
  8.9 0.0 copy-done
  8.9 1.4 %copy-done.1 = f32[1,6,4,64,256]{4,3,2,1,0:T(8,128)S(1)} copy-done((f32[1,6,4,64,256]{4,3,2,1,0:T(8,128)S(1)}, f32[1,6,4,64,256]{4,3,2,1,0:T(8,128)}, u32[]{:S(2)}) %copy-start.1) | copy-done | bytes 1572888
  10.3 1.4 %copy-done.2 = f32[1,6,4,64,256]{4,3,2,1,0:T(8,128)S(1)} copy-done((f32[1,6,4,64,256]{4,3,2,1,0:T(8,128)S(1)}, f32[1,6,4,64,256]{4,3,2,1,0:T(8,128)}, u32[]{:S(2)}) %copy-start.2) | copy-done | bytes 1572888
  11.7 0.7 %copy-done.3 = f32[8,128]{1,0:T(8,128)S(1)} copy-done((f32[8,128]{1,0:T(8,128)S(1)}, f32[8,128]{1,0:T(8,128)}, u32[]{:S(2)}) %copy-start.3) | copy-done | bytes 4120
  12.4 2.8 %first_sweep.1 = (f32[6,2,64,256]{3,2,1,0:T(8,128)S(1)}, f32[6,4,64,256]{3,2,1,0:T(8,128)S(1)}, f32[4,256]{1,0:T(4,128)S(1)}, f32[832,256]{1,0:T(8,128)S(1)}) custom-call(f32[1,6,6]{2,1,0:T(8,128)S(1)} %copy.6.f_ref, f32[1,6,4,64,256]{4,3,2,1,0:T(8,128)S(1)} %copy-done.1, f32[1,4,4,64,256]{4,3,2,1,0:T(8,128)S(1)} %copy-done, ...), custom_call_target="tpu_custom_call" | custom-call | tf_op jit(solution)/shard_map/first_sweep/pallas_call | solution.py:195
  15.2 0.0 collective-permute-done.2
  15.2 2.1 %collective-permute-start.3 = (f32[8,128]{1,0:T(8,128)S(1)}, f32[8,128]{1,0:T(8,128)S(1)}, u32[]{:S(2)}, u32[]{:S(2)}) collective-permute-start(f32[8,128]{1,0:T(8,128)S(1)} %add.6.after), channel_id=1, source_target_pairs={{0,4},{1,5},{2,6},{3,7},{4,0},{5,1},{6,2},{7,3},{8,12},{9,13},{10,... | collective-permute-start | bytes 12296 | tf_op jit(solution)/shard_map/ppermute | solution.py:347
  17.3 1.5 %edge_states.1 = (f32[448,256]{1,0:T(8,128)S(1)}, f32[448,256]{1,0:T(8,128)S(1)}) custom-call(f32[1,6,6]{2,1,0:T(8,128)S(1)} %copy.6.f_ref, f32[1,6,4,64,256]{4,3,2,1,0:T(8,128)S(1)} %copy-done.1, f32[1,4,4,64,256]{4,3,2,1,0:T(8,128)S(1)} %copy-done, f32[8,128]{1,0:T(8,128)S(1)} %add.6.after), custom_call_target="tpu_custom_call" | custom-call | tf_op jit(solution)/shard_map/edge_states/pallas_call | solution.py:138
  18.9 0.3 collective-permute-done.3
  19.1 0.7 %collective-permute-start.5 = (f32[448,256]{1,0:T(8,128)S(1)}, f32[448,256]{1,0:T(8,128)S(1)}, u32[]{:S(2)}, u32[]{:S(2)}) collective-permute-start(f32[448,256]{1,0:T(8,128)S(1)} %get-tuple-element.33.state1), channel_id=1, source_target_pairs={{1,2},{2,1},{3,4},{4,3},{5,6},{6,5},{7,8},{8,7},{9,10},{10,9},{11,... | collective-permute-start | bytes 1376264 | tf_op jit(solution)/shard_map/ppermute | solution.py:339
  19.8 2.7 %collective-permute-done.far0 = f32[6,64,256]{2,1,0:T(8,128)S(1)} collective-permute-done((f32[6,64,256]{2,1,0:T(8,128)}, f32[6,64,256]{2,1,0:T(8,128)S(1)}, u32[]{:S(2)}, u32[]{:S(2)}) %collective-permute-start) | collective-permute-done | bytes 393248 | tf_op jit(solution)/shard_map/ppermute | solution.py:339
  22.5 0.0 collective-permute-done.1.far1
  22.5 1.0 %second_states.1 = (f32[392,256]{1,0:T(8,128)S(1)}, f32[384,256]{1,0:T(8,128)S(1)}) custom-call(f32[1,6,6]{2,1,0:T(8,128)S(1)} %copy.6.f_ref, f32[6,64,256]{2,1,0:T(8,128)S(1)} %collective-permute-done.far0, f32[6,64,256]{2,1,0:T(8,128)S(1)} %collective-permute-done.1.far1, f32[448,256]{1,0:T(8,128)S(1)} %get-tuple-element.27.state0, ...), custom_call_target="tpu_custom_call" | custom-call | tf_op jit(solution)/shard_map/second_states/pallas_call | solution.py:224
  23.5 3.7 %collective-permute-start.4 = (f32[392,256]{1,0:T(8,128)S(1)}, f32[392,256]{1,0:T(8,128)S(1)}, u32[]{:S(2)}, u32[]{:S(2)}) collective-permute-start(f32[392,256]{1,0:T(8,128)S(1)} %get-tuple-element.29.whole0), channel_id=1, source_target_pairs={{0,1},{1,0},{2,3},{3,2},{4,5},{5,4},{6,7},{7,6},{8,9},{9,8},{10,11... | collective-permute-start | bytes 1204232 | tf_op jit(solution)/shard_map/ppermute | solution.py:339
  27.2 2.2 %collective-permute-start.7 = (f32[8,128]{1,0:T(8,128)S(1)}, f32[8,128]{1,0:T(8,128)S(1)}, u32[]{:S(2)}, u32[]{:S(2)}) collective-permute-start(f32[8,128]{1,0:T(8,128)S(1)} %add.7.sums_ref.refs_0_), channel_id=1, source_target_pairs={{0,9},{1,8},{2,11},{3,10},{4,13},{5,12},{6,15},{7,14},{8,1},{9,0},... | collective-permute-start | bytes 12296 | tf_op jit(solution)/shard_map/ppermute | solution.py:347
  29.4 0.5 %collective-permute-start.6 = (f32[8,128]{1,0:T(8,128)S(1)}, f32[8,128]{1,0:T(8,128)S(1)}, u32[]{:S(2)}, u32[]{:S(2)}) collective-permute-start(f32[8,128]{1,0:T(8,128)S(1)} %add.7.sums_ref.refs_0_), channel_id=1, source_target_pairs={{0,8},{1,9},{2,10},{3,11},{4,12},{5,13},{6,14},{7,15},{8,0},{9,1},... | collective-permute-start | bytes 12296 | tf_op jit(solution)/shard_map/ppermute | solution.py:347
  29.9 1.4 %last_sweep.1.sens_ref = f32[4,256]{1,0:T(4,128)S(1)} custom-call(f32[1,4,4,64,256]{4,3,2,1,0:T(8,128)S(1)} %copy-done, f32[6,2,64,256]{3,2,1,0:T(8,128)S(1)} %get-tuple-element.22.inner_ref, f32[392,256]{1,0:T(8,128)S(1)} %get-tuple-element.29.whole0, f32[384,256]{1,0:T(8,128)S(1)} %get-tuple-element.30.whole1, ...), custom_call_target="tpu_custom_call" | custom-call | flops 1100000000 | tf_op jit(solution)/shard_map/last_sweep/pallas_call | solution.py:257
  31.3 1.4 %collective-permute-done.7.refs_2_ = f32[8,128]{1,0:T(8,128)S(1)} collective-permute-done((f32[8,128]{1,0:T(8,128)S(1)}, f32[8,128]{1,0:T(8,128)S(1)}, u32[]{:S(2)}, u32[]{:S(2)}) %collective-permute-start.7) | collective-permute-done | bytes 4128 | tf_op jit(solution)/shard_map/ppermute | solution.py:347
  32.7 2.4 %collective-permute-done.6.refs_1_ = f32[8,128]{1,0:T(8,128)S(1)} collective-permute-done((f32[8,128]{1,0:T(8,128)S(1)}, f32[8,128]{1,0:T(8,128)S(1)}, u32[]{:S(2)}, u32[]{:S(2)}) %collective-permute-start.6) | collective-permute-done | bytes 4128 | tf_op jit(solution)/shard_map/ppermute | solution.py:347
  35.1 0.0 collective-permute-done.5.odd_ref
  35.1 6.5 %collective-permute-done.4.even_ref = f32[392,256]{1,0:T(8,128)S(1)} collective-permute-done((f32[392,256]{1,0:T(8,128)S(1)}, f32[392,256]{1,0:T(8,128)S(1)}, u32[]{:S(2)}, u32[]{:S(2)}) %collective-permute-start.4) | collective-permute-done | bytes 401440 | tf_op jit(solution)/shard_map/ppermute | solution.py:339
  41.6 0.2 node_terms.1
  41.8 0.1 collective-permute-start.8
  41.9 1.2 %collective-permute-done.8.refs_1_ = f32[16,128]{1,0:T(8,128)S(1)} collective-permute-done((f32[16,128]{1,0:T(8,128)S(1)}, f32[16,128]{1,0:T(8,128)S(1)}, u32[]{:S(2)}, u32[]{:S(2)}) %collective-permute-start.8) | collective-permute-done | bytes 8224 | tf_op jit(solution)/shard_map/ppermute | solution.py:351
  43.1 0.6 %gradient.1 = f32[4,128]{1,0:T(4,128)} custom-call(f32[16,128]{1,0:T(8,128)S(1)} %get-tuple-element.35.refs_0_, f32[16,128]{1,0:T(8,128)S(1)} %collective-permute-done.8.refs_1_), custom_call_target="tpu_custom_call" | custom-call | tf_op jit(solution)/shard_map/gradient/pallas_call | solution.py:324
  (6 shorter events, 0.0 us)
Async XLA Ops:
  0.0 8.9 %copy-start = (f32[1,4,4,64,256]{4,3,2,1,0:T(8,128)S(1)}, f32[1,4,4,64,256]{4,3,2,1,0:T(8,128)}, u32[]{:S(2)}) copy-start(f32[1,4,4,64,256]{4,3,2,1,0:T(8,128)} %c_ref.7) | copy-start | bytes 3145732
  0.0 8.9 %copy-start.4 = (f32[1,6,6]{2,0,1:T(1,128)S(1)}, f32[1,6,6]{2,0,1:T(1,128)}, u32[]{:S(2)}) copy-start(f32[1,6,6]{2,0,1:T(1,128)} %param.7) | copy-start | bytes 436
  2.4 20.1 %collective-permute-start = (f32[6,64,256]{2,1,0:T(8,128)}, f32[6,64,256]{2,1,0:T(8,128)S(1)}, u32[]{:S(2)}, u32[]{:S(2)}) collective-permute-start(f32[6,64,256]{2,1,0:T(8,128)} %get-tuple-element.23), channel_id=1, source_target_pairs={{0,1},{1,0},{2,3},{3,2},{4,5},{5,4},{6,7},{7,6},{8,9},{9,8},{10,11... | collective-permute-start | bytes 1179656 | tf_op jit(solution)/shard_map/ppermute | solution.py:339
  5.4 17.1 %collective-permute-start.1 = (f32[6,64,256]{2,1,0:T(8,128)}, f32[6,64,256]{2,1,0:T(8,128)S(1)}, u32[]{:S(2)}, u32[]{:S(2)}) collective-permute-start(f32[6,64,256]{2,1,0:T(8,128)} %get-tuple-element.24), channel_id=1, source_target_pairs={{1,2},{2,1},{3,4},{4,3},{5,6},{6,5},{7,8},{8,7},{9,10},{10,9},{11,... | collective-permute-start | bytes 1179656 | tf_op jit(solution)/shard_map/ppermute | solution.py:339
  6.1 9.1 %collective-permute-start.2 = (f32[8,128]{1,0:T(8,128)}, f32[8,128]{1,0:T(8,128)S(1)}, u32[]{:S(2)}, u32[]{:S(2)}) collective-permute-start(f32[8,128]{1,0:T(8,128)} %get-tuple-element.21.after), channel_id=1, source_target_pairs={{0,2},{1,3},{2,0},{3,1},{4,6},{5,7},{6,4},{7,5},{8,10},{9,11},{10,... | collective-permute-start | bytes 12296 | tf_op jit(solution)/shard_map/ppermute | solution.py:347
  8.9 1.4 %copy-start.1 = (f32[1,6,4,64,256]{4,3,2,1,0:T(8,128)S(1)}, f32[1,6,4,64,256]{4,3,2,1,0:T(8,128)}, u32[]{:S(2)}) copy-start(f32[1,6,4,64,256]{4,3,2,1,0:T(8,128)} %s_ref.5) | copy-start | bytes 4718596
  10.3 1.4 %copy-start.2 = (f32[1,6,4,64,256]{4,3,2,1,0:T(8,128)S(1)}, f32[1,6,4,64,256]{4,3,2,1,0:T(8,128)}, u32[]{:S(2)}) copy-start(f32[1,6,4,64,256]{4,3,2,1,0:T(8,128)} %m_ref.1) | copy-start | bytes 4718596
  11.7 0.7 %copy-start.3 = (f32[8,128]{1,0:T(8,128)S(1)}, f32[8,128]{1,0:T(8,128)}, u32[]{:S(2)}) copy-start(f32[8,128]{1,0:T(8,128)} %get-tuple-element.21.after) | copy-start | bytes 12292
  15.2 3.9 %collective-permute-start.3 = (f32[8,128]{1,0:T(8,128)S(1)}, f32[8,128]{1,0:T(8,128)S(1)}, u32[]{:S(2)}, u32[]{:S(2)}) collective-permute-start(f32[8,128]{1,0:T(8,128)S(1)} %add.6.after), channel_id=1, source_target_pairs={{0,4},{1,5},{2,6},{3,7},{4,0},{5,1},{6,2},{7,3},{8,12},{9,13},{10,... | collective-permute-start | bytes 12296 | tf_op jit(solution)/shard_map/ppermute | solution.py:347
  19.1 16.0 %collective-permute-start.5 = (f32[448,256]{1,0:T(8,128)S(1)}, f32[448,256]{1,0:T(8,128)S(1)}, u32[]{:S(2)}, u32[]{:S(2)}) collective-permute-start(f32[448,256]{1,0:T(8,128)S(1)} %get-tuple-element.33.state1), channel_id=1, source_target_pairs={{1,2},{2,1},{3,4},{4,3},{5,6},{6,5},{7,8},{8,7},{9,10},{10,9},{11,... | collective-permute-start | bytes 1376264 | tf_op jit(solution)/shard_map/ppermute | solution.py:339
  23.5 18.1 %collective-permute-start.4 = (f32[392,256]{1,0:T(8,128)S(1)}, f32[392,256]{1,0:T(8,128)S(1)}, u32[]{:S(2)}, u32[]{:S(2)}) collective-permute-start(f32[392,256]{1,0:T(8,128)S(1)} %get-tuple-element.29.whole0), channel_id=1, source_target_pairs={{0,1},{1,0},{2,3},{3,2},{4,5},{5,4},{6,7},{7,6},{8,9},{9,8},{10,11... | collective-permute-start | bytes 1204232 | tf_op jit(solution)/shard_map/ppermute | solution.py:339
  27.2 5.5 %collective-permute-start.7 = (f32[8,128]{1,0:T(8,128)S(1)}, f32[8,128]{1,0:T(8,128)S(1)}, u32[]{:S(2)}, u32[]{:S(2)}) collective-permute-start(f32[8,128]{1,0:T(8,128)S(1)} %add.7.sums_ref.refs_0_), channel_id=1, source_target_pairs={{0,9},{1,8},{2,11},{3,10},{4,13},{5,12},{6,15},{7,14},{8,1},{9,0},... | collective-permute-start | bytes 12296 | tf_op jit(solution)/shard_map/ppermute | solution.py:347
  29.4 5.7 %collective-permute-start.6 = (f32[8,128]{1,0:T(8,128)S(1)}, f32[8,128]{1,0:T(8,128)S(1)}, u32[]{:S(2)}, u32[]{:S(2)}) collective-permute-start(f32[8,128]{1,0:T(8,128)S(1)} %add.7.sums_ref.refs_0_), channel_id=1, source_target_pairs={{0,8},{1,9},{2,10},{3,11},{4,12},{5,13},{6,14},{7,15},{8,0},{9,1},... | collective-permute-start | bytes 12296 | tf_op jit(solution)/shard_map/ppermute | solution.py:347
  41.8 1.2 %collective-permute-start.8 = (f32[16,128]{1,0:T(8,128)S(1)}, f32[16,128]{1,0:T(8,128)S(1)}, u32[]{:S(2)}, u32[]{:S(2)}) collective-permute-start(f32[16,128]{1,0:T(8,128)S(1)} %get-tuple-element.36), channel_id=1, source_target_pairs={{0,16},{16,0},{1,17},{17,1},{2,18},{18,2},{3,19},{19,3},{4,20},{20... | collective-permute-start | bytes 24584 | tf_op jit(solution)/shard_map/ppermute | solution.py:351

commit v4 on v3

--- a/solution.py
+++ b/solution.py
@@ -115,38 +115,38 @@
     return mix
 
 
-def states_kernel(f_ref, s_ref, c_ref, after, even_ref, odd_ref, q_ref, p_ref):
+def state_kernel(slot, f_ref, s_ref, c_ref, after, out, q_ref, p_ref):
     del after
     nv, nx, ny, nz = s_ref.shape[1:]
     zero = jnp.zeros((ny, nz), jnp.float32)
-    for slot, out in ((0, even_ref), (1, odd_ref)):
-        edge = edge_of(slot, nx)
-        inner = jnp.where(edge == 0, 1, nx - 2)
-        inv = inverse_diag(lambda k: c_ref[0, k, edge])
-        inv_inner = inverse_diag(lambda k: c_ref[0, k, inner])
-        for v in range(nv):
-            p_ref[v] = s_ref[0, v, edge] * inv
-            beside = s_ref[0, v, inner] * inv_inner
-            q_ref[v] = coupled(c_ref, edge, beside, p_ref[v], zero)
-        for w in range(nv):
-            out[pl.ds(w * ny, ny), :] = p_ref[w] + inv * mixed(f_ref, w, lambda v: q_ref[v])
-        out[pl.ds(nv * ny, ny), :] = c_ref[0, 1, edge] * inv
-
-def edge_states(block, source, coef, after):
+    edge = edge_of(slot, nx)
+    inner = jnp.where(edge == 0, 1, nx - 2)
+    inv = inverse_diag(lambda k: c_ref[0, k, edge])
+    inv_inner = inverse_diag(lambda k: c_ref[0, k, inner])
+    for v in range(nv):
+        p_ref[v] = s_ref[0, v, edge] * inv
+        beside = s_ref[0, v, inner] * inv_inner
+        q_ref[v] = coupled(c_ref, edge, beside, p_ref[v], zero)
+    for w in range(nv):
+        out[pl.ds(w * ny, ny), :] = p_ref[w] + inv * mixed(f_ref, w, lambda v: q_ref[v])
+    out[pl.ds(nv * ny, ny), :] = c_ref[0, 1, edge] * inv
+
+
+def edge_second(slot, block, source, coef, after):
     nv, nx, ny, nz = source.shape[1:]
-    rows = (nv + 1) * ny
-    return call(
-        states_kernel,
-        "edge_states",
-        out_shape=(f32(rows, nz),) * 2,
+    return call(
+        functools.partial(state_kernel, slot),
+        f"edge_second{slot}",
+        out_shape=f32((nv + 1) * ny, nz),
         in_specs=[SMEM] + [VMEM] * 2 + [ANY],
-        out_specs=(VMEM,) * 2,
+        out_specs=VMEM,
         scratch_shapes=[pltpu.VMEM((nv, ny, nz), jnp.float32)] * 2,
     )(block, source, coef, after)
 
 
-def first_kernel(f_ref, s_ref, c_ref, m_ref, after, p1_ref, b_ref, sens_ref, weight_ref, p0, q_ref, inv_ref):
+def first_kernel(parts, f_ref, s_ref, c_ref, m_ref, after, p1_ref, b_ref, sens_ref, weight_ref, *refs):
     del after
+    shares, (p0, q_ref, inv_ref) = refs[:parts], refs[parts:]
     nv, nx, ny, nz = s_ref.shape[1:]
 
     def start(x, _):
@@ -186,18 +186,21 @@
             if slot == 1:
                 total = total + weight * mixed(f_ref, w, lambda v: p0[v, edge])
     weight_ref[pl.ds(2 * nv * ny, ny), :] = total
-
-
-def first_sweep(block, source, coef, metric, after):
+    for part, out in enumerate(shares):
+        out[...] = share(weight_ref, parts, 0, nv * ny, part)
+
+
+def first_sweep(parts, block, source, coef, metric, after):
     nv, nx, ny, nz = source.shape[1:]
     assert 2 < nx <= ROWS
     rows = (2 * nv + 1) * ny
     return call(
-        first_kernel,
+        functools.partial(first_kernel, parts),
         "first_sweep",
-        out_shape=(f32(nv, nx - 2, ny, nz), f32(nv, nx, ny, nz), f32(nx, nz), f32(rows, nz)),
+        out_shape=(f32(nv, nx - 2, ny, nz), f32(nv, nx, ny, nz), f32(nx, nz), f32(rows, nz))
+        + (f32(nv * ny, nz // parts),) * parts,
         in_specs=[SMEM] + [VMEM] * 3 + [ANY],
-        out_specs=(VMEM,) * 4,
+        out_specs=(VMEM,) * (4 + parts),
         scratch_shapes=[
             pltpu.VMEM((nv, nx, ny, nz), jnp.float32),
             pltpu.VMEM((nv, ny, nz), jnp.float32),
@@ -206,7 +209,7 @@
     )(block, source, coef, metric, after)
 
 
-def second_kernel(f_ref, far0, far1, state0, state1, sums_ref, whole0, whole1):
+def second_kernel(parts, f_ref, far0, far1, state0, state1, sums_ref, whole0, whole1, *msgs):
     nv, ny, nz = far0.shape
     rows = nv * ny
     for far, state, whole in ((far0, state0, whole0), (far1, state1, whole1)):
@@ -214,19 +217,20 @@
         for w in range(nv):
             mix = mixed(f_ref, w, lambda v: far[v])
             whole[pl.ds(w * ny, ny), :] = state[pl.ds(w * ny, ny), :] + rho * mix
-    for k in range(nz // 128):
-        whole0[pl.ds(rows, ROWS), pl.ds(k * 128, 128)] = sums_ref[...]
-
-
-def second_states(block, far, states, sums):
+    for part, msg in enumerate(msgs):
+        msg[pl.ds(0, rows), :] = share(whole0, parts, 0, rows, part)
+        for k in range(msg.shape[1] // 128):
+            msg[pl.ds(rows, ROWS), pl.ds(k * 128, 128)] = sums_ref[...]
+
+
+def second_states(parts, block, far, states, sums):
     nv, ny, nz = far[0].shape
-    rows = nv * ny
-    return call(
-        second_kernel,
+    return call(
+        functools.partial(second_kernel, parts),
         "second_states",
-        out_shape=(f32(rows + ROWS, nz), f32(rows, nz)),
+        out_shape=(f32(nv * ny, nz),) * 2 + (f32(nv * ny + ROWS, nz // parts),) * parts,
         in_specs=[SMEM] + [VMEM] * 5,
-        out_specs=(VMEM,) * 2,
+        out_specs=(VMEM,) * (2 + parts),
     )(block, *far, *states, sums)
 
 
@@ -274,60 +278,65 @@
     return [w * (1.0 + 2.0 * (o - mean) / spread) for w, o in zip(weight, objective)]
 
 
-def node_kernel(parts, few, sens_ref, weight_ref, even_ref, odd_ref, *refs):
-    sums, outs, acc = refs[:few], refs[few:-1], refs[-1]
+def node_kernel(parts, few, sens_ref, weight_ref, odd_ref, *refs):
+    sums, outs, acc = refs[:few], refs[few + 1 : -1], refs[-1]
     nx, nz = sens_ref.shape
-    rows = even_ref.shape[0] - ROWS
+    rows = odd_ref.shape[0]
     acc[...] = jnp.zeros_like(acc)
     acc[pl.ds(0, nx), :] = sens_ref[...]
-    total = even_ref[pl.ds(rows, ROWS), pl.ds(0, 128)]
-    for other in sums:
+    total = sums[0][...]
+    for other in sums[1:]:
         total = total + other[...]
     for k in range(nz // 128):
         acc[pl.ds(ROWS, ROWS), pl.ds(k * 128, 128)] = total
-    total = weight_ref[pl.ds(0, rows), :] * even_ref[pl.ds(0, rows), :]
-    acc[pl.ds(edge_of(0, nx), 1), :] += jnp.sum(total, axis=0, keepdims=True)
-    total = weight_ref[pl.ds(rows, odd_ref.shape[0]), :] * odd_ref[...]
+    total = weight_ref[pl.ds(weight_ref.shape[0] - rows, rows), :] * odd_ref[...]
     acc[pl.ds(edge_of(1, nx), 1), :] += jnp.sum(total, axis=0, keepdims=True)
     for part, out in enumerate(outs):
         out[...] = share(acc, parts, 0, 2 * ROWS, part)
 
 
-def node_terms(parts, sens, weight, even, odd, sums):
+def node_terms(parts, sens, weight, odd, sums, after):
     nx, nz = sens.shape
     return call(
         functools.partial(node_kernel, parts, len(sums)),
         "node_terms",
         out_shape=(f32(2 * ROWS, nz // parts),) * parts,
-        in_specs=[VMEM] * (4 + len(sums)),
+        in_specs=[VMEM] * (3 + len(sums)) + [ANY],
         out_specs=(VMEM,) * parts,
         scratch_shapes=[pltpu.VMEM((2 * ROWS, nz), jnp.float32)],
-    )(sens, weight, even, odd, *sums)
-
-
-def gradient_kernel(nodes, cells, *refs):
-    terms, out_ref = refs[:-1], refs[-1]
+    )(sens, weight, odd, *sums, after)
+
+
+def gradient_kernel(parts, nodes, cells, *refs):
+    terms, weights, msgs = (refs[k * parts : (k + 1) * parts] for k in range(3))
+    out_ref, acc = refs[3 * parts :]
     nx = out_ref.shape[0]
-    factor = factors(nodes, cells, sum(term[pl.ds(ROWS, ROWS), pl.ds(0, 128)] for term in terms))
+    rows = weights[0].shape[0]
+    sums = sum(r[pl.ds(at, ROWS), pl.ds(0, 128)] for refs, at in ((terms, ROWS), (msgs, rows)) for r in refs)
+    factor = factors(nodes, cells, sums)
     node = lax.axis_index("node")
-    total = jnp.zeros(out_ref.shape, jnp.float32)
-    for part, term in enumerate(terms):
+    out_ref[...] = jnp.zeros_like(out_ref)
+    for part in range(parts):
+        acc[...] = terms[part][pl.ds(0, ROWS), :]
+        total = weights[part][...] * msgs[part][pl.ds(0, rows), :]
+        acc[pl.ds(edge_of(0, nx), 1), :] += jnp.sum(total, axis=0, keepdims=True)
         whose = node if part == 0 else 1 - node
         scale = factor[0]
         for n in range(1, nodes):
             scale = jnp.where(whose == n, factor[n], scale)
-        total = total + term[pl.ds(0, nx), :] * scale[:, :1]
-    out_ref[...] = total
-
-
-def gradient(nodes, cells, nx, terms):
-    return call(
-        functools.partial(gradient_kernel, nodes, cells),
+        out_ref[...] += acc[pl.ds(0, nx), :] * scale[:, :1]
+
+
+def gradient(nodes, cells, nx, terms, weights, msgs):
+    parts, width = len(terms), terms[0].shape[1]
+    return call(
+        functools.partial(gradient_kernel, parts, nodes, cells),
         "gradient",
-        out_shape=f32(nx, terms[0].shape[1]),
-        in_specs=[VMEM] * len(terms),
+        out_shape=f32(nx, width),
+        in_specs=[VMEM] * (3 * parts),
         out_specs=VMEM,
-    )(*terms)
+        scratch_shapes=[pltpu.VMEM((ROWS, width), jnp.float32)],
+    )(*terms, *weights, *msgs)
 
 
 def swap_pairs(value, slot, part=0):
@@ -363,25 +372,28 @@
     assert slabs & (slabs - 1) == 0 and slabs > 4
     *own, sums = edge_state(source, coef, wall)
     far = [swap_pairs(value, slot) for slot, value in enumerate(own)]
-    inner, b, base, weight = first_sweep(block, source, coef, metric, sums)
-    first, *bits, last = [1 << k for k in range(1, slabs.bit_length() - 1)]
+    inner, b, base, weight, *weights = first_sweep(parts, block, source, coef, metric, sums)
+    first, *bits = [1 << k for k in range(1, slabs.bit_length() - 1)]
     sums = after(sums + from_partner(sums, first), base)
-    states = edge_states(block, source, coef, sums)
-    for slab in bits:
+    states = [edge_second(0, block, source, coef, sums)]
+    for slab in bits[:-1]:
         sums = sums + from_partner(sums, slab)
-    odd = swap_pairs(after(states[1], sums), 1)
     if parts == 1:
         sums = lax.psum(sums, "node")
-    edges = second_states(block, far, states, sums)
-    even = swap_pairs(edges[0], 0)
+    states.append(edge_second(1, block, source, coef, sums))
+    odd = swap_pairs(states[1], 1)
+    edges = second_states(parts, block, far, states, sums)
+    evens = [swap_pairs(value, 0, part) for part, value in enumerate(edges[2:])]
     sums = after(sums, edges[0])
-    sums = [sums] + [from_partner(sums, last ^ k) for k in (0, 1)]
-    sens = last_sweep(coef, inner, edges, b, base)
-    terms = list(node_terms(parts, sens, weight, even, odd, sums))
+    sums = [sums] + [from_partner(sums, bits[-1] ^ k) for k in (0, 1)]
+    weights[1:] = [other_core(value) for value in weights[1:]]
+    sens = last_sweep(coef, inner, edges[:2], b, base)
+    terms = list(node_terms(parts, sens, weight, odd, sums, weights[-1]))
+    terms[1:] = [other_core(value) for value in terms[1:]]
+    term = gradient(nodes, cells, nx, terms, weights, evens)
     if parts == 2:
-        terms[1] = other_core(terms[1])
-        return gradient(nodes, cells, nx, terms)
-    total = lax.psum(gradient(nodes, cells, nx, terms), "node")
+        return term
+    total = lax.psum(term, "node")
     width = total.shape[1] // nodes
     return lax.dynamic_slice_in_dim(total, lax.axis_index("node") * width, width, 1)
 

time: 44.5 us -> 43.5 us (0.978); the launches traced: 43.7 us -> 43.2 us
  waiting for transfers between devices: 14.5 us -> 11.6 us
  starting transfers between devices: 15.7 us -> 17.4 us
  Pallas kernels: 9.91 us -> 10.6 us
    ppermute x4, waiting for transfers between devices: 9.22 us -> 3.05 us  [swap_pairs(): return lax.ppermute(value, 'slab', pairs)]
    ppermute x0 -> x1, waiting for transfers between devices: none -> 2.27 us  [swap_pairs(): return lax.ppermute(value, ('node', 'slab'), cross)]
    ppermute x4, starting transfers between devices: 7.65 us -> 9 us  [from_partner(): return lax.ppermute(value, ('node', 'slab'), pairs)]
    ppermute x4, waiting for transfers between devices: 4.09 us -> 5.15 us  [from_partner(): return lax.ppermute(value, ('node', 'slab'), pairs)]
    pallas_call x4 -> x5, Pallas kernels: 5.98 us -> 6.74 us  [the longest x1 2.85 us: first_sweep(): call(functools.partial(first_kernel, parts), 'first_sweep', out_shape=(f3...]
    unnamed x11 -> x13, local copies, waits for them, and re-layouts: 3.5 us -> 3.51 us
    ppermute x1 -> x2, waiting for transfers between devices: 1.16 us -> 1.16 us  [other_core(): return lax.ppermute(value, 'node', [(0, 1), (1, 0)])]
  transfers between devices with their start and end apart: 9 -> 11, of which waited for: 6 -> 7; matrix products, arithmetic and copies ran while one was open for 0% -> 0% of each run, Pallas kernels for 15% -> 17%
where the time goes in v4:
time: 43.5 us; the launch traced here: 43.2 us
  starting transfers between devices  17.4 us (40%)
  waiting for transfers between devices  11.6 us (27%)
  Pallas kernels  10.6 us (24%)
  local copies, waits for them, and re-layouts  3.51 us (8%)
    ppermute x4, starting transfers between devices, from_partner(): return lax.ppermute(value, ('node', 'slab'), pairs)  9 us
    ppermute x4, starting transfers between devices, swap_pairs(): return lax.ppermute(value, 'slab', pairs)  8.09 us
    ppermute x4, waiting for transfers between devices, from_partner(): return lax.ppermute(value, ('node', 'slab'), pairs)  5.15 us
    unnamed x13, local copies, waits for them, and re-layouts  3.51 us
    ppermute x4, waiting for transfers between devices, swap_pairs(): return lax.ppermute(value, 'slab', pairs)  3.05 us
    pallas_call x1, Pallas kernels, first_sweep(): call(functools.partial(first_kernel, parts), 'first_sweep', out_shape=(f3...  2.85 us
    pallas_call x1, Pallas kernels, edge_state(): call(edge_kernel, 'edge_state', out_shape=(f32(nv, ny, nz),) * 2 + (f32(R...  2.36 us
    ppermute x1, waiting for transfers between devices, swap_pairs(): return lax.ppermute(value, ('node', 'slab'), cross)  2.27 us
  transfers between devices with their start and end apart: 11, of which 7 were waited for; matrix products, arithmetic and copies ran while one was open for 0% of the time, Pallas kernels for 17%

profile of v4, /device:TPU:0, one launch (start us, length us, event | category | flops | bytes accessed | tf_op | source)
XLA Modules:
  0.0 43.2 jit_solution(17853691456446930712)
XLA Ops:
  0.0 2.4 %edge_state.1 = (f32[6,64,256]{2,1,0:T(8,128)}, f32[6,64,256]{2,1,0:T(8,128)}, f32[8,128]{1,0:T(8,128)}) custom-call(f32[1,6,4,64,256]{4,3,2,1,0:T(8,128)} %s_ref.7, f32[1,4,4,64,256]{4,3,2,1,0:T(8,128)} %c_ref.9, f32[1,4,256]{2,1,0:T(4,128)} %wall_ref.1), custom_call_target="tpu_custom_call" | custom-call | tf_op jit(solution)/shard_map/edge_state/pallas_call | solution.py:79
  2.4 3.0 %collective-permute-start = (f32[6,64,256]{2,1,0:T(8,128)}, f32[6,64,256]{2,1,0:T(8,128)S(1)}, u32[]{:S(2)}, u32[]{:S(2)}) collective-permute-start(f32[6,64,256]{2,1,0:T(8,128)} %get-tuple-element.24), channel_id=1, source_target_pairs={{0,1},{1,0},{2,3},{3,2},{4,5},{5,4},{6,7},{7,6},{8,9},{9,8},{10,11... | collective-permute-start | bytes 1179656 | tf_op jit(solution)/shard_map/ppermute | solution.py:348
  5.4 0.7 %collective-permute-start.1 = (f32[6,64,256]{2,1,0:T(8,128)}, f32[6,64,256]{2,1,0:T(8,128)S(1)}, u32[]{:S(2)}, u32[]{:S(2)}) collective-permute-start(f32[6,64,256]{2,1,0:T(8,128)} %get-tuple-element.25), channel_id=1, source_target_pairs={{1,2},{2,1},{3,4},{4,3},{5,6},{6,5},{7,8},{8,7},{9,10},{10,9},{11,... | collective-permute-start | bytes 1179656 | tf_op jit(solution)/shard_map/ppermute | solution.py:348
  6.1 2.8 %collective-permute-start.2 = (f32[8,128]{1,0:T(8,128)}, f32[8,128]{1,0:T(8,128)S(1)}, u32[]{:S(2)}, u32[]{:S(2)}) collective-permute-start(f32[8,128]{1,0:T(8,128)} %get-tuple-element.22.after), channel_id=1, source_target_pairs={{0,2},{1,3},{2,0},{3,1},{4,6},{5,7},{6,4},{7,5},{8,10},{9,11},{10,... | collective-permute-start | bytes 12296 | tf_op jit(solution)/shard_map/ppermute | solution.py:356
  8.9 1.4 %copy-done.1 = f32[1,6,4,64,256]{4,3,2,1,0:T(8,128)S(1)} copy-done((f32[1,6,4,64,256]{4,3,2,1,0:T(8,128)S(1)}, f32[1,6,4,64,256]{4,3,2,1,0:T(8,128)}, u32[]{:S(2)}) %copy-start.1) | copy-done | bytes 1572888
  10.3 1.4 %copy-done.2 = f32[1,6,4,64,256]{4,3,2,1,0:T(8,128)S(1)} copy-done((f32[1,6,4,64,256]{4,3,2,1,0:T(8,128)S(1)}, f32[1,6,4,64,256]{4,3,2,1,0:T(8,128)}, u32[]{:S(2)}) %copy-start.2) | copy-done | bytes 1572888
  11.7 0.7 %copy-done.3 = f32[8,128]{1,0:T(8,128)S(1)} copy-done((f32[8,128]{1,0:T(8,128)S(1)}, f32[8,128]{1,0:T(8,128)}, u32[]{:S(2)}) %copy-start.3) | copy-done | bytes 4120
  12.4 2.8 %first_sweep.1 = (f32[6,2,64,256]{3,2,1,0:T(8,128)S(1)}, f32[6,4,64,256]{3,2,1,0:T(8,128)S(1)}, f32[4,256]{1,0:T(4,128)S(1)}, f32[832,256]{1,0:T(8,128)S(1)}, f3...) custom-call(f32[1,6,6]{2,1,0:T(8,128)S(1)} %copy.6.f_ref, f32[1,6,4,64,256]{4,3,2,1,0:T(8,128)S(1)} %copy-done.1, ...), custom_call_target="tpu_custom_call" | custom-call | tf_op jit(solution)/shard_map/first_sweep/pallas_call | solution.py:197
  15.2 0.0 collective-permute-done.2
  15.3 2.1 %collective-permute-start.3 = (f32[8,128]{1,0:T(8,128)S(1)}, f32[8,128]{1,0:T(8,128)S(1)}, u32[]{:S(2)}, u32[]{:S(2)}) collective-permute-start(f32[8,128]{1,0:T(8,128)S(1)} %add.6.after), channel_id=1, source_target_pairs={{0,4},{1,5},{2,6},{3,7},{4,0},{5,1},{6,2},{7,3},{8,12},{9,13},{10,... | collective-permute-start | bytes 12296 | tf_op jit(solution)/shard_map/ppermute | solution.py:356
  17.4 1.8 %collective-permute-done.3 = f32[8,128]{1,0:T(8,128)S(1)} collective-permute-done((f32[8,128]{1,0:T(8,128)S(1)}, f32[8,128]{1,0:T(8,128)S(1)}, u32[]{:S(2)}, u32[]{:S(2)}) %collective-permute-start.3) | collective-permute-done | bytes 4128 | tf_op jit(solution)/shard_map/ppermute | solution.py:356
  19.1 1.1 %edge_second1.1.state1 = f32[448,256]{1,0:T(8,128)S(1)} custom-call(f32[1,6,6]{2,1,0:T(8,128)S(1)} %copy.6.f_ref, f32[1,6,4,64,256]{4,3,2,1,0:T(8,128)S(1)} %copy-done.1, f32[1,4,4,64,256]{4,3,2,1,0:T(8,128)S(1)} %copy-done, f32[8,128]{1,0:T(8,128)S(1)} %add.7.after.sums_ref.refs_0_), custom_call_target="tpu_custom_call" | custom-call | tf_op jit(solution)/shard_map/edge_second1/pallas_call | solution.py:137
  20.2 0.7 %collective-permute-start.4 = (f32[448,256]{1,0:T(8,128)S(1)}, f32[448,256]{1,0:T(8,128)S(1)}, u32[]{:S(2)}, u32[]{:S(2)}) collective-permute-start(f32[448,256]{1,0:T(8,128)S(1)} %edge_second1.1.state1), channel_id=1, source_target_pairs={{1,2},{2,1},{3,4},{4,3},{5,6},{6,5},{7,8},{8,7},{9,10},{10,9},{11,... | collective-permute-start | bytes 1376264 | tf_op jit(solution)/shard_map/ppermute | solution.py:348
  20.9 0.1 collective-permute-start.7
  21.0 1.1 %edge_second0.1.state0 = f32[448,256]{1,0:T(8,128)S(1)} custom-call(f32[1,6,6]{2,1,0:T(8,128)S(1)} %copy.6.f_ref, f32[1,6,4,64,256]{4,3,2,1,0:T(8,128)S(1)} %copy-done.1, f32[1,4,4,64,256]{4,3,2,1,0:T(8,128)S(1)} %copy-done, f32[8,128]{1,0:T(8,128)S(1)} %add.6.after), custom_call_target="tpu_custom_call" | custom-call | tf_op jit(solution)/shard_map/edge_second0/pallas_call | solution.py:137
  22.1 0.4 collective-permute-done.far0
  22.5 0.0 collective-permute-done.1.far1
  22.5 1.0 %second_states.1 = (f32[384,256]{1,0:T(8,128)S(1)}, f32[384,256]{1,0:T(8,128)S(1)}, f32[392,128]{1,0:T(8,128)S(1)}, f32[392,128]{1,0:T(8,128)S(1)}) custom-call(f32[1,6,6]{2,1,0:T(8,128)S(1)} %copy.6.f_ref, f32[6,64,256]{2,1,0:T(8,128)S(1)} %collective-permute-done.far0, f32[6,64,256]{2,1,0:T(8,128)S(1)} %collective-permute-done.1.far1, ...), custom_call_target="tpu_custom_call" | custom-call | tf_op jit(solution)/shard_map/second_states/pallas_call | solution.py:228
  23.5 3.7 %collective-permute-start.9 = (f32[392,128]{1,0:T(8,128)S(1)}, f32[392,128]{1,0:T(8,128)S(1)}, u32[]{:S(2)}, u32[]{:S(2)}) collective-permute-start(f32[392,128]{1,0:T(8,128)S(1)} %get-tuple-element.37), channel_id=1, source_target_pairs={{0,1},{1,0},{2,3},{3,2},{4,5},{5,4},{6,7},{7,6},{8,9},{9,8},{10,11... | collective-permute-start | bytes 602120 | tf_op jit(solution)/shard_map/ppermute | solution.py:348
  27.2 0.2 collective-permute-start.10
  27.4 4.0 %collective-permute-start.6 = (f32[8,128]{1,0:T(8,128)S(1)}, f32[8,128]{1,0:T(8,128)S(1)}, u32[]{:S(2)}, u32[]{:S(2)}) collective-permute-start(f32[8,128]{1,0:T(8,128)S(1)} %add.7.after.sums_ref.refs_0_), channel_id=1, source_target_pairs={{0,9},{1,8},{2,11},{3,10},{4,13},{5,12},{6,15},{7,14},{8,1},{9,0},... | collective-permute-start | bytes 12296 | tf_op jit(solution)/shard_map/ppermute | solution.py:356
  31.5 0.0 collective-permute-done.7.refs_3_
  31.5 0.0 collective-permute-start.5
  31.5 1.4 %last_sweep.1.sens_ref = f32[4,256]{1,0:T(4,128)S(1)} custom-call(f32[1,4,4,64,256]{4,3,2,1,0:T(8,128)S(1)} %copy-done, f32[6,2,64,256]{3,2,1,0:T(8,128)S(1)} %get-tuple-element.23.inner_ref, f32[384,256]{1,0:T(8,128)S(1)} %get-tuple-element.28.whole0, f32[384,256]{1,0:T(8,128)S(1)} %get-tuple-element.29.whole1, ...), custom_call_target="tpu_custom_call" | custom-call | flops 1100000000 | tf_op jit(solution)/shard_map/last_sweep/pallas_call | solution.py:261
  32.9 0.2 collective-permute-done.6.refs_2_
  33.0 3.2 %collective-permute-done.5.refs_1_ = f32[8,128]{1,0:T(8,128)S(1)} collective-permute-done((f32[8,128]{1,0:T(8,128)S(1)}, f32[8,128]{1,0:T(8,128)S(1)}, u32[]{:S(2)}, u32[]{:S(2)}) %collective-permute-start.5) | collective-permute-done | bytes 4128 | tf_op jit(solution)/shard_map/ppermute | solution.py:356
  36.3 0.1 node_terms.1
  36.4 0.1 collective-permute-start.8
  36.5 1.2 %collective-permute-done.8.refs_1_ = f32[16,128]{1,0:T(8,128)S(1)} collective-permute-done((f32[16,128]{1,0:T(8,128)S(1)}, f32[16,128]{1,0:T(8,128)S(1)}, u32[]{:S(2)}, u32[]{:S(2)}) %collective-permute-start.8) | collective-permute-done | bytes 8224 | tf_op jit(solution)/shard_map/ppermute | solution.py:360
  37.6 2.7 %collective-permute-done.9.refs_4_ = f32[392,128]{1,0:T(8,128)S(1)} collective-permute-done((f32[392,128]{1,0:T(8,128)S(1)}, f32[392,128]{1,0:T(8,128)S(1)}, u32[]{:S(2)}, u32[]{:S(2)}) %collective-permute-start.9) | collective-permute-done | bytes 200736 | tf_op jit(solution)/shard_map/ppermute | solution.py:348
  40.3 2.3 %collective-permute-done.10.refs_5_ = f32[392,128]{1,0:T(8,128)S(1)} collective-permute-done((f32[392,128]{1,0:T(8,128)S(1)}, f32[392,128]{1,0:T(8,128)S(1)}, u32[]{:S(2)}, u32[]{:S(2)}) %collective-permute-start.10) | collective-permute-done | bytes 200736 | tf_op jit(solution)/shard_map/ppermute | solution.py:350
  42.5 0.7 %gradient.1 = f32[4,128]{1,0:T(4,128)} custom-call(f32[16,128]{1,0:T(8,128)S(1)} %get-tuple-element.34.refs_0_, f32[16,128]{1,0:T(8,128)S(1)} %collective-permute-done.8.refs_1_, f32[384,128]{1,0:T(8,128)S(1)} %get-tuple-element.36.refs_2_, f32[384,128]{1,0:T(8,128)S(1)} %collective-permute-done.7.refs_3_, f32[392,128]{1,0:T(8,128)S(1)} %collective-permute-done.9.refs_4_, ...), custom_call_target="tpu_custom_call" | custom-call | tf_op jit(solution)/shard_map/gradient/pallas_call | solution.py:332
  (13 shorter events, 0.0 us)
Async XLA Ops:
  0.0 8.9 %copy-start = (f32[1,4,4,64,256]{4,3,2,1,0:T(8,128)S(1)}, f32[1,4,4,64,256]{4,3,2,1,0:T(8,128)}, u32[]{:S(2)}) copy-start(f32[1,4,4,64,256]{4,3,2,1,0:T(8,128)} %c_ref.9) | copy-start | bytes 3145732
  0.0 8.9 %copy-start.5 = (f32[1,6,6]{2,0,1:T(1,128)S(1)}, f32[1,6,6]{2,0,1:T(1,128)}, u32[]{:S(2)}) copy-start(f32[1,6,6]{2,0,1:T(1,128)} %param.7) | copy-start | bytes 436
  2.4 20.1 %collective-permute-start = (f32[6,64,256]{2,1,0:T(8,128)}, f32[6,64,256]{2,1,0:T(8,128)S(1)}, u32[]{:S(2)}, u32[]{:S(2)}) collective-permute-start(f32[6,64,256]{2,1,0:T(8,128)} %get-tuple-element.24), channel_id=1, source_target_pairs={{0,1},{1,0},{2,3},{3,2},{4,5},{5,4},{6,7},{7,6},{8,9},{9,8},{10,11... | collective-permute-start | bytes 1179656 | tf_op jit(solution)/shard_map/ppermute | solution.py:348
  5.4 17.1 %collective-permute-start.1 = (f32[6,64,256]{2,1,0:T(8,128)}, f32[6,64,256]{2,1,0:T(8,128)S(1)}, u32[]{:S(2)}, u32[]{:S(2)}) collective-permute-start(f32[6,64,256]{2,1,0:T(8,128)} %get-tuple-element.25), channel_id=1, source_target_pairs={{1,2},{2,1},{3,4},{4,3},{5,6},{6,5},{7,8},{8,7},{9,10},{10,9},{11,... | collective-permute-start | bytes 1179656 | tf_op jit(solution)/shard_map/ppermute | solution.py:348
  6.1 9.2 %collective-permute-start.2 = (f32[8,128]{1,0:T(8,128)}, f32[8,128]{1,0:T(8,128)S(1)}, u32[]{:S(2)}, u32[]{:S(2)}) collective-permute-start(f32[8,128]{1,0:T(8,128)} %get-tuple-element.22.after), channel_id=1, source_target_pairs={{0,2},{1,3},{2,0},{3,1},{4,6},{5,7},{6,4},{7,5},{8,10},{9,11},{10,... | collective-permute-start | bytes 12296 | tf_op jit(solution)/shard_map/ppermute | solution.py:356
  8.9 1.4 %copy-start.1 = (f32[1,6,4,64,256]{4,3,2,1,0:T(8,128)S(1)}, f32[1,6,4,64,256]{4,3,2,1,0:T(8,128)}, u32[]{:S(2)}) copy-start(f32[1,6,4,64,256]{4,3,2,1,0:T(8,128)} %s_ref.7) | copy-start | bytes 4718596
  10.3 1.4 %copy-start.2 = (f32[1,6,4,64,256]{4,3,2,1,0:T(8,128)S(1)}, f32[1,6,4,64,256]{4,3,2,1,0:T(8,128)}, u32[]{:S(2)}) copy-start(f32[1,6,4,64,256]{4,3,2,1,0:T(8,128)} %m_ref.1) | copy-start | bytes 4718596
  11.7 0.7 %copy-start.3 = (f32[8,128]{1,0:T(8,128)S(1)}, f32[8,128]{1,0:T(8,128)}, u32[]{:S(2)}) copy-start(f32[8,128]{1,0:T(8,128)} %get-tuple-element.22.after) | copy-start | bytes 12292
  12.4 2.9 %copy-start.4 = (f32[8,128]{1,0:T(8,128)S(1)}, f32[8,128]{1,0:T(8,128)}, u32[]{:S(2)}) copy-start(f32[8,128]{1,0:T(8,128)} %get-tuple-element.22.after) | copy-start | bytes 12292
  15.3 3.9 %collective-permute-start.3 = (f32[8,128]{1,0:T(8,128)S(1)}, f32[8,128]{1,0:T(8,128)S(1)}, u32[]{:S(2)}, u32[]{:S(2)}) collective-permute-start(f32[8,128]{1,0:T(8,128)S(1)} %add.6.after), channel_id=1, source_target_pairs={{0,4},{1,5},{2,6},{3,7},{4,0},{5,1},{6,2},{7,3},{8,12},{9,13},{10,... | collective-permute-start | bytes 12296 | tf_op jit(solution)/shard_map/ppermute | solution.py:356
  20.2 16.0 %collective-permute-start.4 = (f32[448,256]{1,0:T(8,128)S(1)}, f32[448,256]{1,0:T(8,128)S(1)}, u32[]{:S(2)}, u32[]{:S(2)}) collective-permute-start(f32[448,256]{1,0:T(8,128)S(1)} %edge_second1.1.state1), channel_id=1, source_target_pairs={{1,2},{2,1},{3,4},{4,3},{5,6},{6,5},{7,8},{8,7},{9,10},{10,9},{11,... | collective-permute-start | bytes 1376264 | tf_op jit(solution)/shard_map/ppermute | solution.py:348
  20.9 10.5 %collective-permute-start.7 = (f32[384,128]{1,0:T(8,128)S(1)}, f32[384,128]{1,0:T(8,128)S(1)}, u32[]{:S(2)}, u32[]{:S(2)}) collective-permute-start(f32[384,128]{1,0:T(8,128)S(1)} %get-tuple-element.33), channel_id=1, source_target_pairs={{0,16},{16,0},{1,17},{17,1},{2,18},{18,2},{3,19},{19,3},{4,20},{20... | collective-permute-start | bytes 589832 | tf_op jit(solution)/shard_map/ppermute | solution.py:360
  23.5 16.8 %collective-permute-start.9 = (f32[392,128]{1,0:T(8,128)S(1)}, f32[392,128]{1,0:T(8,128)S(1)}, u32[]{:S(2)}, u32[]{:S(2)}) collective-permute-start(f32[392,128]{1,0:T(8,128)S(1)} %get-tuple-element.37), channel_id=1, source_target_pairs={{0,1},{1,0},{2,3},{3,2},{4,5},{5,4},{6,7},{7,6},{8,9},{9,8},{10,11... | collective-permute-start | bytes 602120 | tf_op jit(solution)/shard_map/ppermute | solution.py:348
  27.2 15.3 %collective-permute-start.10 = (f32[392,128]{1,0:T(8,128)S(1)}, f32[392,128]{1,0:T(8,128)S(1)}, u32[]{:S(2)}, u32[]{:S(2)}) collective-permute-start(f32[392,128]{1,0:T(8,128)S(1)} %get-tuple-element.38), channel_id=1, source_target_pairs={{0,17},{1,16},{2,19},{3,18},{4,21},{5,20},{6,23},{7,22},{8,25},{9,... | collective-permute-start | bytes 602120 | tf_op jit(solution)/shard_map/ppermute | solution.py:350
  27.4 5.6 %collective-permute-start.6 = (f32[8,128]{1,0:T(8,128)S(1)}, f32[8,128]{1,0:T(8,128)S(1)}, u32[]{:S(2)}, u32[]{:S(2)}) collective-permute-start(f32[8,128]{1,0:T(8,128)S(1)} %add.7.after.sums_ref.refs_0_), channel_id=1, source_target_pairs={{0,9},{1,8},{2,11},{3,10},{4,13},{5,12},{6,15},{7,14},{8,1},{9,0},... | collective-permute-start | bytes 12296 | tf_op jit(solution)/shard_map/ppermute | solution.py:356
  31.5 4.8 %collective-permute-start.5 = (f32[8,128]{1,0:T(8,128)S(1)}, f32[8,128]{1,0:T(8,128)S(1)}, u32[]{:S(2)}, u32[]{:S(2)}) collective-permute-start(f32[8,128]{1,0:T(8,128)S(1)} %add.7.after.sums_ref.refs_0_), channel_id=1, source_target_pairs={{0,8},{1,9},{2,10},{3,11},{4,12},{5,13},{6,14},{7,15},{8,0},{9,1},... | collective-permute-start | bytes 12296 | tf_op jit(solution)/shard_map/ppermute | solution.py:356
  36.4 1.2 %collective-permute-start.8 = (f32[16,128]{1,0:T(8,128)S(1)}, f32[16,128]{1,0:T(8,128)S(1)}, u32[]{:S(2)}, u32[]{:S(2)}) collective-permute-start(f32[16,128]{1,0:T(8,128)S(1)} %get-tuple-element.35), channel_id=1, source_target_pairs={{0,16},{16,0},{1,17},{17,1},{2,18},{18,2},{3,19},{19,3},{4,20},{20... | collective-permute-start | bytes 24584 | tf_op jit(solution)/shard_map/ppermute | solution.py:360

commit v5 on v4

--- a/solution.py
+++ b/solution.py
@@ -144,9 +144,8 @@
     )(block, source, coef, after)
 
 
-def first_kernel(parts, f_ref, s_ref, c_ref, m_ref, after, p1_ref, b_ref, sens_ref, weight_ref, *refs):
+def first_kernel(f_ref, s_ref, c_ref, m_ref, after, p1_ref, b_ref, sens_ref, p0, q_ref, inv_ref):
     del after
-    shares, (p0, q_ref, inv_ref) = refs[:parts], refs[parts:]
     nv, nx, ny, nz = s_ref.shape[1:]
 
     def start(x, _):
@@ -177,36 +176,50 @@
 
     lax.fori_loop(1, nx - 1, first, 0)
 
-    for slot in (0, 1):
-        edge = edge_of(slot, nx)
-        total = jnp.zeros((ny, nz), jnp.float32)
-        for w in range(nv):
-            weight = c_ref[0, 1, edge] * b_ref[w, edge]
-            weight_ref[pl.ds((slot * nv + w) * ny, ny), :] = weight
-            if slot == 1:
-                total = total + weight * mixed(f_ref, w, lambda v: p0[v, edge])
-    weight_ref[pl.ds(2 * nv * ny, ny), :] = total
-    for part, out in enumerate(shares):
-        out[...] = share(weight_ref, parts, 0, nv * ny, part)
-
-
-def first_sweep(parts, block, source, coef, metric, after):
+
+def first_sweep(block, source, coef, metric, after):
     nv, nx, ny, nz = source.shape[1:]
     assert 2 < nx <= ROWS
-    rows = (2 * nv + 1) * ny
-    return call(
-        functools.partial(first_kernel, parts),
+    return call(
+        first_kernel,
         "first_sweep",
-        out_shape=(f32(nv, nx - 2, ny, nz), f32(nv, nx, ny, nz), f32(nx, nz), f32(rows, nz))
-        + (f32(nv * ny, nz // parts),) * parts,
+        out_shape=(f32(nv, nx - 2, ny, nz), f32(nv, nx, ny, nz), f32(nx, nz)),
         in_specs=[SMEM] + [VMEM] * 3 + [ANY],
-        out_specs=(VMEM,) * (4 + parts),
+        out_specs=(VMEM,) * 3,
         scratch_shapes=[
             pltpu.VMEM((nv, nx, ny, nz), jnp.float32),
             pltpu.VMEM((nv, ny, nz), jnp.float32),
             pltpu.VMEM((nx, ny, nz), jnp.float32),
         ],
     )(block, source, coef, metric, after)
+
+
+def weights_kernel(parts, f_ref, c_ref, b_ref, own_ref, after, weight_ref, *shares):
+    del after
+    nv, nx, ny, nz = b_ref.shape
+    total = jnp.zeros((ny, nz), jnp.float32)
+    for slot in (0, 1):
+        edge = edge_of(slot, nx)
+        for w in range(nv):
+            weight = c_ref[0, 1, edge] * b_ref[w, edge]
+            weight_ref[pl.ds((slot * nv + w) * ny, ny), :] = weight
+            if slot == 1:
+                total = total + weight * mixed(f_ref, w, lambda v: own_ref[v])
+    weight_ref[pl.ds(2 * nv * ny, ny), :] = total
+    for part, out in enumerate(shares):
+        out[...] = share(weight_ref, parts, 0, nv * ny, part)
+
+
+def edge_weights(parts, block, coef, b, own, after):
+    nv, nx, ny, nz = b.shape
+    rows = (2 * nv + 1) * ny
+    return call(
+        functools.partial(weights_kernel, parts),
+        "edge_weights",
+        out_shape=(f32(rows, nz),) + (f32(nv * ny, nz // parts),) * parts,
+        in_specs=[SMEM] + [VMEM] * 3 + [ANY],
+        out_specs=(VMEM,) * (1 + parts),
+    )(block, coef, b, own, after)
 
 
 def second_kernel(parts, f_ref, far0, far1, state0, state1, sums_ref, whole0, whole1, *msgs):
@@ -372,7 +385,7 @@
     assert slabs & (slabs - 1) == 0 and slabs > 4
     *own, sums = edge_state(source, coef, wall)
     far = [swap_pairs(value, slot) for slot, value in enumerate(own)]
-    inner, b, base, weight, *weights = first_sweep(parts, block, source, coef, metric, sums)
+    inner, b, base = first_sweep(block, source, coef, metric, sums)
     first, *bits = [1 << k for k in range(1, slabs.bit_length() - 1)]
     sums = after(sums + from_partner(sums, first), base)
     states = [edge_second(0, block, source, coef, sums)]
@@ -380,12 +393,13 @@
         sums = sums + from_partner(sums, slab)
     if parts == 1:
         sums = lax.psum(sums, "node")
-    states.append(edge_second(1, block, source, coef, sums))
+    states.append(edge_second(1, block, source, coef, after(sums, states[0])))
     odd = swap_pairs(states[1], 1)
     edges = second_states(parts, block, far, states, sums)
     evens = [swap_pairs(value, 0, part) for part, value in enumerate(edges[2:])]
     sums = after(sums, edges[0])
     sums = [sums] + [from_partner(sums, bits[-1] ^ k) for k in (0, 1)]
+    weight, *weights = edge_weights(parts, block, coef, b, own[1], states[1])
     weights[1:] = [other_core(value) for value in weights[1:]]
     sens = last_sweep(coef, inner, edges[:2], b, base)
     terms = list(node_terms(parts, sens, weight, odd, sums, weights[-1]))

time: 43.5 us -> 43.1 us (level)
  Pallas kernels: 10.6 us -> 11.1 us
  starting transfers between devices: 17.4 us -> 16.9 us
    pallas_call x1 -> x2, Pallas kernels: 2.85 us -> 3.44 us  [the longest x1 2.53 us: first_sweep(): call(first_kernel, 'first_sweep', out_shape=(f32(nv, nx - 2, ny, nz), f32...]
    ppermute x4, waiting for transfers between devices: 5.15 us -> 4.56 us  [from_partner(): return lax.ppermute(value, ('node', 'slab'), pairs)]
  transfers between devices with their start and end apart: 11 -> 11, of which waited for: 7 -> 7; matrix products, arithmetic and copies ran while one was open for 0% -> 0% of each run, Pallas kernels for 17% -> 19%
where the time goes in v5:
time: 43.1 us; the launch traced here: 42.9 us
  starting transfers between devices  16.9 us (39%)
  waiting for transfers between devices  11.2 us (26%)
  Pallas kernels  11.1 us (26%)
  local copies, waits for them, and re-layouts  3.5 us (8%)
    ppermute x4, starting transfers between devices, from_partner(): return lax.ppermute(value, ('node', 'slab'), pairs)  8.96 us
    ppermute x4, starting transfers between devices, swap_pairs(): return lax.ppermute(value, 'slab', pairs)  7.78 us
    ppermute x4, waiting for transfers between devices, from_partner(): return lax.ppermute(value, ('node', 'slab'), pairs)  4.56 us
    unnamed x13, local copies, waits for them, and re-layouts  3.5 us
    ppermute x4, waiting for transfers between devices, swap_pairs(): return lax.ppermute(value, 'slab', pairs)  3.27 us
    pallas_call x1, Pallas kernels, first_sweep(): call(first_kernel, 'first_sweep', out_shape=(f32(nv, nx - 2, ny, nz), f32...  2.53 us
    pallas_call x1, Pallas kernels, edge_state(): call(edge_kernel, 'edge_state', out_shape=(f32(nv, ny, nz),) * 2 + (f32(R...  2.34 us
    ppermute x1, waiting for transfers between devices, swap_pairs(): return lax.ppermute(value, ('node', 'slab'), cross)  2.25 us
  transfers between devices with their start and end apart: 11, of which 7 were waited for; matrix products, arithmetic and copies ran while one was open for 0% of the time, Pallas kernels for 19%

profile of v5, /device:TPU:0, one launch (start us, length us, event | category | flops | bytes accessed | tf_op | source)
XLA Modules:
  0.0 42.9 jit_solution(13259710460720516835)
XLA Ops:
  0.0 2.3 %edge_state.1 = (f32[6,64,256]{2,1,0:T(8,128)}, f32[6,64,256]{2,1,0:T(8,128)}, f32[8,128]{1,0:T(8,128)}) custom-call(f32[1,6,4,64,256]{4,3,2,1,0:T(8,128)} %s_ref.7, f32[1,4,4,64,256]{4,3,2,1,0:T(8,128)} %c_ref.11, f32[1,4,256]{2,1,0:T(4,128)} %wall_ref.1), custom_call_target="tpu_custom_call" | custom-call | tf_op jit(solution)/shard_map/edge_state/pallas_call | solution.py:79
  2.4 3.0 %collective-permute-start = (f32[6,64,256]{2,1,0:T(8,128)}, f32[6,64,256]{2,1,0:T(8,128)S(1)}, u32[]{:S(2)}, u32[]{:S(2)}) collective-permute-start(f32[6,64,256]{2,1,0:T(8,128)} %get-tuple-element.25), channel_id=1, source_target_pairs={{0,1},{1,0},{2,3},{3,2},{4,5},{5,4},{6,7},{7,6},{8,9},{9,8},{10,11... | collective-permute-start | bytes 1179656 | tf_op jit(solution)/shard_map/ppermute | solution.py:361
  5.4 0.7 %collective-permute-start.1 = (f32[6,64,256]{2,1,0:T(8,128)}, f32[6,64,256]{2,1,0:T(8,128)S(1)}, u32[]{:S(2)}, u32[]{:S(2)}) collective-permute-start(f32[6,64,256]{2,1,0:T(8,128)} %get-tuple-element.26.own_ref), channel_id=1, source_target_pairs={{1,2},{2,1},{3,4},{4,3},{5,6},{6,5},{7,8},{8,7},{9,10},{10,9},{11,... | collective-permute-start | bytes 1179656 | tf_op jit(solution)/shard_map/ppermute | solution.py:361
  6.0 2.8 %collective-permute-start.2 = (f32[8,128]{1,0:T(8,128)}, f32[8,128]{1,0:T(8,128)S(1)}, u32[]{:S(2)}, u32[]{:S(2)}) collective-permute-start(f32[8,128]{1,0:T(8,128)} %get-tuple-element.23.after), channel_id=1, source_target_pairs={{0,2},{1,3},{2,0},{3,1},{4,6},{5,7},{6,4},{7,5},{8,10},{9,11},{10,... | collective-permute-start | bytes 12296 | tf_op jit(solution)/shard_map/ppermute | solution.py:369
  8.9 1.4 %copy-done.1 = f32[1,6,4,64,256]{4,3,2,1,0:T(8,128)S(1)} copy-done((f32[1,6,4,64,256]{4,3,2,1,0:T(8,128)S(1)}, f32[1,6,4,64,256]{4,3,2,1,0:T(8,128)}, u32[]{:S(2)}) %copy-start.1) | copy-done | bytes 1572888
  10.3 1.4 %copy-done.2 = f32[1,6,4,64,256]{4,3,2,1,0:T(8,128)S(1)} copy-done((f32[1,6,4,64,256]{4,3,2,1,0:T(8,128)S(1)}, f32[1,6,4,64,256]{4,3,2,1,0:T(8,128)}, u32[]{:S(2)}) %copy-start.2) | copy-done | bytes 1572888
  11.7 0.7 %copy-done.4 = f32[8,128]{1,0:T(8,128)S(1)} copy-done((f32[8,128]{1,0:T(8,128)S(1)}, f32[8,128]{1,0:T(8,128)}, u32[]{:S(2)}) %copy-start.4) | copy-done | bytes 4120
  12.4 2.5 %first_sweep.1 = (f32[6,2,64,256]{3,2,1,0:T(8,128)S(1)}, f32[6,4,64,256]{3,2,1,0:T(8,128)S(1)}, f32[4,256]{1,0:T(4,128)S(1)}) custom-call(f32[1,6,6]{2,1,0:T(8,128)S(1)} %copy.6.f_ref, f32[1,6,4,64,256]{4,3,2,1,0:T(8,128)S(1)} %copy-done.1, f32[1,4,4,64,256]{4,3,2,1,0:T(8,128)S(1)} %copy-done, f32[1,6,4,64,256]{4,3,2,1,0:T(8,128)S(1)} %copy-done.2, ...), custom_call_target="tpu_custom_call" | custom-call | tf_op jit(solution)/shard_map/first_sweep/pallas_call | solution.py:183
  14.9 0.0 collective-permute-done.2
  14.9 2.1 %collective-permute-start.3 = (f32[8,128]{1,0:T(8,128)S(1)}, f32[8,128]{1,0:T(8,128)S(1)}, u32[]{:S(2)}, u32[]{:S(2)}) collective-permute-start(f32[8,128]{1,0:T(8,128)S(1)} %add.6.after), channel_id=1, source_target_pairs={{0,4},{1,5},{2,6},{3,7},{4,0},{5,1},{6,2},{7,3},{8,12},{9,13},{10,... | collective-permute-start | bytes 12296 | tf_op jit(solution)/shard_map/ppermute | solution.py:369
  17.0 1.1 %edge_second0.1.state0 = f32[448,256]{1,0:T(8,128)S(1)} custom-call(f32[1,6,6]{2,1,0:T(8,128)S(1)} %copy.6.f_ref, f32[1,6,4,64,256]{4,3,2,1,0:T(8,128)S(1)} %copy-done.1, f32[1,4,4,64,256]{4,3,2,1,0:T(8,128)S(1)} %copy-done, f32[8,128]{1,0:T(8,128)S(1)} %add.6.after), custom_call_target="tpu_custom_call" | custom-call | tf_op jit(solution)/shard_map/edge_second0/pallas_call | solution.py:137
  18.1 1.0 %collective-permute-done.3 = f32[8,128]{1,0:T(8,128)S(1)} collective-permute-done((f32[8,128]{1,0:T(8,128)S(1)}, f32[8,128]{1,0:T(8,128)S(1)}, u32[]{:S(2)}, u32[]{:S(2)}) %collective-permute-start.3) | collective-permute-done | bytes 4128 | tf_op jit(solution)/shard_map/ppermute | solution.py:369
  19.1 1.1 %edge_second1.1.state1.after = f32[448,256]{1,0:T(8,128)S(1)} custom-call(f32[1,6,6]{2,1,0:T(8,128)S(1)} %copy.6.f_ref, f32[1,6,4,64,256]{4,3,2,1,0:T(8,128)S(1)} %copy-done.1, f32[1,4,4,64,256]{4,3,2,1,0:T(8,128)S(1)} %copy-done, f32[8,128]{1,0:T(8,128)S(1)} %add.7.after.sums_ref.refs_0_), custom_call_target="tpu_custom_call" | custom-call | tf_op jit(solution)/shard_map/edge_second1/pallas_call | solution.py:137
  20.2 0.7 %collective-permute-start.4 = (f32[448,256]{1,0:T(8,128)S(1)}, f32[448,256]{1,0:T(8,128)S(1)}, u32[]{:S(2)}, u32[]{:S(2)}) collective-permute-start(f32[448,256]{1,0:T(8,128)S(1)} %edge_second1.1.state1.after), channel_id=1, source_target_pairs={{1,2},{2,1},{3,4},{4,3},{5,6},{6,5},{7,8},{8,7},{9,10},{10,9},{11,... | collective-permute-start | bytes 1376264 | tf_op jit(solution)/shard_map/ppermute | solution.py:361
  20.9 0.9 %edge_weights.1 = (f32[832,256]{1,0:T(8,128)S(1)}, f32[384,128]{1,0:T(8,128)S(1)}, f32[384,128]{1,0:T(8,128)S(1)}) custom-call(f32[1,6,6]{2,1,0:T(8,128)S(1)} %copy.6.f_ref, f32[1,4,4,64,256]{4,3,2,1,0:T(8,128)S(1)} %copy-done, f32[6,4,64,256]{3,2,1,0:T(8,128)S(1)} %get-tuple-element.32.b_ref, f32[6,64,256]{2,1,0:T(8,128)S(1)} %copy-done.3, ...), custom_call_target="tpu_custom_call" | custom-call | tf_op jit(solution)/shard_map/edge_weights/pallas_call | solution.py:216
  21.8 0.1 collective-permute-start.7
  21.9 0.6 %collective-permute-done.far0 = f32[6,64,256]{2,1,0:T(8,128)S(1)} collective-permute-done((f32[6,64,256]{2,1,0:T(8,128)}, f32[6,64,256]{2,1,0:T(8,128)S(1)}, u32[]{:S(2)}, u32[]{:S(2)}) %collective-permute-start) | collective-permute-done | bytes 393248 | tf_op jit(solution)/shard_map/ppermute | solution.py:361
  22.5 0.0 collective-permute-done.1.far1
  22.5 1.0 %second_states.1 = (f32[384,256]{1,0:T(8,128)S(1)}, f32[384,256]{1,0:T(8,128)S(1)}, f32[392,128]{1,0:T(8,128)S(1)}, f32[392,128]{1,0:T(8,128)S(1)}) custom-call(f32[1,6,6]{2,1,0:T(8,128)S(1)} %copy.6.f_ref, f32[6,64,256]{2,1,0:T(8,128)S(1)} %collective-permute-done.far0, f32[6,64,256]{2,1,0:T(8,128)S(1)} %collective-permute-done.1.far1, ...), custom_call_target="tpu_custom_call" | custom-call | tf_op jit(solution)/shard_map/second_states/pallas_call | solution.py:241
  23.5 3.4 %collective-permute-start.9 = (f32[392,128]{1,0:T(8,128)S(1)}, f32[392,128]{1,0:T(8,128)S(1)}, u32[]{:S(2)}, u32[]{:S(2)}) collective-permute-start(f32[392,128]{1,0:T(8,128)S(1)} %get-tuple-element.39), channel_id=1, source_target_pairs={{0,1},{1,0},{2,3},{3,2},{4,5},{5,4},{6,7},{7,6},{8,9},{9,8},{10,11... | collective-permute-start | bytes 602120 | tf_op jit(solution)/shard_map/ppermute | solution.py:361
  26.9 4.0 %collective-permute-start.6 = (f32[8,128]{1,0:T(8,128)S(1)}, f32[8,128]{1,0:T(8,128)S(1)}, u32[]{:S(2)}, u32[]{:S(2)}) collective-permute-start(f32[8,128]{1,0:T(8,128)S(1)} %add.7.after.sums_ref.refs_0_), channel_id=1, source_target_pairs={{0,9},{1,8},{2,11},{3,10},{4,13},{5,12},{6,15},{7,14},{8,1},{9,0},... | collective-permute-start | bytes 12296 | tf_op jit(solution)/shard_map/ppermute | solution.py:369
  30.9 0.0 collective-permute-start.5
  30.9 1.4 %last_sweep.1.sens_ref = f32[4,256]{1,0:T(4,128)S(1)} custom-call(f32[1,4,4,64,256]{4,3,2,1,0:T(8,128)S(1)} %copy-done, f32[6,2,64,256]{3,2,1,0:T(8,128)S(1)} %get-tuple-element.24.inner_ref, f32[384,256]{1,0:T(8,128)S(1)} %get-tuple-element.30.whole0, f32[384,256]{1,0:T(8,128)S(1)} %get-tuple-element.31.whole1, ...), custom_call_target="tpu_custom_call" | custom-call | flops 1100000000 | tf_op jit(solution)/shard_map/last_sweep/pallas_call | solution.py:274
  32.3 0.2 collective-permute-done.6.refs_2_
  32.5 3.4 %collective-permute-done.5.refs_1_ = f32[8,128]{1,0:T(8,128)S(1)} collective-permute-done((f32[8,128]{1,0:T(8,128)S(1)}, f32[8,128]{1,0:T(8,128)S(1)}, u32[]{:S(2)}, u32[]{:S(2)}) %collective-permute-start.5) | collective-permute-done | bytes 4128 | tf_op jit(solution)/shard_map/ppermute | solution.py:369
  35.9 0.0 collective-permute-done.4.odd_ref
  35.9 0.1 node_terms.1
  36.0 0.1 collective-permute-start.8
  36.1 1.2 %collective-permute-done.8.refs_1_ = f32[16,128]{1,0:T(8,128)S(1)} collective-permute-done((f32[16,128]{1,0:T(8,128)S(1)}, f32[16,128]{1,0:T(8,128)S(1)}, u32[]{:S(2)}, u32[]{:S(2)}) %collective-permute-start.8) | collective-permute-done | bytes 8224 | tf_op jit(solution)/shard_map/ppermute | solution.py:373
  37.2 2.7 %collective-permute-done.9.refs_4_ = f32[392,128]{1,0:T(8,128)S(1)} collective-permute-done((f32[392,128]{1,0:T(8,128)S(1)}, f32[392,128]{1,0:T(8,128)S(1)}, u32[]{:S(2)}, u32[]{:S(2)}) %collective-permute-start.9) | collective-permute-done | bytes 200736 | tf_op jit(solution)/shard_map/ppermute | solution.py:361
  39.9 2.3 %collective-permute-done.10.refs_5_ = f32[392,128]{1,0:T(8,128)S(1)} collective-permute-done((f32[392,128]{1,0:T(8,128)S(1)}, f32[392,128]{1,0:T(8,128)S(1)}, u32[]{:S(2)}, u32[]{:S(2)}) %collective-permute-start.10) | collective-permute-done | bytes 200736 | tf_op jit(solution)/shard_map/ppermute | solution.py:363
  42.2 0.7 %gradient.1 = f32[4,128]{1,0:T(4,128)} custom-call(f32[16,128]{1,0:T(8,128)S(1)} %get-tuple-element.36.refs_0_, f32[16,128]{1,0:T(8,128)S(1)} %collective-permute-done.8.refs_1_, f32[384,128]{1,0:T(8,128)S(1)} %get-tuple-element.38.refs_2_, f32[384,128]{1,0:T(8,128)S(1)} %collective-permute-done.7.refs_3_, f32[392,128]{1,0:T(8,128)S(1)} %collective-permute-done.9.refs_4_, ...), custom_call_target="tpu_custom_call" | custom-call | tf_op jit(solution)/shard_map/gradient/pallas_call | solution.py:345
  (14 shorter events, 0.0 us)
Async XLA Ops:
  0.0 8.9 %copy-start = (f32[1,4,4,64,256]{4,3,2,1,0:T(8,128)S(1)}, f32[1,4,4,64,256]{4,3,2,1,0:T(8,128)}, u32[]{:S(2)}) copy-start(f32[1,4,4,64,256]{4,3,2,1,0:T(8,128)} %c_ref.11) | copy-start | bytes 3145732
  0.0 8.9 %copy-start.5 = (f32[1,6,6]{2,0,1:T(1,128)S(1)}, f32[1,6,6]{2,0,1:T(1,128)}, u32[]{:S(2)}) copy-start(f32[1,6,6]{2,0,1:T(1,128)} %param.7) | copy-start | bytes 436
  2.4 20.1 %collective-permute-start = (f32[6,64,256]{2,1,0:T(8,128)}, f32[6,64,256]{2,1,0:T(8,128)S(1)}, u32[]{:S(2)}, u32[]{:S(2)}) collective-permute-start(f32[6,64,256]{2,1,0:T(8,128)} %get-tuple-element.25), channel_id=1, source_target_pairs={{0,1},{1,0},{2,3},{3,2},{4,5},{5,4},{6,7},{7,6},{8,9},{9,8},{10,11... | collective-permute-start | bytes 1179656 | tf_op jit(solution)/shard_map/ppermute | solution.py:361
  5.4 17.1 %collective-permute-start.1 = (f32[6,64,256]{2,1,0:T(8,128)}, f32[6,64,256]{2,1,0:T(8,128)S(1)}, u32[]{:S(2)}, u32[]{:S(2)}) collective-permute-start(f32[6,64,256]{2,1,0:T(8,128)} %get-tuple-element.26.own_ref), channel_id=1, source_target_pairs={{1,2},{2,1},{3,4},{4,3},{5,6},{6,5},{7,8},{8,7},{9,10},{10,9},{11,... | collective-permute-start | bytes 1179656 | tf_op jit(solution)/shard_map/ppermute | solution.py:361
  6.0 8.9 %collective-permute-start.2 = (f32[8,128]{1,0:T(8,128)}, f32[8,128]{1,0:T(8,128)S(1)}, u32[]{:S(2)}, u32[]{:S(2)}) collective-permute-start(f32[8,128]{1,0:T(8,128)} %get-tuple-element.23.after), channel_id=1, source_target_pairs={{0,2},{1,3},{2,0},{3,1},{4,6},{5,7},{6,4},{7,5},{8,10},{9,11},{10,... | collective-permute-start | bytes 12296 | tf_op jit(solution)/shard_map/ppermute | solution.py:369
  8.9 1.4 %copy-start.1 = (f32[1,6,4,64,256]{4,3,2,1,0:T(8,128)S(1)}, f32[1,6,4,64,256]{4,3,2,1,0:T(8,128)}, u32[]{:S(2)}) copy-start(f32[1,6,4,64,256]{4,3,2,1,0:T(8,128)} %s_ref.7) | copy-start | bytes 4718596
  10.3 1.4 %copy-start.2 = (f32[1,6,4,64,256]{4,3,2,1,0:T(8,128)S(1)}, f32[1,6,4,64,256]{4,3,2,1,0:T(8,128)}, u32[]{:S(2)}) copy-start(f32[1,6,4,64,256]{4,3,2,1,0:T(8,128)} %m_ref.1) | copy-start | bytes 4718596
  11.7 0.7 %copy-start.4 = (f32[8,128]{1,0:T(8,128)S(1)}, f32[8,128]{1,0:T(8,128)}, u32[]{:S(2)}) copy-start(f32[8,128]{1,0:T(8,128)} %get-tuple-element.23.after) | copy-start | bytes 12292
  14.9 4.2 %collective-permute-start.3 = (f32[8,128]{1,0:T(8,128)S(1)}, f32[8,128]{1,0:T(8,128)S(1)}, u32[]{:S(2)}, u32[]{:S(2)}) collective-permute-start(f32[8,128]{1,0:T(8,128)S(1)} %add.6.after), channel_id=1, source_target_pairs={{0,4},{1,5},{2,6},{3,7},{4,0},{5,1},{6,2},{7,3},{8,12},{9,13},{10,... | collective-permute-start | bytes 12296 | tf_op jit(solution)/shard_map/ppermute | solution.py:369
  18.1 2.8 %copy-start.3 = (f32[6,64,256]{2,1,0:T(8,128)S(1)}, f32[6,64,256]{2,1,0:T(8,128)}, u32[]{:S(2)}) copy-start(f32[6,64,256]{2,1,0:T(8,128)} %get-tuple-element.26.own_ref) | copy-start | bytes 1179652
  20.2 15.7 %collective-permute-start.4 = (f32[448,256]{1,0:T(8,128)S(1)}, f32[448,256]{1,0:T(8,128)S(1)}, u32[]{:S(2)}, u32[]{:S(2)}) collective-permute-start(f32[448,256]{1,0:T(8,128)S(1)} %edge_second1.1.state1.after), channel_id=1, source_target_pairs={{1,2},{2,1},{3,4},{4,3},{5,6},{6,5},{7,8},{8,7},{9,10},{10,9},{11,... | collective-permute-start | bytes 1376264 | tf_op jit(solution)/shard_map/ppermute | solution.py:361
  21.8 9.1 %collective-permute-start.7 = (f32[384,128]{1,0:T(8,128)S(1)}, f32[384,128]{1,0:T(8,128)S(1)}, u32[]{:S(2)}, u32[]{:S(2)}) collective-permute-start(f32[384,128]{1,0:T(8,128)S(1)} %get-tuple-element.35), channel_id=1, source_target_pairs={{0,16},{16,0},{1,17},{17,1},{2,18},{18,2},{3,19},{19,3},{4,20},{20... | collective-permute-start | bytes 589832 | tf_op jit(solution)/shard_map/ppermute | solution.py:373
  23.5 16.4 %collective-permute-start.9 = (f32[392,128]{1,0:T(8,128)S(1)}, f32[392,128]{1,0:T(8,128)S(1)}, u32[]{:S(2)}, u32[]{:S(2)}) collective-permute-start(f32[392,128]{1,0:T(8,128)S(1)} %get-tuple-element.39), channel_id=1, source_target_pairs={{0,1},{1,0},{2,3},{3,2},{4,5},{5,4},{6,7},{7,6},{8,9},{9,8},{10,11... | collective-permute-start | bytes 602120 | tf_op jit(solution)/shard_map/ppermute | solution.py:361
  26.9 15.3 %collective-permute-start.10 = (f32[392,128]{1,0:T(8,128)S(1)}, f32[392,128]{1,0:T(8,128)S(1)}, u32[]{:S(2)}, u32[]{:S(2)}) collective-permute-start(f32[392,128]{1,0:T(8,128)S(1)} %get-tuple-element.40), channel_id=1, source_target_pairs={{0,17},{1,16},{2,19},{3,18},{4,21},{5,20},{6,23},{7,22},{8,25},{9,... | collective-permute-start | bytes 602120 | tf_op jit(solution)/shard_map/ppermute | solution.py:363
  26.9 5.6 %collective-permute-start.6 = (f32[8,128]{1,0:T(8,128)S(1)}, f32[8,128]{1,0:T(8,128)S(1)}, u32[]{:S(2)}, u32[]{:S(2)}) collective-permute-start(f32[8,128]{1,0:T(8,128)S(1)} %add.7.after.sums_ref.refs_0_), channel_id=1, source_target_pairs={{0,9},{1,8},{2,11},{3,10},{4,13},{5,12},{6,15},{7,14},{8,1},{9,0},... | collective-permute-start | bytes 12296 | tf_op jit(solution)/shard_map/ppermute | solution.py:369
  30.9 5.0 %collective-permute-start.5 = (f32[8,128]{1,0:T(8,128)S(1)}, f32[8,128]{1,0:T(8,128)S(1)}, u32[]{:S(2)}, u32[]{:S(2)}) collective-permute-start(f32[8,128]{1,0:T(8,128)S(1)} %add.7.after.sums_ref.refs_0_), channel_id=1, source_target_pairs={{0,8},{1,9},{2,10},{3,11},{4,12},{5,13},{6,14},{7,15},{8,0},{9,1},... | collective-permute-start | bytes 12296 | tf_op jit(solution)/shard_map/ppermute | solution.py:369
  36.0 1.2 %collective-permute-start.8 = (f32[16,128]{1,0:T(8,128)S(1)}, f32[16,128]{1,0:T(8,128)S(1)}, u32[]{:S(2)}, u32[]{:S(2)}) collective-permute-start(f32[16,128]{1,0:T(8,128)S(1)} %get-tuple-element.37), channel_id=1, source_target_pairs={{0,16},{16,0},{1,17},{17,1},{2,18},{18,2},{3,19},{19,3},{4,20},{20... | collective-permute-start | bytes 24584 | tf_op jit(solution)/shard_map/ppermute | solution.py:373

commit v6 on v5

--- a/solution.py
+++ b/solution.py
@@ -115,33 +115,61 @@
     return mix
 
 
-def state_kernel(slot, f_ref, s_ref, c_ref, after, out, q_ref, p_ref):
+def state_kernel(f_ref, s_ref, c_ref, after, out, part, q_ref, p_ref):
     del after
     nv, nx, ny, nz = s_ref.shape[1:]
     zero = jnp.zeros((ny, nz), jnp.float32)
-    edge = edge_of(slot, nx)
-    inner = jnp.where(edge == 0, 1, nx - 2)
-    inv = inverse_diag(lambda k: c_ref[0, k, edge])
-    inv_inner = inverse_diag(lambda k: c_ref[0, k, inner])
-    for v in range(nv):
-        p_ref[v] = s_ref[0, v, edge] * inv
-        beside = s_ref[0, v, inner] * inv_inner
-        q_ref[v] = coupled(c_ref, edge, beside, p_ref[v], zero)
-    for w in range(nv):
-        out[pl.ds(w * ny, ny), :] = p_ref[w] + inv * mixed(f_ref, w, lambda v: q_ref[v])
-    out[pl.ds(nv * ny, ny), :] = c_ref[0, 1, edge] * inv
-
-
-def edge_second(slot, block, source, coef, after):
+    for slot in (0, 1):
+        edge = edge_of(slot, nx)
+        inner = jnp.where(edge == 0, 1, nx - 2)
+        inv = inverse_diag(lambda k: c_ref[0, k, edge])
+        inv_inner = inverse_diag(lambda k: c_ref[0, k, inner])
+        for v in range(nv):
+            p = s_ref[0, v, edge] * inv
+            beside = s_ref[0, v, inner] * inv_inner
+            q = coupled(c_ref, edge, beside, p, zero)
+            if slot == 0:
+                p_ref[v], q_ref[v] = p, q
+            else:
+                part[v], part[nv + v] = p, q * inv
+        rho = c_ref[0, 1, edge] * inv
+        if slot == 0:
+            for w in range(nv):
+                out[pl.ds(w * ny, ny), :] = p_ref[w] + inv * mixed(f_ref, w, lambda v: q_ref[v])
+            out[pl.ds(nv * ny, ny), :] = rho
+        else:
+            part[2 * nv] = rho
+
+
+def even_second(block, source, coef, after):
     nv, nx, ny, nz = source.shape[1:]
     return call(
-        functools.partial(state_kernel, slot),
-        f"edge_second{slot}",
-        out_shape=f32((nv + 1) * ny, nz),
+        state_kernel,
+        "even_second",
+        out_shape=(f32((nv + 1) * ny, nz), f32(2 * nv + 1, ny, nz)),
         in_specs=[SMEM] + [VMEM] * 2 + [ANY],
-        out_specs=VMEM,
+        out_specs=(VMEM,) * 2,
         scratch_shapes=[pltpu.VMEM((nv, ny, nz), jnp.float32)] * 2,
     )(block, source, coef, after)
+
+
+def odd_kernel(f_ref, part, after, out):
+    del after
+    nv, ny = f_ref.shape[1], part.shape[1]
+    for w in range(nv):
+        out[pl.ds(w * ny, ny), :] = part[w] + mixed(f_ref, w, lambda v: part[nv + v])
+    out[pl.ds(nv * ny, ny), :] = part[2 * nv]
+
+
+def odd_second(block, part, after):
+    count, ny, nz = part.shape
+    return call(
+        odd_kernel,
+        "odd_second",
+        out_shape=f32((count + 1) // 2 * ny, nz),
+        in_specs=[SMEM, VMEM, ANY],
+        out_specs=VMEM,
+    )(block, part, after)
 
 
 def first_kernel(f_ref, s_ref, c_ref, m_ref, after, p1_ref, b_ref, sens_ref, p0, q_ref, inv_ref):
@@ -388,12 +416,12 @@
     inner, b, base = first_sweep(block, source, coef, metric, sums)
     first, *bits = [1 << k for k in range(1, slabs.bit_length() - 1)]
     sums = after(sums + from_partner(sums, first), base)
-    states = [edge_second(0, block, source, coef, sums)]
+    even, part = even_second(block, source, coef, sums)
     for slab in bits[:-1]:
         sums = sums + from_partner(sums, slab)
     if parts == 1:
         sums = lax.psum(sums, "node")
-    states.append(edge_second(1, block, source, coef, after(sums, states[0])))
+    states = [even, odd_second(block, part, sums)]
     odd = swap_pairs(states[1], 1)
     edges = second_states(parts, block, far, states, sums)
     evens = [swap_pairs(value, 0, part) for part, value in enumerate(edges[2:])]

time: 43.1 us -> 42.8 us (level)
  no operation moved by 1% of the time
where the time goes in v6:
time: 42.8 us; the launch traced here: 42.6 us
  starting transfers between devices  16.6 us (39%)
  waiting for transfers between devices  11.3 us (26%)
  Pallas kernels  11.1 us (26%)
  local copies, waits for them, and re-layouts  3.5 us (8%)
    ppermute x4, starting transfers between devices, from_partner(): return lax.ppermute(value, ('node', 'slab'), pairs)  8.67 us
    ppermute x4, starting transfers between devices, swap_pairs(): return lax.ppermute(value, 'slab', pairs)  7.76 us
    ppermute x4, waiting for transfers between devices, from_partner(): return lax.ppermute(value, ('node', 'slab'), pairs)  4.26 us
    ppermute x4, waiting for transfers between devices, swap_pairs(): return lax.ppermute(value, 'slab', pairs)  3.61 us
    unnamed x13, local copies, waits for them, and re-layouts  3.5 us
    pallas_call x1, Pallas kernels, first_sweep(): call(first_kernel, 'first_sweep', out_shape=(f32(nv, nx - 2, ny, nz), f32...  2.53 us
    pallas_call x1, Pallas kernels, edge_state(): call(edge_kernel, 'edge_state', out_shape=(f32(nv, ny, nz),) * 2 + (f32(R...  2.34 us
    ppermute x1, waiting for transfers between devices, swap_pairs(): return lax.ppermute(value, ('node', 'slab'), cross)  2.22 us
  transfers between devices with their start and end apart: 11, of which 7 were waited for; matrix products, arithmetic and copies ran while one was open for 0% of the time, Pallas kernels for 19%

profile of v6, /device:TPU:0, one launch (start us, length us, event | category | flops | bytes accessed | tf_op | source)
XLA Modules:
  0.0 42.6 jit_solution(16150739646157700952)
XLA Ops:
  0.0 2.3 %edge_state.1 = (f32[6,64,256]{2,1,0:T(8,128)}, f32[6,64,256]{2,1,0:T(8,128)}, f32[8,128]{1,0:T(8,128)}) custom-call(f32[1,6,4,64,256]{4,3,2,1,0:T(8,128)} %s_ref.5, f32[1,4,4,64,256]{4,3,2,1,0:T(8,128)} %c_ref.9, f32[1,4,256]{2,1,0:T(4,128)} %wall_ref.1), custom_call_target="tpu_custom_call" | custom-call | tf_op jit(solution)/shard_map/edge_state/pallas_call | solution.py:79
  2.4 3.0 %collective-permute-start = (f32[6,64,256]{2,1,0:T(8,128)}, f32[6,64,256]{2,1,0:T(8,128)S(1)}, u32[]{:S(2)}, u32[]{:S(2)}) collective-permute-start(f32[6,64,256]{2,1,0:T(8,128)} %get-tuple-element.26), channel_id=1, source_target_pairs={{0,1},{1,0},{2,3},{3,2},{4,5},{5,4},{6,7},{7,6},{8,9},{9,8},{10,11... | collective-permute-start | bytes 1179656 | tf_op jit(solution)/shard_map/ppermute | solution.py:389
  5.4 0.7 %collective-permute-start.1 = (f32[6,64,256]{2,1,0:T(8,128)}, f32[6,64,256]{2,1,0:T(8,128)S(1)}, u32[]{:S(2)}, u32[]{:S(2)}) collective-permute-start(f32[6,64,256]{2,1,0:T(8,128)} %get-tuple-element.27.own_ref), channel_id=1, source_target_pairs={{1,2},{2,1},{3,4},{4,3},{5,6},{6,5},{7,8},{8,7},{9,10},{10,9},{11,... | collective-permute-start | bytes 1179656 | tf_op jit(solution)/shard_map/ppermute | solution.py:389
  6.0 2.8 %collective-permute-start.2 = (f32[8,128]{1,0:T(8,128)}, f32[8,128]{1,0:T(8,128)S(1)}, u32[]{:S(2)}, u32[]{:S(2)}) collective-permute-start(f32[8,128]{1,0:T(8,128)} %get-tuple-element.24.after), channel_id=1, source_target_pairs={{0,2},{1,3},{2,0},{3,1},{4,6},{5,7},{6,4},{7,5},{8,10},{9,11},{10,... | collective-permute-start | bytes 12296 | tf_op jit(solution)/shard_map/ppermute | solution.py:397
  8.9 1.4 %copy-done.1 = f32[1,6,4,64,256]{4,3,2,1,0:T(8,128)S(1)} copy-done((f32[1,6,4,64,256]{4,3,2,1,0:T(8,128)S(1)}, f32[1,6,4,64,256]{4,3,2,1,0:T(8,128)}, u32[]{:S(2)}) %copy-start.1) | copy-done | bytes 1572888
  10.3 1.4 %copy-done.2 = f32[1,6,4,64,256]{4,3,2,1,0:T(8,128)S(1)} copy-done((f32[1,6,4,64,256]{4,3,2,1,0:T(8,128)S(1)}, f32[1,6,4,64,256]{4,3,2,1,0:T(8,128)}, u32[]{:S(2)}) %copy-start.2) | copy-done | bytes 1572888
  11.7 0.7 %copy-done.4 = f32[8,128]{1,0:T(8,128)S(1)} copy-done((f32[8,128]{1,0:T(8,128)S(1)}, f32[8,128]{1,0:T(8,128)}, u32[]{:S(2)}) %copy-start.4) | copy-done | bytes 4120
  12.4 2.5 %first_sweep.1 = (f32[6,2,64,256]{3,2,1,0:T(8,128)S(1)}, f32[6,4,64,256]{3,2,1,0:T(8,128)S(1)}, f32[4,256]{1,0:T(4,128)S(1)}) custom-call(f32[1,6,6]{2,1,0:T(8,128)S(1)} %copy.6.f_ref, f32[1,6,4,64,256]{4,3,2,1,0:T(8,128)S(1)} %copy-done.1, f32[1,4,4,64,256]{4,3,2,1,0:T(8,128)S(1)} %copy-done, f32[1,6,4,64,256]{4,3,2,1,0:T(8,128)S(1)} %copy-done.2, ...), custom_call_target="tpu_custom_call" | custom-call | tf_op jit(solution)/shard_map/first_sweep/pallas_call | solution.py:211
  14.9 0.0 collective-permute-done.2
  14.9 2.1 %collective-permute-start.3 = (f32[8,128]{1,0:T(8,128)S(1)}, f32[8,128]{1,0:T(8,128)S(1)}, u32[]{:S(2)}, u32[]{:S(2)}) collective-permute-start(f32[8,128]{1,0:T(8,128)S(1)} %add.6.after), channel_id=1, source_target_pairs={{0,4},{1,5},{2,6},{3,7},{4,0},{5,1},{6,2},{7,3},{8,12},{9,13},{10,... | collective-permute-start | bytes 12296 | tf_op jit(solution)/shard_map/ppermute | solution.py:397
  17.0 1.4 %even_second.1 = (f32[448,256]{1,0:T(8,128)S(1)}, f32[13,64,256]{2,1,0:T(8,128)S(1)}) custom-call(f32[1,6,6]{2,1,0:T(8,128)S(1)} %copy.6.f_ref, f32[1,6,4,64,256]{4,3,2,1,0:T(8,128)S(1)} %copy-done.1, f32[1,4,4,64,256]{4,3,2,1,0:T(8,128)S(1)} %copy-done, f32[8,128]{1,0:T(8,128)S(1)} %add.6.after), custom_call_target="tpu_custom_call" | custom-call | tf_op jit(solution)/shard_map/even_second/pallas_call | solution.py:146
  18.4 0.7 %collective-permute-done.3 = f32[8,128]{1,0:T(8,128)S(1)} collective-permute-done((f32[8,128]{1,0:T(8,128)S(1)}, f32[8,128]{1,0:T(8,128)S(1)}, u32[]{:S(2)}, u32[]{:S(2)}) %collective-permute-start.3) | collective-permute-done | bytes 4128 | tf_op jit(solution)/shard_map/ppermute | solution.py:397
  19.1 0.8 %odd_second.1.state1.after = f32[448,256]{1,0:T(8,128)S(1)} custom-call(f32[1,6,6]{2,1,0:T(8,128)S(1)} %copy.6.f_ref, f32[13,64,256]{2,1,0:T(8,128)S(1)} %get-tuple-element.31.part, f32[8,128]{1,0:T(8,128)S(1)} %add.7.after.sums_ref.refs_0_), custom_call_target="tpu_custom_call" | custom-call | tf_op jit(solution)/shard_map/odd_second/pallas_call | solution.py:166
  19.9 0.7 %collective-permute-start.4 = (f32[448,256]{1,0:T(8,128)S(1)}, f32[448,256]{1,0:T(8,128)S(1)}, u32[]{:S(2)}, u32[]{:S(2)}) collective-permute-start(f32[448,256]{1,0:T(8,128)S(1)} %odd_second.1.state1.after), channel_id=1, source_target_pairs={{1,2},{2,1},{3,4},{4,3},{5,6},{6,5},{7,8},{8,7},{9,10},{10,9},{11,... | collective-permute-start | bytes 1376264 | tf_op jit(solution)/shard_map/ppermute | solution.py:389
  20.6 0.9 %edge_weights.1 = (f32[832,256]{1,0:T(8,128)S(1)}, f32[384,128]{1,0:T(8,128)S(1)}, f32[384,128]{1,0:T(8,128)S(1)}) custom-call(f32[1,6,6]{2,1,0:T(8,128)S(1)} %copy.6.f_ref, f32[1,4,4,64,256]{4,3,2,1,0:T(8,128)S(1)} %copy-done, f32[6,4,64,256]{3,2,1,0:T(8,128)S(1)} %get-tuple-element.34.b_ref, f32[6,64,256]{2,1,0:T(8,128)S(1)} %copy-done.3, ...), custom_call_target="tpu_custom_call" | custom-call | tf_op jit(solution)/shard_map/edge_weights/pallas_call | solution.py:244
  21.5 0.1 collective-permute-start.7
  21.6 0.9 %collective-permute-done.far0 = f32[6,64,256]{2,1,0:T(8,128)S(1)} collective-permute-done((f32[6,64,256]{2,1,0:T(8,128)}, f32[6,64,256]{2,1,0:T(8,128)S(1)}, u32[]{:S(2)}, u32[]{:S(2)}) %collective-permute-start) | collective-permute-done | bytes 393248 | tf_op jit(solution)/shard_map/ppermute | solution.py:389
  22.5 0.0 collective-permute-done.1.far1
  22.5 1.0 %second_states.1 = (f32[384,256]{1,0:T(8,128)S(1)}, f32[384,256]{1,0:T(8,128)S(1)}, f32[392,128]{1,0:T(8,128)S(1)}, f32[392,128]{1,0:T(8,128)S(1)}) custom-call(f32[1,6,6]{2,1,0:T(8,128)S(1)} %copy.6.f_ref, f32[6,64,256]{2,1,0:T(8,128)S(1)} %collective-permute-done.far0, f32[6,64,256]{2,1,0:T(8,128)S(1)} %collective-permute-done.1.far1, ...), custom_call_target="tpu_custom_call" | custom-call | tf_op jit(solution)/shard_map/second_states/pallas_call | solution.py:269
  23.5 3.4 %collective-permute-start.9 = (f32[392,128]{1,0:T(8,128)S(1)}, f32[392,128]{1,0:T(8,128)S(1)}, u32[]{:S(2)}, u32[]{:S(2)}) collective-permute-start(f32[392,128]{1,0:T(8,128)S(1)} %get-tuple-element.41), channel_id=1, source_target_pairs={{0,1},{1,0},{2,3},{3,2},{4,5},{5,4},{6,7},{7,6},{8,9},{9,8},{10,11... | collective-permute-start | bytes 602120 | tf_op jit(solution)/shard_map/ppermute | solution.py:389
  26.9 0.0 collective-permute-start.10
  26.9 3.7 %collective-permute-start.6 = (f32[8,128]{1,0:T(8,128)S(1)}, f32[8,128]{1,0:T(8,128)S(1)}, u32[]{:S(2)}, u32[]{:S(2)}) collective-permute-start(f32[8,128]{1,0:T(8,128)S(1)} %add.7.after.sums_ref.refs_0_), channel_id=1, source_target_pairs={{0,9},{1,8},{2,11},{3,10},{4,13},{5,12},{6,15},{7,14},{8,1},{9,0},... | collective-permute-start | bytes 12296 | tf_op jit(solution)/shard_map/ppermute | solution.py:397
  30.6 0.0 collective-permute-start.5
  30.6 1.4 %last_sweep.1.sens_ref = f32[4,256]{1,0:T(4,128)S(1)} custom-call(f32[1,4,4,64,256]{4,3,2,1,0:T(8,128)S(1)} %copy-done, f32[6,2,64,256]{3,2,1,0:T(8,128)S(1)} %get-tuple-element.25.inner_ref, f32[384,256]{1,0:T(8,128)S(1)} %get-tuple-element.32.whole0, f32[384,256]{1,0:T(8,128)S(1)} %get-tuple-element.33.whole1, ...), custom_call_target="tpu_custom_call" | custom-call | flops 1100000000 | tf_op jit(solution)/shard_map/last_sweep/pallas_call | solution.py:302
  32.0 0.3 collective-permute-done.6.refs_2_
  32.3 3.3 %collective-permute-done.5.refs_1_ = f32[8,128]{1,0:T(8,128)S(1)} collective-permute-done((f32[8,128]{1,0:T(8,128)S(1)}, f32[8,128]{1,0:T(8,128)S(1)}, u32[]{:S(2)}, u32[]{:S(2)}) %collective-permute-start.5) | collective-permute-done | bytes 4128 | tf_op jit(solution)/shard_map/ppermute | solution.py:397
  35.6 0.1 node_terms.1
  35.7 0.1 collective-permute-start.8
  35.8 1.2 %collective-permute-done.8.refs_1_ = f32[16,128]{1,0:T(8,128)S(1)} collective-permute-done((f32[16,128]{1,0:T(8,128)S(1)}, f32[16,128]{1,0:T(8,128)S(1)}, u32[]{:S(2)}, u32[]{:S(2)}) %collective-permute-start.8) | collective-permute-done | bytes 8224 | tf_op jit(solution)/shard_map/ppermute | solution.py:401
  36.9 2.7 %collective-permute-done.9.refs_4_ = f32[392,128]{1,0:T(8,128)S(1)} collective-permute-done((f32[392,128]{1,0:T(8,128)S(1)}, f32[392,128]{1,0:T(8,128)S(1)}, u32[]{:S(2)}, u32[]{:S(2)}) %collective-permute-start.9) | collective-permute-done | bytes 200736 | tf_op jit(solution)/shard_map/ppermute | solution.py:389
  39.7 2.2 %collective-permute-done.10.refs_5_ = f32[392,128]{1,0:T(8,128)S(1)} collective-permute-done((f32[392,128]{1,0:T(8,128)S(1)}, f32[392,128]{1,0:T(8,128)S(1)}, u32[]{:S(2)}, u32[]{:S(2)}) %collective-permute-start.10) | collective-permute-done | bytes 200736 | tf_op jit(solution)/shard_map/ppermute | solution.py:391
  41.9 0.7 %gradient.1 = f32[4,128]{1,0:T(4,128)} custom-call(f32[16,128]{1,0:T(8,128)S(1)} %get-tuple-element.38.refs_0_, f32[16,128]{1,0:T(8,128)S(1)} %collective-permute-done.8.refs_1_, f32[384,128]{1,0:T(8,128)S(1)} %get-tuple-element.40.refs_2_, f32[384,128]{1,0:T(8,128)S(1)} %collective-permute-done.7.refs_3_, f32[392,128]{1,0:T(8,128)S(1)} %collective-permute-done.9.refs_4_, ...), custom_call_target="tpu_custom_call" | custom-call | tf_op jit(solution)/shard_map/gradient/pallas_call | solution.py:373
  (14 shorter events, 0.0 us)
Async XLA Ops:
  0.0 8.9 %copy-start = (f32[1,4,4,64,256]{4,3,2,1,0:T(8,128)S(1)}, f32[1,4,4,64,256]{4,3,2,1,0:T(8,128)}, u32[]{:S(2)}) copy-start(f32[1,4,4,64,256]{4,3,2,1,0:T(8,128)} %c_ref.9) | copy-start | bytes 3145732
  0.0 8.9 %copy-start.5 = (f32[1,6,6]{2,0,1:T(1,128)S(1)}, f32[1,6,6]{2,0,1:T(1,128)}, u32[]{:S(2)}) copy-start(f32[1,6,6]{2,0,1:T(1,128)} %param.7) | copy-start | bytes 436
  2.4 20.1 %collective-permute-start = (f32[6,64,256]{2,1,0:T(8,128)}, f32[6,64,256]{2,1,0:T(8,128)S(1)}, u32[]{:S(2)}, u32[]{:S(2)}) collective-permute-start(f32[6,64,256]{2,1,0:T(8,128)} %get-tuple-element.26), channel_id=1, source_target_pairs={{0,1},{1,0},{2,3},{3,2},{4,5},{5,4},{6,7},{7,6},{8,9},{9,8},{10,11... | collective-permute-start | bytes 1179656 | tf_op jit(solution)/shard_map/ppermute | solution.py:389
  5.4 17.1 %collective-permute-start.1 = (f32[6,64,256]{2,1,0:T(8,128)}, f32[6,64,256]{2,1,0:T(8,128)S(1)}, u32[]{:S(2)}, u32[]{:S(2)}) collective-permute-start(f32[6,64,256]{2,1,0:T(8,128)} %get-tuple-element.27.own_ref), channel_id=1, source_target_pairs={{1,2},{2,1},{3,4},{4,3},{5,6},{6,5},{7,8},{8,7},{9,10},{10,9},{11,... | collective-permute-start | bytes 1179656 | tf_op jit(solution)/shard_map/ppermute | solution.py:389
  6.0 8.9 %collective-permute-start.2 = (f32[8,128]{1,0:T(8,128)}, f32[8,128]{1,0:T(8,128)S(1)}, u32[]{:S(2)}, u32[]{:S(2)}) collective-permute-start(f32[8,128]{1,0:T(8,128)} %get-tuple-element.24.after), channel_id=1, source_target_pairs={{0,2},{1,3},{2,0},{3,1},{4,6},{5,7},{6,4},{7,5},{8,10},{9,11},{10,... | collective-permute-start | bytes 12296 | tf_op jit(solution)/shard_map/ppermute | solution.py:397
  8.9 1.4 %copy-start.1 = (f32[1,6,4,64,256]{4,3,2,1,0:T(8,128)S(1)}, f32[1,6,4,64,256]{4,3,2,1,0:T(8,128)}, u32[]{:S(2)}) copy-start(f32[1,6,4,64,256]{4,3,2,1,0:T(8,128)} %s_ref.5) | copy-start | bytes 4718596
  10.3 1.4 %copy-start.2 = (f32[1,6,4,64,256]{4,3,2,1,0:T(8,128)S(1)}, f32[1,6,4,64,256]{4,3,2,1,0:T(8,128)}, u32[]{:S(2)}) copy-start(f32[1,6,4,64,256]{4,3,2,1,0:T(8,128)} %m_ref.1) | copy-start | bytes 4718596
  11.7 0.7 %copy-start.4 = (f32[8,128]{1,0:T(8,128)S(1)}, f32[8,128]{1,0:T(8,128)}, u32[]{:S(2)}) copy-start(f32[8,128]{1,0:T(8,128)} %get-tuple-element.24.after) | copy-start | bytes 12292
  14.9 5.7 %copy-start.3 = (f32[6,64,256]{2,1,0:T(8,128)S(1)}, f32[6,64,256]{2,1,0:T(8,128)}, u32[]{:S(2)}) copy-start(f32[6,64,256]{2,1,0:T(8,128)} %get-tuple-element.27.own_ref) | copy-start | bytes 1179652
  14.9 4.2 %collective-permute-start.3 = (f32[8,128]{1,0:T(8,128)S(1)}, f32[8,128]{1,0:T(8,128)S(1)}, u32[]{:S(2)}, u32[]{:S(2)}) collective-permute-start(f32[8,128]{1,0:T(8,128)S(1)} %add.6.after), channel_id=1, source_target_pairs={{0,4},{1,5},{2,6},{3,7},{4,0},{5,1},{6,2},{7,3},{8,12},{9,13},{10,... | collective-permute-start | bytes 12296 | tf_op jit(solution)/shard_map/ppermute | solution.py:397
  19.9 15.7 %collective-permute-start.4 = (f32[448,256]{1,0:T(8,128)S(1)}, f32[448,256]{1,0:T(8,128)S(1)}, u32[]{:S(2)}, u32[]{:S(2)}) collective-permute-start(f32[448,256]{1,0:T(8,128)S(1)} %odd_second.1.state1.after), channel_id=1, source_target_pairs={{1,2},{2,1},{3,4},{4,3},{5,6},{6,5},{7,8},{8,7},{9,10},{10,9},{11,... | collective-permute-start | bytes 1376264 | tf_op jit(solution)/shard_map/ppermute | solution.py:389
  21.5 9.1 %collective-permute-start.7 = (f32[384,128]{1,0:T(8,128)S(1)}, f32[384,128]{1,0:T(8,128)S(1)}, u32[]{:S(2)}, u32[]{:S(2)}) collective-permute-start(f32[384,128]{1,0:T(8,128)S(1)} %get-tuple-element.37), channel_id=1, source_target_pairs={{0,16},{16,0},{1,17},{17,1},{2,18},{18,2},{3,19},{19,3},{4,20},{20... | collective-permute-start | bytes 589832 | tf_op jit(solution)/shard_map/ppermute | solution.py:401
  23.5 16.1 %collective-permute-start.9 = (f32[392,128]{1,0:T(8,128)S(1)}, f32[392,128]{1,0:T(8,128)S(1)}, u32[]{:S(2)}, u32[]{:S(2)}) collective-permute-start(f32[392,128]{1,0:T(8,128)S(1)} %get-tuple-element.41), channel_id=1, source_target_pairs={{0,1},{1,0},{2,3},{3,2},{4,5},{5,4},{6,7},{7,6},{8,9},{9,8},{10,11... | collective-permute-start | bytes 602120 | tf_op jit(solution)/shard_map/ppermute | solution.py:389
  26.9 15.0 %collective-permute-start.10 = (f32[392,128]{1,0:T(8,128)S(1)}, f32[392,128]{1,0:T(8,128)S(1)}, u32[]{:S(2)}, u32[]{:S(2)}) collective-permute-start(f32[392,128]{1,0:T(8,128)S(1)} %get-tuple-element.42), channel_id=1, source_target_pairs={{0,17},{1,16},{2,19},{3,18},{4,21},{5,20},{6,23},{7,22},{8,25},{9,... | collective-permute-start | bytes 602120 | tf_op jit(solution)/shard_map/ppermute | solution.py:391
  26.9 5.4 %collective-permute-start.6 = (f32[8,128]{1,0:T(8,128)S(1)}, f32[8,128]{1,0:T(8,128)S(1)}, u32[]{:S(2)}, u32[]{:S(2)}) collective-permute-start(f32[8,128]{1,0:T(8,128)S(1)} %add.7.after.sums_ref.refs_0_), channel_id=1, source_target_pairs={{0,9},{1,8},{2,11},{3,10},{4,13},{5,12},{6,15},{7,14},{8,1},{9,0},... | collective-permute-start | bytes 12296 | tf_op jit(solution)/shard_map/ppermute | solution.py:397
  30.6 5.0 %collective-permute-start.5 = (f32[8,128]{1,0:T(8,128)S(1)}, f32[8,128]{1,0:T(8,128)S(1)}, u32[]{:S(2)}, u32[]{:S(2)}) collective-permute-start(f32[8,128]{1,0:T(8,128)S(1)} %add.7.after.sums_ref.refs_0_), channel_id=1, source_target_pairs={{0,8},{1,9},{2,10},{3,11},{4,12},{5,13},{6,14},{7,15},{8,0},{9,1},... | collective-permute-start | bytes 12296 | tf_op jit(solution)/shard_map/ppermute | solution.py:397
  35.7 1.2 %collective-permute-start.8 = (f32[16,128]{1,0:T(8,128)S(1)}, f32[16,128]{1,0:T(8,128)S(1)}, u32[]{:S(2)}, u32[]{:S(2)}) collective-permute-start(f32[16,128]{1,0:T(8,128)S(1)} %get-tuple-element.39), channel_id=1, source_target_pairs={{0,16},{16,0},{1,17},{17,1},{2,18},{18,2},{3,19},{19,3},{4,20},{20... | collective-permute-start | bytes 24584 | tf_op jit(solution)/shard_map/ppermute | solution.py:401

commit v7 on v6

--- a/solution.py
+++ b/solution.py
@@ -139,6 +139,8 @@
             out[pl.ds(nv * ny, ny), :] = rho
         else:
             part[2 * nv] = rho
+            for w in range(nv // 2):
+                part[w] = part[w] + mixed(f_ref, w, lambda v: part[nv + v])
 
 
 def even_second(block, source, coef, after):
@@ -157,7 +159,8 @@
     del after
     nv, ny = f_ref.shape[1], part.shape[1]
     for w in range(nv):
-        out[pl.ds(w * ny, ny), :] = part[w] + mixed(f_ref, w, lambda v: part[nv + v])
+        mix = mixed(f_ref, w, lambda v: part[nv + v]) if w >= nv // 2 else 0.0
+        out[pl.ds(w * ny, ny), :] = part[w] + mix
     out[pl.ds(nv * ny, ny), :] = part[2 * nv]
 
 

time: 42.8 us -> 42.8 us (level)
  no operation moved by 1% of the time
where the time goes in v7:
time: 42.8 us; the launch traced here: 42.5 us
  starting transfers between devices  16.5 us (39%)
  waiting for transfers between devices  11.3 us (26%)
  Pallas kernels  11.1 us (26%)
  local copies, waits for them, and re-layouts  3.5 us (8%)
    ppermute x4, starting transfers between devices, from_partner(): return lax.ppermute(value, ('node', 'slab'), pairs)  8.6 us
    ppermute x4, starting transfers between devices, swap_pairs(): return lax.ppermute(value, 'slab', pairs)  7.76 us
    ppermute x4, waiting for transfers between devices, from_partner(): return lax.ppermute(value, ('node', 'slab'), pairs)  4.18 us
    ppermute x4, waiting for transfers between devices, swap_pairs(): return lax.ppermute(value, 'slab', pairs)  3.77 us
    unnamed x13, local copies, waits for them, and re-layouts  3.5 us
    pallas_call x1, Pallas kernels, first_sweep(): call(first_kernel, 'first_sweep', out_shape=(f32(nv, nx - 2, ny, nz), f32...  2.53 us
    pallas_call x1, Pallas kernels, edge_state(): call(edge_kernel, 'edge_state', out_shape=(f32(nv, ny, nz),) * 2 + (f32(R...  2.34 us
    ppermute x1, waiting for transfers between devices, swap_pairs(): return lax.ppermute(value, ('node', 'slab'), cross)  2.17 us
  transfers between devices with their start and end apart: 11, of which 7 were waited for; matrix products, arithmetic and copies ran while one was open for 0% of the time, Pallas kernels for 19%

profile of v7, /device:TPU:0, one launch (start us, length us, event | category | flops | bytes accessed | tf_op | source)
XLA Modules:
  0.0 42.5 jit_solution(7100908750333158708)
XLA Ops:
  0.0 2.3 %edge_state.1 = (f32[6,64,256]{2,1,0:T(8,128)}, f32[6,64,256]{2,1,0:T(8,128)}, f32[8,128]{1,0:T(8,128)}) custom-call(f32[1,6,4,64,256]{4,3,2,1,0:T(8,128)} %s_ref.5, f32[1,4,4,64,256]{4,3,2,1,0:T(8,128)} %c_ref.9, f32[1,4,256]{2,1,0:T(4,128)} %wall_ref.1), custom_call_target="tpu_custom_call" | custom-call | tf_op jit(solution)/shard_map/edge_state/pallas_call | solution.py:79
  2.4 3.0 %collective-permute-start = (f32[6,64,256]{2,1,0:T(8,128)}, f32[6,64,256]{2,1,0:T(8,128)S(1)}, u32[]{:S(2)}, u32[]{:S(2)}) collective-permute-start(f32[6,64,256]{2,1,0:T(8,128)} %get-tuple-element.26), channel_id=1, source_target_pairs={{0,1},{1,0},{2,3},{3,2},{4,5},{5,4},{6,7},{7,6},{8,9},{9,8},{10,11... | collective-permute-start | bytes 1179656 | tf_op jit(solution)/shard_map/ppermute | solution.py:392
  5.4 0.7 %collective-permute-start.1 = (f32[6,64,256]{2,1,0:T(8,128)}, f32[6,64,256]{2,1,0:T(8,128)S(1)}, u32[]{:S(2)}, u32[]{:S(2)}) collective-permute-start(f32[6,64,256]{2,1,0:T(8,128)} %get-tuple-element.27.own_ref), channel_id=1, source_target_pairs={{1,2},{2,1},{3,4},{4,3},{5,6},{6,5},{7,8},{8,7},{9,10},{10,9},{11,... | collective-permute-start | bytes 1179656 | tf_op jit(solution)/shard_map/ppermute | solution.py:392
  6.0 2.8 %collective-permute-start.2 = (f32[8,128]{1,0:T(8,128)}, f32[8,128]{1,0:T(8,128)S(1)}, u32[]{:S(2)}, u32[]{:S(2)}) collective-permute-start(f32[8,128]{1,0:T(8,128)} %get-tuple-element.24.after), channel_id=1, source_target_pairs={{0,2},{1,3},{2,0},{3,1},{4,6},{5,7},{6,4},{7,5},{8,10},{9,11},{10,... | collective-permute-start | bytes 12296 | tf_op jit(solution)/shard_map/ppermute | solution.py:400
  8.9 1.4 %copy-done.1 = f32[1,6,4,64,256]{4,3,2,1,0:T(8,128)S(1)} copy-done((f32[1,6,4,64,256]{4,3,2,1,0:T(8,128)S(1)}, f32[1,6,4,64,256]{4,3,2,1,0:T(8,128)}, u32[]{:S(2)}) %copy-start.1) | copy-done | bytes 1572888
  10.3 1.4 %copy-done.2 = f32[1,6,4,64,256]{4,3,2,1,0:T(8,128)S(1)} copy-done((f32[1,6,4,64,256]{4,3,2,1,0:T(8,128)S(1)}, f32[1,6,4,64,256]{4,3,2,1,0:T(8,128)}, u32[]{:S(2)}) %copy-start.2) | copy-done | bytes 1572888
  11.7 0.7 %copy-done.4 = f32[8,128]{1,0:T(8,128)S(1)} copy-done((f32[8,128]{1,0:T(8,128)S(1)}, f32[8,128]{1,0:T(8,128)}, u32[]{:S(2)}) %copy-start.4) | copy-done | bytes 4120
  12.4 2.5 %first_sweep.1 = (f32[6,2,64,256]{3,2,1,0:T(8,128)S(1)}, f32[6,4,64,256]{3,2,1,0:T(8,128)S(1)}, f32[4,256]{1,0:T(4,128)S(1)}) custom-call(f32[1,6,6]{2,1,0:T(8,128)S(1)} %copy.6.f_ref, f32[1,6,4,64,256]{4,3,2,1,0:T(8,128)S(1)} %copy-done.1, f32[1,4,4,64,256]{4,3,2,1,0:T(8,128)S(1)} %copy-done, f32[1,6,4,64,256]{4,3,2,1,0:T(8,128)S(1)} %copy-done.2, ...), custom_call_target="tpu_custom_call" | custom-call | tf_op jit(solution)/shard_map/first_sweep/pallas_call | solution.py:214
  14.9 0.0 collective-permute-done.2
  14.9 2.1 %collective-permute-start.3 = (f32[8,128]{1,0:T(8,128)S(1)}, f32[8,128]{1,0:T(8,128)S(1)}, u32[]{:S(2)}, u32[]{:S(2)}) collective-permute-start(f32[8,128]{1,0:T(8,128)S(1)} %add.6.after), channel_id=1, source_target_pairs={{0,4},{1,5},{2,6},{3,7},{4,0},{5,1},{6,2},{7,3},{8,12},{9,13},{10,... | collective-permute-start | bytes 12296 | tf_op jit(solution)/shard_map/ppermute | solution.py:400
  17.0 1.5 %even_second.1 = (f32[448,256]{1,0:T(8,128)S(1)}, f32[13,64,256]{2,1,0:T(8,128)S(1)}) custom-call(f32[1,6,6]{2,1,0:T(8,128)S(1)} %copy.6.f_ref, f32[1,6,4,64,256]{4,3,2,1,0:T(8,128)S(1)} %copy-done.1, f32[1,4,4,64,256]{4,3,2,1,0:T(8,128)S(1)} %copy-done, f32[8,128]{1,0:T(8,128)S(1)} %add.6.after), custom_call_target="tpu_custom_call" | custom-call | tf_op jit(solution)/shard_map/even_second/pallas_call | solution.py:148
  18.5 0.6 %collective-permute-done.3 = f32[8,128]{1,0:T(8,128)S(1)} collective-permute-done((f32[8,128]{1,0:T(8,128)S(1)}, f32[8,128]{1,0:T(8,128)S(1)}, u32[]{:S(2)}, u32[]{:S(2)}) %collective-permute-start.3) | collective-permute-done | bytes 4128 | tf_op jit(solution)/shard_map/ppermute | solution.py:400
  19.1 0.7 %odd_second.1.state1.after = f32[448,256]{1,0:T(8,128)S(1)} custom-call(f32[1,6,6]{2,1,0:T(8,128)S(1)} %copy.6.f_ref, f32[13,64,256]{2,1,0:T(8,128)S(1)} %get-tuple-element.31.part, f32[8,128]{1,0:T(8,128)S(1)} %add.7.after.sums_ref.refs_0_), custom_call_target="tpu_custom_call" | custom-call | tf_op jit(solution)/shard_map/odd_second/pallas_call | solution.py:169
  19.8 0.7 %collective-permute-start.4 = (f32[448,256]{1,0:T(8,128)S(1)}, f32[448,256]{1,0:T(8,128)S(1)}, u32[]{:S(2)}, u32[]{:S(2)}) collective-permute-start(f32[448,256]{1,0:T(8,128)S(1)} %odd_second.1.state1.after), channel_id=1, source_target_pairs={{1,2},{2,1},{3,4},{4,3},{5,6},{6,5},{7,8},{8,7},{9,10},{10,9},{11,... | collective-permute-start | bytes 1376264 | tf_op jit(solution)/shard_map/ppermute | solution.py:392
  20.5 0.9 %edge_weights.1 = (f32[832,256]{1,0:T(8,128)S(1)}, f32[384,128]{1,0:T(8,128)S(1)}, f32[384,128]{1,0:T(8,128)S(1)}) custom-call(f32[1,6,6]{2,1,0:T(8,128)S(1)} %copy.6.f_ref, f32[1,4,4,64,256]{4,3,2,1,0:T(8,128)S(1)} %copy-done, f32[6,4,64,256]{3,2,1,0:T(8,128)S(1)} %get-tuple-element.34.b_ref, f32[6,64,256]{2,1,0:T(8,128)S(1)} %copy-done.3, ...), custom_call_target="tpu_custom_call" | custom-call | tf_op jit(solution)/shard_map/edge_weights/pallas_call | solution.py:247
  21.5 0.1 collective-permute-start.7
  21.5 0.9 %collective-permute-done.far0 = f32[6,64,256]{2,1,0:T(8,128)S(1)} collective-permute-done((f32[6,64,256]{2,1,0:T(8,128)}, f32[6,64,256]{2,1,0:T(8,128)S(1)}, u32[]{:S(2)}, u32[]{:S(2)}) %collective-permute-start) | collective-permute-done | bytes 393248 | tf_op jit(solution)/shard_map/ppermute | solution.py:392
  22.5 1.0 %second_states.1 = (f32[384,256]{1,0:T(8,128)S(1)}, f32[384,256]{1,0:T(8,128)S(1)}, f32[392,128]{1,0:T(8,128)S(1)}, f32[392,128]{1,0:T(8,128)S(1)}) custom-call(f32[1,6,6]{2,1,0:T(8,128)S(1)} %copy.6.f_ref, f32[6,64,256]{2,1,0:T(8,128)S(1)} %collective-permute-done.far0, f32[6,64,256]{2,1,0:T(8,128)S(1)} %collective-permute-done.1.far1, ...), custom_call_target="tpu_custom_call" | custom-call | tf_op jit(solution)/shard_map/second_states/pallas_call | solution.py:272
  23.5 3.4 %collective-permute-start.9 = (f32[392,128]{1,0:T(8,128)S(1)}, f32[392,128]{1,0:T(8,128)S(1)}, u32[]{:S(2)}, u32[]{:S(2)}) collective-permute-start(f32[392,128]{1,0:T(8,128)S(1)} %get-tuple-element.41), channel_id=1, source_target_pairs={{0,1},{1,0},{2,3},{3,2},{4,5},{5,4},{6,7},{7,6},{8,9},{9,8},{10,11... | collective-permute-start | bytes 602120 | tf_op jit(solution)/shard_map/ppermute | solution.py:392
  26.9 3.6 %collective-permute-start.6 = (f32[8,128]{1,0:T(8,128)S(1)}, f32[8,128]{1,0:T(8,128)S(1)}, u32[]{:S(2)}, u32[]{:S(2)}) collective-permute-start(f32[8,128]{1,0:T(8,128)S(1)} %add.7.after.sums_ref.refs_0_), channel_id=1, source_target_pairs={{0,9},{1,8},{2,11},{3,10},{4,13},{5,12},{6,15},{7,14},{8,1},{9,0},... | collective-permute-start | bytes 12296 | tf_op jit(solution)/shard_map/ppermute | solution.py:400
  30.5 0.0 collective-permute-done.7.refs_3_
  30.5 0.0 collective-permute-start.5
  30.6 1.4 %last_sweep.1.sens_ref = f32[4,256]{1,0:T(4,128)S(1)} custom-call(f32[1,4,4,64,256]{4,3,2,1,0:T(8,128)S(1)} %copy-done, f32[6,2,64,256]{3,2,1,0:T(8,128)S(1)} %get-tuple-element.25.inner_ref, f32[384,256]{1,0:T(8,128)S(1)} %get-tuple-element.32.whole0, f32[384,256]{1,0:T(8,128)S(1)} %get-tuple-element.33.whole1, ...), custom_call_target="tpu_custom_call" | custom-call | flops 1100000000 | tf_op jit(solution)/shard_map/last_sweep/pallas_call | solution.py:305
  31.9 0.4 collective-permute-done.6.refs_2_
  32.3 3.2 %collective-permute-done.5.refs_1_ = f32[8,128]{1,0:T(8,128)S(1)} collective-permute-done((f32[8,128]{1,0:T(8,128)S(1)}, f32[8,128]{1,0:T(8,128)S(1)}, u32[]{:S(2)}, u32[]{:S(2)}) %collective-permute-start.5) | collective-permute-done | bytes 4128 | tf_op jit(solution)/shard_map/ppermute | solution.py:400
  35.5 0.0 collective-permute-done.4.odd_ref
  35.5 0.1 node_terms.1
  35.6 0.1 collective-permute-start.8
  35.7 1.2 %collective-permute-done.8.refs_1_ = f32[16,128]{1,0:T(8,128)S(1)} collective-permute-done((f32[16,128]{1,0:T(8,128)S(1)}, f32[16,128]{1,0:T(8,128)S(1)}, u32[]{:S(2)}, u32[]{:S(2)}) %collective-permute-start.8) | collective-permute-done | bytes 8224 | tf_op jit(solution)/shard_map/ppermute | solution.py:404
  36.8 2.8 %collective-permute-done.9.refs_4_ = f32[392,128]{1,0:T(8,128)S(1)} collective-permute-done((f32[392,128]{1,0:T(8,128)S(1)}, f32[392,128]{1,0:T(8,128)S(1)}, u32[]{:S(2)}, u32[]{:S(2)}) %collective-permute-start.9) | collective-permute-done | bytes 200736 | tf_op jit(solution)/shard_map/ppermute | solution.py:392
  39.7 2.2 %collective-permute-done.10.refs_5_ = f32[392,128]{1,0:T(8,128)S(1)} collective-permute-done((f32[392,128]{1,0:T(8,128)S(1)}, f32[392,128]{1,0:T(8,128)S(1)}, u32[]{:S(2)}, u32[]{:S(2)}) %collective-permute-start.10) | collective-permute-done | bytes 200736 | tf_op jit(solution)/shard_map/ppermute | solution.py:394
  41.8 0.7 %gradient.1 = f32[4,128]{1,0:T(4,128)} custom-call(f32[16,128]{1,0:T(8,128)S(1)} %get-tuple-element.38.refs_0_, f32[16,128]{1,0:T(8,128)S(1)} %collective-permute-done.8.refs_1_, f32[384,128]{1,0:T(8,128)S(1)} %get-tuple-element.40.refs_2_, f32[384,128]{1,0:T(8,128)S(1)} %collective-permute-done.7.refs_3_, f32[392,128]{1,0:T(8,128)S(1)} %collective-permute-done.9.refs_4_, ...), custom_call_target="tpu_custom_call" | custom-call | tf_op jit(solution)/shard_map/gradient/pallas_call | solution.py:376
  (14 shorter events, 0.0 us)
Async XLA Ops:
  0.0 8.9 %copy-start = (f32[1,4,4,64,256]{4,3,2,1,0:T(8,128)S(1)}, f32[1,4,4,64,256]{4,3,2,1,0:T(8,128)}, u32[]{:S(2)}) copy-start(f32[1,4,4,64,256]{4,3,2,1,0:T(8,128)} %c_ref.9) | copy-start | bytes 3145732
  0.0 8.9 %copy-start.5 = (f32[1,6,6]{2,0,1:T(1,128)S(1)}, f32[1,6,6]{2,0,1:T(1,128)}, u32[]{:S(2)}) copy-start(f32[1,6,6]{2,0,1:T(1,128)} %param.7) | copy-start | bytes 436
  2.4 20.1 %collective-permute-start = (f32[6,64,256]{2,1,0:T(8,128)}, f32[6,64,256]{2,1,0:T(8,128)S(1)}, u32[]{:S(2)}, u32[]{:S(2)}) collective-permute-start(f32[6,64,256]{2,1,0:T(8,128)} %get-tuple-element.26), channel_id=1, source_target_pairs={{0,1},{1,0},{2,3},{3,2},{4,5},{5,4},{6,7},{7,6},{8,9},{9,8},{10,11... | collective-permute-start | bytes 1179656 | tf_op jit(solution)/shard_map/ppermute | solution.py:392
  5.4 17.1 %collective-permute-start.1 = (f32[6,64,256]{2,1,0:T(8,128)}, f32[6,64,256]{2,1,0:T(8,128)S(1)}, u32[]{:S(2)}, u32[]{:S(2)}) collective-permute-start(f32[6,64,256]{2,1,0:T(8,128)} %get-tuple-element.27.own_ref), channel_id=1, source_target_pairs={{1,2},{2,1},{3,4},{4,3},{5,6},{6,5},{7,8},{8,7},{9,10},{10,9},{11,... | collective-permute-start | bytes 1179656 | tf_op jit(solution)/shard_map/ppermute | solution.py:392
  6.0 8.9 %collective-permute-start.2 = (f32[8,128]{1,0:T(8,128)}, f32[8,128]{1,0:T(8,128)S(1)}, u32[]{:S(2)}, u32[]{:S(2)}) collective-permute-start(f32[8,128]{1,0:T(8,128)} %get-tuple-element.24.after), channel_id=1, source_target_pairs={{0,2},{1,3},{2,0},{3,1},{4,6},{5,7},{6,4},{7,5},{8,10},{9,11},{10,... | collective-permute-start | bytes 12296 | tf_op jit(solution)/shard_map/ppermute | solution.py:400
  8.9 1.4 %copy-start.1 = (f32[1,6,4,64,256]{4,3,2,1,0:T(8,128)S(1)}, f32[1,6,4,64,256]{4,3,2,1,0:T(8,128)}, u32[]{:S(2)}) copy-start(f32[1,6,4,64,256]{4,3,2,1,0:T(8,128)} %s_ref.5) | copy-start | bytes 4718596
  10.3 1.4 %copy-start.2 = (f32[1,6,4,64,256]{4,3,2,1,0:T(8,128)S(1)}, f32[1,6,4,64,256]{4,3,2,1,0:T(8,128)}, u32[]{:S(2)}) copy-start(f32[1,6,4,64,256]{4,3,2,1,0:T(8,128)} %m_ref.1) | copy-start | bytes 4718596
  11.7 0.7 %copy-start.4 = (f32[8,128]{1,0:T(8,128)S(1)}, f32[8,128]{1,0:T(8,128)}, u32[]{:S(2)}) copy-start(f32[8,128]{1,0:T(8,128)} %get-tuple-element.24.after) | copy-start | bytes 12292
  14.9 5.6 %copy-start.3 = (f32[6,64,256]{2,1,0:T(8,128)S(1)}, f32[6,64,256]{2,1,0:T(8,128)}, u32[]{:S(2)}) copy-start(f32[6,64,256]{2,1,0:T(8,128)} %get-tuple-element.27.own_ref) | copy-start | bytes 1179652
  14.9 4.2 %collective-permute-start.3 = (f32[8,128]{1,0:T(8,128)S(1)}, f32[8,128]{1,0:T(8,128)S(1)}, u32[]{:S(2)}, u32[]{:S(2)}) collective-permute-start(f32[8,128]{1,0:T(8,128)S(1)} %add.6.after), channel_id=1, source_target_pairs={{0,4},{1,5},{2,6},{3,7},{4,0},{5,1},{6,2},{7,3},{8,12},{9,13},{10,... | collective-permute-start | bytes 12296 | tf_op jit(solution)/shard_map/ppermute | solution.py:400
  19.8 15.7 %collective-permute-start.4 = (f32[448,256]{1,0:T(8,128)S(1)}, f32[448,256]{1,0:T(8,128)S(1)}, u32[]{:S(2)}, u32[]{:S(2)}) collective-permute-start(f32[448,256]{1,0:T(8,128)S(1)} %odd_second.1.state1.after), channel_id=1, source_target_pairs={{1,2},{2,1},{3,4},{4,3},{5,6},{6,5},{7,8},{8,7},{9,10},{10,9},{11,... | collective-permute-start | bytes 1376264 | tf_op jit(solution)/shard_map/ppermute | solution.py:392
  21.5 9.1 %collective-permute-start.7 = (f32[384,128]{1,0:T(8,128)S(1)}, f32[384,128]{1,0:T(8,128)S(1)}, u32[]{:S(2)}, u32[]{:S(2)}) collective-permute-start(f32[384,128]{1,0:T(8,128)S(1)} %get-tuple-element.37), channel_id=1, source_target_pairs={{0,16},{16,0},{1,17},{17,1},{2,18},{18,2},{3,19},{19,3},{4,20},{20... | collective-permute-start | bytes 589832 | tf_op jit(solution)/shard_map/ppermute | solution.py:404
  23.5 16.2 %collective-permute-start.9 = (f32[392,128]{1,0:T(8,128)S(1)}, f32[392,128]{1,0:T(8,128)S(1)}, u32[]{:S(2)}, u32[]{:S(2)}) collective-permute-start(f32[392,128]{1,0:T(8,128)S(1)} %get-tuple-element.41), channel_id=1, source_target_pairs={{0,1},{1,0},{2,3},{3,2},{4,5},{5,4},{6,7},{7,6},{8,9},{9,8},{10,11... | collective-permute-start | bytes 602120 | tf_op jit(solution)/shard_map/ppermute | solution.py:392
  26.9 14.9 %collective-permute-start.10 = (f32[392,128]{1,0:T(8,128)S(1)}, f32[392,128]{1,0:T(8,128)S(1)}, u32[]{:S(2)}, u32[]{:S(2)}) collective-permute-start(f32[392,128]{1,0:T(8,128)S(1)} %get-tuple-element.42), channel_id=1, source_target_pairs={{0,17},{1,16},{2,19},{3,18},{4,21},{5,20},{6,23},{7,22},{8,25},{9,... | collective-permute-start | bytes 602120 | tf_op jit(solution)/shard_map/ppermute | solution.py:394
  26.9 5.4 %collective-permute-start.6 = (f32[8,128]{1,0:T(8,128)S(1)}, f32[8,128]{1,0:T(8,128)S(1)}, u32[]{:S(2)}, u32[]{:S(2)}) collective-permute-start(f32[8,128]{1,0:T(8,128)S(1)} %add.7.after.sums_ref.refs_0_), channel_id=1, source_target_pairs={{0,9},{1,8},{2,11},{3,10},{4,13},{5,12},{6,15},{7,14},{8,1},{9,0},... | collective-permute-start | bytes 12296 | tf_op jit(solution)/shard_map/ppermute | solution.py:400
  30.5 5.0 %collective-permute-start.5 = (f32[8,128]{1,0:T(8,128)S(1)}, f32[8,128]{1,0:T(8,128)S(1)}, u32[]{:S(2)}, u32[]{:S(2)}) collective-permute-start(f32[8,128]{1,0:T(8,128)S(1)} %add.7.after.sums_ref.refs_0_), channel_id=1, source_target_pairs={{0,8},{1,9},{2,10},{3,11},{4,12},{5,13},{6,14},{7,15},{8,0},{9,1},... | collective-permute-start | bytes 12296 | tf_op jit(solution)/shard_map/ppermute | solution.py:400
  35.6 1.2 %collective-permute-start.8 = (f32[16,128]{1,0:T(8,128)S(1)}, f32[16,128]{1,0:T(8,128)S(1)}, u32[]{:S(2)}, u32[]{:S(2)}) collective-permute-start(f32[16,128]{1,0:T(8,128)S(1)} %get-tuple-element.39), channel_id=1, source_target_pairs={{0,16},{16,0},{1,17},{17,1},{2,18},{18,2},{3,19},{19,3},{4,20},{20... | collective-permute-start | bytes 24584 | tf_op jit(solution)/shard_map/ppermute | solution.py:404
